TPU v7x, 128 devices: a whole 4x4x4 slice. The times are simulated.
128 devices in a mesh: section: 8 (over x_hi, y), ctx: 16 (over z, x_lo, core).
Axes of the slice: x: 4 (x_hi: 2, x_lo: 2; x = x_hi * 2 + x_lo), y: 4, z: 4, core: 2. Of those that a mesh axis runs over, the one named last changes fastest.
Arguments:
- down_in: bfloat16 [8, 2048, 4096], P('section', 'ctx')
- up_in: bfloat16 [8, 2048, 4096], P('section', 'ctx')
- down_cot: bfloat16 [8, 2048, 4096], P('section', 'ctx'), may hold values from -6 to 6
- up_cot: bfloat16 [8, 2048, 4096], P('section', 'ctx'), may hold values from -6 to 6
- kv_weight: bfloat16 [2, 8, 4096, 1024], P(None, 'section'), as said below
- norm_gain: float32 [2, 8, 4096], P(None, 'section'), as said below
- span_ids: int32 [16], replicated, may hold values from 0 to 15, each once
Outputs:
- down_out: bfloat16 [8, 2048, 4096], P('section', 'ctx')
- up_out: bfloat16 [8, 2048, 4096], P('section', 'ctx')
- down_grad: bfloat16 [8, 2048, 4096], P('section', 'ctx')
- up_grad: bfloat16 [8, 2048, 4096], P('section', 'ctx')
- kv_grad: float32 [8, 4096, 1024], P('section', 'ctx')
- gain_grad: float32 [8, 4096], P('section', 'ctx')
Inputs may be any that keep to these rules, and one draw needn't show every extreme that they name: kv_weight[1, s] equals kv_weight[0, 7 - s]: copy 1 is the layer of the mirrored section. norm_gain[1, s] equals norm_gain[0, 7 - s]; all entries are positive.
All inputs are finite; a program needn't handle non-finite values.
Results may differ from a plain program's by a relative error of at most 0.027.
Values may be sent and summed in bfloat16 or wider, within the bound.
A program may use at most 192 MiB of HBM per device.

v0:
```python
import math

import jax
import jax.numpy as jnp
from jax import lax
from jax.sharding import PartitionSpec as P

HEAD = 128
KV_HEADS = 4


EPS = 1e-05


def from_behind(array, axis, by):
    size = lax.axis_size(axis)
    return lax.ppermute(array, axis, [(i, (i + by) % size) for i in range(size)])


def swapped(block, axis, distance):
    count = lax.axis_size(axis)
    route = []
    for low in range(count):
        high = low | 1 << distance
        if high != low and high < count:
            route += [(low, high), (high, low)]
    return lax.ppermute(block, axis, route)


def prepare(x, gain, weight):
    xf = x.astype(jnp.float32)
    recip = lax.rsqrt(jnp.mean(xf * xf, -1, keepdims=True) + EPS)
    normed = xf * recip
    act = (normed * gain[None, :]).astype(jnp.bfloat16)
    kv = jnp.dot(act, weight, preferred_element_type=jnp.float32).astype(jnp.bfloat16)
    return (xf, recip, normed, act, kv)


def attend_block(carry, piece, key_pos, query, query_pos):
    top, total, acc = carry
    count = piece.shape[0]
    half = piece.shape[1] // 2
    keys = piece[:, :half].reshape(count, KV_HEADS, HEAD)
    vals = piece[:, half:].reshape(count, KV_HEADS, HEAD)
    scores = jnp.einsum(
        "tkgd,nkd->kgtn", query, keys, preferred_element_type=jnp.float32
    ) * HEAD ** (-0.5)
    visible = key_pos[None, :] <= query_pos[:, None]
    new_top = jnp.maximum(top, jnp.max(jnp.where(visible, scores, -1e30), -1))
    expo = jnp.where(visible, jnp.exp(scores - new_top[..., None]), 0.0)
    fade = jnp.exp(top - new_top)
    total = total * fade + jnp.sum(expo, -1)
    acc = acc * fade[..., None] + jnp.einsum(
        "kgtn,nkd->kgtd", expo.astype(jnp.bfloat16), vals, preferred_element_type=jnp.float32
    )
    return (new_top, total, acc)


def guarded(carry, piece, key_pos, query, query_pos):
    return lax.cond(
        jnp.min(key_pos) <= jnp.max(query_pos),
        lambda state: attend_block(state, piece, key_pos, query, query_pos),
        lambda state: state,
        carry,
    )


def finish(carry, tok, width):
    top, total, acc = carry
    mixed = jnp.transpose(acc / total[..., None], (2, 0, 1, 3)).reshape(tok, width)
    return (mixed, top + jnp.log(total))


def gather_all(kv_down, kv_up):
    return (
        lax.all_gather(kv_down, "ctx", axis=0, tiled=True),
        lax.all_gather(kv_up, "ctx", axis=0, tiled=True),
    )


def backward_terms(whole, query, query_pos, key_pos, cot, mixed, lse, block):
    tok = query.shape[0]
    group = query.shape[2]
    rows = whole.shape[0]
    half = whole.shape[1] // 2
    scale = HEAD ** (-0.5)
    dout = cot.reshape(tok, KV_HEADS, group, HEAD)
    delta = jnp.transpose(
        jnp.sum(dout.astype(jnp.float32) * mixed.reshape(tok, KV_HEADS, group, HEAD), -1), (1, 2, 0)
    )

    def step(index, state):
        first = index * block
        piece = lax.dynamic_slice_in_dim(whole, first, block, 0)
        kpos = lax.dynamic_slice_in_dim(key_pos, first, block, 0)

        def work(inner):
            dquery, terms = inner
            keys = piece[:, :half].reshape(block, KV_HEADS, HEAD)
            vals = piece[:, half:].reshape(block, KV_HEADS, HEAD)
            scores = (
                jnp.einsum("tkgd,nkd->kgtn", query, keys, preferred_element_type=jnp.float32)
                * scale
            )
            visible = kpos[None, :] <= query_pos[:, None]
            prob = jnp.where(visible, jnp.exp(scores - lse[..., None]), 0.0)
            dprob = jnp.einsum("tkgd,nkd->kgtn", dout, vals, preferred_element_type=jnp.float32)
            dscore = (prob * (dprob - delta[..., None]) * scale).astype(jnp.bfloat16)
            dquery = dquery + jnp.einsum(
                "kgtn,nkd->tkgd", dscore, keys, preferred_element_type=jnp.float32
            )
            dkey = jnp.einsum("kgtn,tkgd->nkd", dscore, query, preferred_element_type=jnp.float32)
            dval = jnp.einsum(
                "kgtn,tkgd->nkd",
                prob.astype(jnp.bfloat16),
                dout,
                preferred_element_type=jnp.float32,
            )
            fresh = jnp.concatenate([dkey.reshape(block, half), dval.reshape(block, half)], 1)
            return (dquery, lax.dynamic_update_slice_in_dim(terms, fresh, first, 0))

        return lax.cond(jnp.min(kpos) <= jnp.max(query_pos), work, lambda inner: inner, state)

    start_state = (
        jnp.zeros((tok, KV_HEADS, group, HEAD), jnp.float32),
        jnp.zeros((rows, 2 * half), jnp.float32),
    )
    dquery, terms = lax.fori_loop(0, rows // block, step, start_state)
    return (dquery.reshape(tok, KV_HEADS * group * HEAD), terms)


def complete(recip, normed, act, cot, gain, weight, dquery, dkv_sum):
    dkv_b = dkv_sum.astype(jnp.bfloat16)
    dact = dquery + lax.dot_general(
        dkv_b, weight, (((1,), (1,)), ((), ())), preferred_element_type=jnp.float32
    )
    wpart = lax.dot_general(
        act, dkv_b, (((0,), (0,)), ((), ())), preferred_element_type=jnp.float32
    )
    gpart = jnp.sum(dact * normed, 0)
    dnormed = dact * gain[None, :]
    dx = (
        cot.astype(jnp.float32)
        + recip * (dnormed - normed * jnp.mean(dnormed * normed, -1, keepdims=True))
    ).astype(jnp.bfloat16)
    return (dx, wpart, gpart)


def per_device(down_in, up_in, down_cot, up_cot, kv_weight, norm_gain, span_ids):
    tok = down_in.shape[1]
    width = down_in.shape[2]
    group = width // (KV_HEADS * HEAD)
    rows = tok * lax.axis_size("ctx")
    block = math.gcd(512, rows)
    own = lax.axis_index("ctx")
    steps_local = jnp.arange(tok, dtype=jnp.int32)
    key_pos = (span_ids[:, None] * tok + steps_local[None, :]).reshape(-1)
    query_pos = lax.dynamic_slice_in_dim(key_pos, own * tok, tok, 0)
    xf_d, recip_d, normed_d, act_d, kv_d = prepare(down_in[0], norm_gain[0, 0], kv_weight[0, 0])
    xf_u, recip_u, normed_u, act_u, kv_u = prepare(up_in[0], norm_gain[1, 0], kv_weight[1, 0])
    query_d = act_d.reshape(tok, KV_HEADS, group, HEAD)
    query_u = act_u.reshape(tok, KV_HEADS, group, HEAD)
    start = (
        jnp.full((KV_HEADS, group, tok), -1e30, jnp.float32),
        jnp.zeros((KV_HEADS, group, tok), jnp.float32),
        jnp.zeros((KV_HEADS, group, tok, HEAD), jnp.float32),
    )
    whole_d, whole_u = gather_all(kv_d, kv_u)

    def forward_step(index, carries):
        first = index * block
        kpos = lax.dynamic_slice_in_dim(key_pos, first, block, 0)
        piece_d = lax.dynamic_slice_in_dim(whole_d, first, block, 0)
        piece_u = lax.dynamic_slice_in_dim(whole_u, first, block, 0)
        return (
            guarded(carries[0], piece_d, kpos, query_d, query_pos),
            guarded(carries[1], piece_u, kpos, query_u, query_pos),
        )

    carry_d, carry_u = lax.fori_loop(0, rows // block, forward_step, (start, start))
    mixed_d, lse_d = finish(carry_d, tok, width)
    mixed_u, lse_u = finish(carry_u, tok, width)
    y_down = (xf_d + mixed_d).astype(jnp.bfloat16)
    y_up = (xf_u + mixed_u).astype(jnp.bfloat16)
    down_out = from_behind(y_down, "section", 1)
    up_out = from_behind(y_up, "section", -1)
    dquery_d, terms_d = backward_terms(
        whole_d, query_d, query_pos, key_pos, down_cot[0], mixed_d, lse_d, block
    )
    dquery_u, terms_u = backward_terms(
        whole_u, query_u, query_pos, key_pos, up_cot[0], mixed_u, lse_u, block
    )
    dkv_d, dkv_u = (
        lax.psum_scatter(
            terms_d.astype(jnp.bfloat16), "ctx", scatter_dimension=0, tiled=True
        ).astype(jnp.float32),
        lax.psum_scatter(
            terms_u.astype(jnp.bfloat16), "ctx", scatter_dimension=0, tiled=True
        ).astype(jnp.float32),
    )
    grad_d, wpart_d, gpart_d = complete(
        recip_d, normed_d, act_d, down_cot[0], norm_gain[0, 0], kv_weight[0, 0], dquery_d, dkv_d
    )
    grad_u, wpart_u, gpart_u = complete(
        recip_u, normed_u, act_u, up_cot[0], norm_gain[1, 0], kv_weight[1, 0], dquery_u, dkv_u
    )
    wshare, gshare = (
        lax.psum_scatter(
            jnp.stack([wpart_d, wpart_u]).astype(jnp.bfloat16),
            "ctx",
            scatter_dimension=1,
            tiled=True,
        ).astype(jnp.float32),
        lax.psum_scatter(
            jnp.stack([gpart_d, gpart_u]).astype(jnp.bfloat16),
            "ctx",
            scatter_dimension=1,
            tiled=True,
        ).astype(jnp.float32),
    )
    moving = (wshare[1], gshare[1])
    for bit in range(lax.axis_size("section").bit_length() - 1):
        moving = (
            swapped(moving[0].astype(jnp.bfloat16), "section", bit).astype(jnp.float32),
            swapped(moving[1].astype(jnp.bfloat16), "section", bit).astype(jnp.float32),
        )
    mirror_w, mirror_g = moving
    kv_grad = (wshare[0] + mirror_w)[None]
    gain_grad = (gshare[0] + mirror_g)[None]
    return (down_out[None], up_out[None], grad_d[None], grad_u[None], kv_grad, gain_grad)


def solution(mesh):
    in_specs = (
        P("section", "ctx", None),
        P("section", "ctx", None),
        P("section", "ctx", None),
        P("section", "ctx", None),
        P(None, "section", None, None),
        P(None, "section", None),
        P(),
    )
    out_specs = (
        P("section", "ctx", None),
        P("section", "ctx", None),
        P("section", "ctx", None),
        P("section", "ctx", None),
        P("section", "ctx", None),
        P("section", "ctx"),
    )
    return jax.shard_map(
        per_device, mesh=mesh, in_specs=in_specs, out_specs=out_specs, check_vma=False
    )
```

profile of v0, /device:TPU:1, one launch (start us, length us, event | category | flops | bytes accessed | tf_op | source)
XLA Modules:
  0.0 773.1 jit_solution(11362917868456859874)
XLA Ops:
  9.5 5.8 fusion.89
  15.7 5.5 fusion.92
  36.0 20.5 %all-gather.3.cloned.1.call-done = bf16[2048,1024]{1,0:T(8,128)(2,1)} async-done(((bf16[128,1024]{1,0:T(8,128)(2,1)}), bf16[2048,1024]{1,0:T(8,128)(2,1)}) %all-gather.3.cloned.1.call-update) | async-done | bytes 4194320 | tf_op jit(solution)/shard_map/all_gather | solution.py:76
  56.5 6.5 copy.99
  63.0 32.7 %all-gather.5.cloned.1.call-done = bf16[2048,1024]{1,0:T(8,128)(2,1)} async-done(((bf16[128,1024]{1,0:T(8,128)(2,1)}), bf16[2048,1024]{1,0:T(8,128)(2,1)}) %all-gather.5.cloned.1.call-update) | async-done | bytes 4194320 | tf_op jit(solution)/shard_map/all_gather | solution.py:77
  95.7 6.6 copy.101
  105.4 63.4 %while.56 = (s32[]{:T(128)}, f32[4,8,128]{2,1,0:T(8,128)S(1)}, f32[4,8,128]{2,1,0:T(8,128)S(1)}, f32[4,8,128,128]{3,2,1,0:T(8,128)}, f32[4,8,128]{2,1,0:T(8,128)...) while((s32[]{:T(128)}, f32[4,8,128]{2,1,0:T(8,128)S(1)}, ...), condition=%wide.region_13.14_spmd, body=%wide.region_3.13_spmd.sunk | while | flops 2195866112 | bytes 101721720 | solution.py:180
  107.6 9.2 %conditional.8 = ((f32[4,8,128]{2,1,0:T(8,128)S(1)}, f32[4,8,128]{2,1,0:T(8,128)S(1)}, f32[4,8,128,128]{3,2,1,0:T(8,128)})) conditional(s32[]{:T(128)} %convert_element_type.312, (f32[4,8,128]{2,1,0:T(8,128)S(1)}, f32[4,8,128]{2,1,0:T(8,128)S(1)}, f32[4,8,128,128]{3,2,1,0:T(8,128)}) %tuple.168, (s32[512]{0:T(512)S(1)}, s32[128]{0:T(128)S(1)}, ...), branch_computations={%region_5.0_spmd, %region_6.8_spmd} | conditional | flops 1097932800 | bytes 50858604 | solution.py:60
  112.3 3.1 multiply_add_fusion
  116.7 9.1 %conditional.9 = ((f32[4,8,128]{2,1,0:T(8,128)S(1)}, f32[4,8,128]{2,1,0:T(8,128)S(1)}, f32[4,8,128,128]{3,2,1,0:T(8,128)})) conditional(s32[]{:T(128)} %convert_element_type.312, (f32[4,8,128]{2,1,0:T(8,128)S(1)}, f32[4,8,128]{2,1,0:T(8,128)S(1)}, f32[4,8,128,128]{3,2,1,0:T(8,128)}) %tuple.170, (s32[512]{0:T(512)S(1)}, s32[128]{0:T(128)S(1)}, ...), branch_computations={%region_9.9_spmd, %region_10.12_spmd} | conditional | flops 1097932800 | bytes 50858604 | solution.py:60
  121.5 3.1 multiply_add_fusion.2
  127.8 9.2 %conditional.8 = ((f32[4,8,128]{2,1,0:T(8,128)S(1)}, f32[4,8,128]{2,1,0:T(8,128)S(1)}, f32[4,8,128,128]{3,2,1,0:T(8,128)})) conditional(s32[]{:T(128)} %convert_element_type.312, (f32[4,8,128]{2,1,0:T(8,128)S(1)}, f32[4,8,128]{2,1,0:T(8,128)S(1)}, f32[4,8,128,128]{3,2,1,0:T(8,128)}) %tuple.168, (s32[512]{0:T(512)S(1)}, s32[128]{0:T(128)S(1)}, ...), branch_computations={%region_5.0_spmd, %region_6.8_spmd} | conditional | flops 1097932800 | bytes 50858604 | solution.py:60
  132.6 3.1 multiply_add_fusion
  137.0 9.1 %conditional.9 = ((f32[4,8,128]{2,1,0:T(8,128)S(1)}, f32[4,8,128]{2,1,0:T(8,128)S(1)}, f32[4,8,128,128]{3,2,1,0:T(8,128)})) conditional(s32[]{:T(128)} %convert_element_type.312, (f32[4,8,128]{2,1,0:T(8,128)S(1)}, f32[4,8,128]{2,1,0:T(8,128)S(1)}, f32[4,8,128,128]{3,2,1,0:T(8,128)}) %tuple.170, (s32[512]{0:T(512)S(1)}, s32[128]{0:T(128)S(1)}, ...), branch_computations={%region_9.9_spmd, %region_10.12_spmd} | conditional | flops 1097932800 | bytes 50858604 | solution.py:60
  141.7 3.1 multiply_add_fusion.2
  148.1 9.2 %conditional.8 = ((f32[4,8,128]{2,1,0:T(8,128)S(1)}, f32[4,8,128]{2,1,0:T(8,128)S(1)}, f32[4,8,128,128]{3,2,1,0:T(8,128)})) conditional(s32[]{:T(128)} %convert_element_type.312, (f32[4,8,128]{2,1,0:T(8,128)S(1)}, f32[4,8,128]{2,1,0:T(8,128)S(1)}, f32[4,8,128,128]{3,2,1,0:T(8,128)}) %tuple.168, (s32[512]{0:T(512)S(1)}, s32[128]{0:T(128)S(1)}, ...), branch_computations={%region_5.0_spmd, %region_6.8_spmd} | conditional | flops 1097932800 | bytes 50858604 | solution.py:60
  152.8 3.1 multiply_add_fusion
  157.3 9.1 %conditional.9 = ((f32[4,8,128]{2,1,0:T(8,128)S(1)}, f32[4,8,128]{2,1,0:T(8,128)S(1)}, f32[4,8,128,128]{3,2,1,0:T(8,128)})) conditional(s32[]{:T(128)} %convert_element_type.312, (f32[4,8,128]{2,1,0:T(8,128)S(1)}, f32[4,8,128]{2,1,0:T(8,128)S(1)}, f32[4,8,128,128]{3,2,1,0:T(8,128)}) %tuple.170, (s32[512]{0:T(512)S(1)}, s32[128]{0:T(128)S(1)}, ...), branch_computations={%region_9.9_spmd, %region_10.12_spmd} | conditional | flops 1097932800 | bytes 50858604 | solution.py:60
  162.0 3.1 multiply_add_fusion.2
  170.8 2.9 copy.103
  173.7 5.2 fusion.72
  179.1 2.5 broadcast.129.clone.1
  181.5 57.5 %while.58 = (s32[]{:T(128)}, f32[128,4,8,128]{3,0,2,1:T(8,128)S(1)}, bf16[2048,1024]{0,1:T(8,128)(2,1)}, s32[2048]{0:T(1024)S(1)}, s32[]{:T(128)}, /*index=5*/s3...) while((s32[]{:T(128)}, ...), condition=%wide.region_27.0_spmd, body=%wide.region_23.27_spmd.sunk | while | flops 2710110720 | bytes 124509192 | solution.py:128
  183.5 16.5 %conditional.11 = ((f32[128,4,8,128]{3,0,2,1:T(8,128)S(1)}, bf16[2048,1024]{0,1:T(8,128)(2,1)})) conditional(s32[]{:T(128)} %convert_element_type.314, (f32[128,4,8,128]{3,0,2,1:T(8,128)S(1)}, bf16[2048,1024]{0,1:T(8,128)(2,1)}) %tuple.178, (s32[512]{0:T(512)S(1)}, s32[128]{0:T(128)S(1)}, bf16[2048,1024]{0,1:T(8,128)(2,1)}, s32[]{:T(128)}, ...), branch_computations={%region_25.25_spmd, %region_26.26_spmd} | conditional | flops 2710110208 | bytes 124504776 | solution.py:122
  186.3 3.2 fusion.43
  189.5 2.4 bitcast_add_fusion.1
  191.9 5.5 fusion.47
  202.0 16.5 %conditional.11 = ((f32[128,4,8,128]{3,0,2,1:T(8,128)S(1)}, bf16[2048,1024]{0,1:T(8,128)(2,1)})) conditional(s32[]{:T(128)} %convert_element_type.314, (f32[128,4,8,128]{3,0,2,1:T(8,128)S(1)}, bf16[2048,1024]{0,1:T(8,128)(2,1)}) %tuple.178, (s32[512]{0:T(512)S(1)}, s32[128]{0:T(128)S(1)}, bf16[2048,1024]{0,1:T(8,128)(2,1)}, s32[]{:T(128)}, ...), branch_computations={%region_25.25_spmd, %region_26.26_spmd} | conditional | flops 2710110208 | bytes 124504776 | solution.py:122
  204.8 3.2 fusion.43
  210.4 5.5 fusion.47
  220.5 16.5 %conditional.11 = ((f32[128,4,8,128]{3,0,2,1:T(8,128)S(1)}, bf16[2048,1024]{0,1:T(8,128)(2,1)})) conditional(s32[]{:T(128)} %convert_element_type.314, (f32[128,4,8,128]{3,0,2,1:T(8,128)S(1)}, bf16[2048,1024]{0,1:T(8,128)(2,1)}) %tuple.178, (s32[512]{0:T(512)S(1)}, s32[128]{0:T(128)S(1)}, bf16[2048,1024]{0,1:T(8,128)(2,1)}, s32[]{:T(128)}, ...), branch_computations={%region_25.25_spmd, %region_26.26_spmd} | conditional | flops 2710110208 | bytes 124504776 | solution.py:122
  223.3 3.2 fusion.43
  226.5 2.4 bitcast_add_fusion.1
  228.9 5.5 fusion.47
  239.0 7.0 copy.165
  246.4 2.5 broadcast.129.clone
  248.9 57.9 %while.57 = (s32[]{:T(128)}, f32[128,4,8,128]{3,0,2,1:T(8,128)S(1)}, bf16[2048,1024]{0,1:T(8,128)(2,1)}, s32[2048]{0:T(1024)S(1)}, s32[]{:T(128)}, /*index=5*/s3...) while((s32[]{:T(128)}, ...), condition=%wide.region_19.0_spmd, body=%wide.region_15.19_spmd.sunk | while | flops 2710110720 | bytes 124509192 | solution.py:128
  251.1 16.5 %conditional.10 = ((f32[128,4,8,128]{3,0,2,1:T(8,128)S(1)}, bf16[2048,1024]{0,1:T(8,128)(2,1)})) conditional(s32[]{:T(128)} %convert_element_type.313, (f32[128,4,8,128]{3,0,2,1:T(8,128)S(1)}, bf16[2048,1024]{0,1:T(8,128)(2,1)}) %tuple.174, (s32[512]{0:T(512)S(1)}, s32[128]{0:T(128)S(1)}, bf16[2048,1024]{0,1:T(8,128)(2,1)}, s32[]{:T(128)}, ...), branch_computations={%region_17.17_spmd, %region_18.18_spmd} | conditional | flops 2710110208 | bytes 124504776 | solution.py:122
  253.8 3.2 fusion.32
  259.5 5.5 fusion.36
  269.6 16.5 %conditional.10 = ((f32[128,4,8,128]{3,0,2,1:T(8,128)S(1)}, bf16[2048,1024]{0,1:T(8,128)(2,1)})) conditional(s32[]{:T(128)} %convert_element_type.313, (f32[128,4,8,128]{3,0,2,1:T(8,128)S(1)}, bf16[2048,1024]{0,1:T(8,128)(2,1)}) %tuple.174, (s32[512]{0:T(512)S(1)}, s32[128]{0:T(128)S(1)}, bf16[2048,1024]{0,1:T(8,128)(2,1)}, s32[]{:T(128)}, ...), branch_computations={%region_17.17_spmd, %region_18.18_spmd} | conditional | flops 2710110208 | bytes 124504776 | solution.py:122
  272.4 3.2 fusion.32
  278.0 5.5 fusion.36
  288.1 16.7 %conditional.10 = ((f32[128,4,8,128]{3,0,2,1:T(8,128)S(1)}, bf16[2048,1024]{0,1:T(8,128)(2,1)})) conditional(s32[]{:T(128)} %convert_element_type.313, (f32[128,4,8,128]{3,0,2,1:T(8,128)S(1)}, bf16[2048,1024]{0,1:T(8,128)(2,1)}) %tuple.174, (s32[512]{0:T(512)S(1)}, s32[128]{0:T(128)S(1)}, bf16[2048,1024]{0,1:T(8,128)(2,1)}, s32[]{:T(128)}, ...), branch_computations={%region_17.17_spmd, %region_18.18_spmd} | conditional | flops 2710110208 | bytes 124504776 | solution.py:122
  291.0 3.2 fusion.32
  296.6 5.6 fusion.36
  306.8 6.4 copy.163
  313.4 34.5 %reduce-scatter.15.cloned.1.call-done = bf16[128,1024]{1,0:T(8,128)(2,1)} async-done(((bf16[2048,1024]{1,0:T(8,128)(2,1)}), bf16[128,1024]{1,0:T(8,128)(2,1)}) %reduce-scatter.15.cloned.1.call-update) | async-done | bytes 262160
  348.0 7.0 convert_bitcast_fusion
  355.0 76.5 %reduce-scatter.13.cloned.1.call-done = bf16[128,1024]{1,0:T(8,128)(2,1)} async-done(((bf16[2048,1024]{1,0:T(8,128)(2,1)}), bf16[128,1024]{1,0:T(8,128)(2,1)}) %reduce-scatter.13.cloned.1.call-update) | async-done | bytes 262160
  431.5 3.6 convert_bitcast_fusion.1
  435.1 6.8 pad_maximum_fusion
  442.1 2.5 copy.109
  444.7 3.1 copy.161
  447.7 2.6 copy.112
  450.3 3.0 copy.162
  453.3 8.0 %fusion.86 = (bf16[4096]{0:T(1024)(128)(2,1)S(1)}, f32[128]{0:T(128)S(1)}, f32[128,4096]{1,0:T(8,128)S(1)}) fusion(bf16[1,128,4096]{2,1,0:T(8,128)(2,1)S(1)} %copy-done.13, f32[128]{0:T(128)S(1)} %copy-done.35, f32[4096]{0:T(1024)S(1)} %bitcast.344, bf16[128,1024]{1,0:T(8,128)(2,1)S(1)} %copy-done.31, bf16[2,1,4096,1024]{3,2,1,0:T(8,128)(2,1)} %param.25, ...), kind=kOutput, calls=%fused_computation.114 | convolution fusion | flops 1077931904 | bytes 13919232 | tf_op jit(solution)/shard_map/dot_general | solution.py:134
  464.8 158.8 %reduce-scatter.11.cloned.1.call-done = bf16[2,256,1024]{2,1,0:T(8,128)(2,1)} async-done(((bf16[2,4096,1024]{2,1,0:T(8,128)(2,1)}), bf16[2,256,1024]{2,1,0:T(8,128)(2,1)}) %reduce-scatter.11.cloned.1.call-update) | async-done | bytes 1048592 | tf_op jit(solution)/shard_map/reduce_scatter | solution.py:208
  625.9 8.1 %multiply_reduce_fusion = (bf16[4096]{0:T(1024)(128)(2,1)S(1)}, f32[128]{0:T(128)S(1)}, f32[128,4096]{1,0:T(8,128)S(1)}) fusion(bf16[1,128,4096]{2,1,0:T(8,128)(2,1)S(1)} %copy-done.15, f32[128]{0:T(128)S(1)} %copy-done.33, f32[4096]{0:T(1024)S(1)} %bitcast.339, bf16[128,1024]{1,0:T(8,128)(2,1)S(1)} %copy-done.30, bf16[2,1,4096,1024]{3,2,1,0:T(8,128)(2,1)} %param.25, ...), kind=kOutput, calls=%fused_computation.117 | convolution fusion | flops 1077931904 | bytes 13919232 | tf_op jit(solution)/shard_map/dot_general | solution.py:134
  635.6 25.2 %collective-permute-start.3 = (bf16[256,1024]{1,0:T(8,128)(2,1)S(1)}, bf16[256,1024]{1,0:T(8,128)(2,1)}, u32[]{:S(2)}, u32[]{:S(2)}) collective-permute-start(bf16[256,1024]{1,0:T(8,128)(2,1)S(1)} %collective-permute-done.2), channel_id=1, source_target_pairs={{0,32},{32,0},{16,48},{48,16},{64,96},{96,64},{80,112},{112,80},{1... | collective-permute-start | bytes 1572872 | tf_op jit(solution)/shard_map/ppermute | solution.py:27
  664.8 7.2 collective-permute-done.3
  672.0 2.4 collective-permute-start.4
  675.9 73.9 %reduce-scatter.17.cloned.1.call-done = bf16[256,2]{1,0:T(8,128)(2,1)} async-done(((bf16[4096,2]{1,0:T(8,128)(2,1)}), bf16[256,2]{1,0:T(8,128)(2,1)}) %reduce-scatter.17.cloned.1.call-update) | async-done | bytes 1040
  757.2 3.0 collective-permute-start.7
  (279 shorter events, 135.5 us)
Async XLA Ops:
  7.2 49.3 %all-gather.3.cloned.1.call-start = ((), (), s32[]{:S(2)}) async-start(), calls=%async_computation.4 | async-start | bytes 4456448 | tf_op jit(solution)/shard_map/all_gather | solution.py:76
  8.7 15.9 %copy-start.34 = (f32[128]{0:T(128)}, f32[128]{0:T(128)S(1)}, u32[]{:S(2)}) copy-start(f32[128]{0:T(128)S(1)} %add_rsqrt_fusion.1) | copy-start | bytes 1540
  9.5 15.1 %copy-start.28 = (f32[1,1,4096]{2,1,0:T(1,128)}, f32[1,1,4096]{2,1,0:T(1,128)S(1)}, u32[]{:S(2)}) copy-start(f32[1,1,4096]{2,1,0:T(1,128)S(1)} %get-tuple-element.1177) | copy-start | bytes 49156
  9.5 17.7 %copy-start.26 = (f32[1,1,4096]{2,1,0:T(1,128)}, f32[1,1,4096]{2,1,0:T(1,128)S(1)}, u32[]{:S(2)}) copy-start(f32[1,1,4096]{2,1,0:T(1,128)S(1)} %get-tuple-element.1176) | copy-start | bytes 49156
  9.5 5.9 copy-start.14
  15.3 80.4 %all-gather.5.cloned.1.call-start = ((), (), s32[]{:S(2)}) async-start(), calls=%async_computation.5 | async-start | bytes 4456448 | tf_op jit(solution)/shard_map/all_gather | solution.py:77
  15.7 11.6 %copy-start.32 = (f32[128]{0:T(128)}, f32[128]{0:T(128)S(1)}, u32[]{:S(2)}) copy-start(f32[128]{0:T(128)S(1)} %add_rsqrt_fusion) | copy-start | bytes 1540
  15.7 5.6 copy-start.12
  21.2 326.7 %reduce-scatter.15.cloned.1.call-start = ((), (), s32[]{:S(2)}) async-start(), calls=%async_computation.8 | async-start | bytes 4456448
  26.5 6.4 copy-start.8
  27.3 8.0 %copy-start.36 = (s32[16]{0:T(128)S(1)}, s32[16]{0:T(128)}, u32[]{:S(2)}) copy-start(s32[16]{0:T(128)} %param.27) | copy-start | bytes 196
  102.2 3.2 copy-start.10
  110.5 1.8 copy-start.18
  119.6 1.8 copy-start.20
  130.8 1.8 copy-start.18
  139.9 1.8 copy-start.20
  151.0 1.8 copy-start.18
  160.2 1.8 copy-start.20
  186.1 3.4 copy-start
  189.5 2.4 copy-start.2
  191.9 5.5 copy-start.3
  203.3 1.5 copy-start.25
  204.6 3.4 copy-start
  208.0 2.4 copy-start.2
  210.4 5.5 copy-start.3
  223.1 3.3 copy-start
  226.5 2.4 copy-start.2
  228.9 5.5 copy-start.3
  239.0 7.0 copy-start.6
  246.1 2.8 copy-start.9
  246.1 185.4 %reduce-scatter.13.cloned.1.call-start = ((), (), s32[]{:S(2)}) async-start(), calls=%async_computation.7 | async-start | bytes 4456448
  253.7 3.4 copy-start.1
  257.0 2.4 copy-start.4
  259.4 5.5 copy-start.5
  272.2 3.4 copy-start.1
  275.6 2.4 copy-start.4
  278.0 5.5 copy-start.5
  290.8 3.4 copy-start.1
  294.2 2.4 copy-start.4
  296.6 5.6 copy-start.5
  313.3 34.7 %copy-start.27 = (f32[1,1,4096]{2,1,0:T(1,128)S(1)}, f32[1,1,4096]{2,1,0:T(1,128)}, u32[]{:S(2)}) copy-start(f32[1,1,4096]{2,1,0:T(1,128)} %copy-done.26) | copy-start | bytes 49156
  313.3 34.7 %copy-start.33 = (f32[128]{0:T(128)S(1)}, f32[128]{0:T(128)}, u32[]{:S(2)}) copy-start(f32[128]{0:T(128)} %copy-done.32) | copy-start | bytes 1540
  313.3 118.2 %copy-start.13 = (bf16[1,128,4096]{2,1,0:T(8,128)(2,1)S(1)}, bf16[1,128,4096]{2,1,0:T(8,128)(2,1)}, u32[]{:S(2)}) copy-start(bf16[1,128,4096]{2,1,0:T(8,128)(2,1)} %param.21) | copy-start | bytes 3145732
  313.3 118.2 %copy-start.29 = (f32[1,1,4096]{2,1,0:T(1,128)S(1)}, f32[1,1,4096]{2,1,0:T(1,128)}, u32[]{:S(2)}) copy-start(f32[1,1,4096]{2,1,0:T(1,128)} %copy-done.28) | copy-start | bytes 49156
  313.3 118.2 %copy-start.35 = (f32[128]{0:T(128)S(1)}, f32[128]{0:T(128)}, u32[]{:S(2)}) copy-start(f32[128]{0:T(128)} %copy-done.34) | copy-start | bytes 1540
  313.4 310.2 %reduce-scatter.11.cloned.1.call-start = ((), (), s32[]{:S(2)}) async-start(), calls=%async_computation.6 | async-start | bytes 17825792 | tf_op jit(solution)/shard_map/reduce_scatter | solution.py:208
  431.5 3.6 copy-start.11
  441.9 307.9 %reduce-scatter.17.cloned.1.call-start = ((), (), s32[]{:S(2)}) async-start(), calls=%async_computation.9 | async-start | bytes 1114112
  444.7 3.1 copy-start.7
  447.7 5.6 copy-start.31
  453.3 8.1 %copy-start.17 = (f32[128,4096]{1,0:T(8,128)S(1)}, f32[128,4096]{1,0:T(8,128)}, u32[]{:S(2)}) copy-start(f32[128,4096]{1,0:T(8,128)} %copy.161) | copy-start | bytes 6291460
  453.3 8.1 %copy-start.22 = (bf16[1,128,4096]{2,1,0:T(8,128)(2,1)S(1)}, bf16[1,128,4096]{2,1,0:T(8,128)(2,1)}, u32[]{:S(2)}) copy-start(bf16[1,128,4096]{2,1,0:T(8,128)(2,1)} %param.23) | copy-start | bytes 3145732
  461.4 164.5 %copy-start.15 = (bf16[1,128,4096]{2,1,0:T(8,128)(2,1)S(1)}, bf16[1,128,4096]{2,1,0:T(8,128)(2,1)}, u32[]{:S(2)}) copy-start(bf16[1,128,4096]{2,1,0:T(8,128)(2,1)} %param.22) | copy-start | bytes 3145732
  461.4 164.5 %copy-start.30 = (bf16[128,1024]{1,0:T(8,128)(2,1)S(1)}, bf16[128,1024]{1,0:T(8,128)(2,1)}, u32[]{:S(2)}) copy-start(bf16[128,1024]{1,0:T(8,128)(2,1)} %reduce-scatter.15.cloned.1.call-done) | copy-start | bytes 786436
  463.6 298.1 %collective-permute-start = (bf16[128,4096]{1,0:T(8,128)(2,1)}, bf16[128,4096]{1,0:T(8,128)(2,1)S(1)}, u32[]{:S(2)}, u32[]{:S(2)}) collective-permute-start(bf16[128,4096]{1,0:T(8,128)(2,1)} %get-tuple-element.1173), channel_id=1, source_target_pairs={{0,16},{16,32},{32,48},{48,64},{64,80},{80,96},{96,112},{112,0},{1... | collective-permute-start | bytes 3145736 | tf_op jit(solution)/shard_map/ppermute | solution.py:17
  624.6 10.9 %collective-permute-start.2 = (bf16[256,1024]{1,0:T(8,128)(2,1)S(1)}, bf16[256,1024]{1,0:T(8,128)(2,1)S(1)}, u32[]{:S(2)}, u32[]{:S(2)}) collective-permute-start(bf16[256,1024]{1,0:T(8,128)(2,1)S(1)} %slice_bitcast_fusion), channel_id=1, source_target_pairs={{0,16},{16,0},{32,48},{48,32},{64,80},{80,64},{96,112},{112,96},{1... | collective-permute-start | bytes 1572872 | tf_op jit(solution)/shard_map/ppermute | solution.py:27
  625.9 34.8 %copy-start.16 = (f32[128,4096]{1,0:T(8,128)S(1)}, f32[128,4096]{1,0:T(8,128)}, u32[]{:S(2)}) copy-start(f32[128,4096]{1,0:T(8,128)} %copy.162) | copy-start | bytes 6291460
  625.9 34.8 %copy-start.23 = (bf16[1,128,4096]{2,1,0:T(8,128)(2,1)S(1)}, bf16[1,128,4096]{2,1,0:T(8,128)(2,1)}, u32[]{:S(2)}) copy-start(bf16[1,128,4096]{2,1,0:T(8,128)(2,1)} %param.24) | copy-start | bytes 3145732
  635.6 36.4 %collective-permute-start.3 = (bf16[256,1024]{1,0:T(8,128)(2,1)S(1)}, bf16[256,1024]{1,0:T(8,128)(2,1)}, u32[]{:S(2)}, u32[]{:S(2)}) collective-permute-start(bf16[256,1024]{1,0:T(8,128)(2,1)S(1)} %collective-permute-done.2), channel_id=1, source_target_pairs={{0,32},{32,0},{16,48},{48,16},{64,96},{96,64},{80,112},{112,80},{1... | collective-permute-start | bytes 1572872 | tf_op jit(solution)/shard_map/ppermute | solution.py:27
  662.6 99.1 %collective-permute-start.1 = (bf16[128,4096]{1,0:T(8,128)(2,1)S(1)}, bf16[128,4096]{1,0:T(8,128)(2,1)S(1)}, u32[]{:S(2)}, u32[]{:S(2)}) collective-permute-start(bf16[128,4096]{1,0:T(8,128)(2,1)S(1)} %get-tuple-element.1171), channel_id=1, source_target_pairs={{0,112},{16,0},{32,16},{48,32},{64,48},{80,64},{96,80},{112,96},{1... | collective-permute-start | bytes 3145736 | tf_op jit(solution)/shard_map/ppermute | solution.py:17
  672.0 89.7 %collective-permute-start.4 = (bf16[256,1024]{1,0:T(8,128)(2,1)}, bf16[256,1024]{1,0:T(8,128)(2,1)}, u32[]{:S(2)}, u32[]{:S(2)}) collective-permute-start(bf16[256,1024]{1,0:T(8,128)(2,1)} %collective-permute-done.3), channel_id=1, source_target_pairs={{0,64},{64,0},{16,80},{80,16},{32,96},{96,32},{48,112},{112,48},{1... | collective-permute-start | bytes 1572872 | tf_op jit(solution)/shard_map/ppermute | solution.py:27
  750.8 2.5 collective-permute-start.5
  753.3 3.9 collective-permute-start.6
  757.2 3.9 collective-permute-start.7
  (11 other events, 15.3 us)
Sparse Core Ops, SparseCore 0:
  15.4 41.0 all-gather.2
  58.2 37.4 all-gather.4
  246.2 101.7 reduce-scatter.14
  350.2 81.2 reduce-scatter.12
  442.0 181.5 reduce-scatter.10
  676.0 73.6 reduce-scatter.16
where the time goes:
time: 786 us; the launch traced here: 773 us
  waiting for transfers between devices  410 us (52%)
  matrix products  148 us (19%)
  local copies, waits for them, and re-layouts  90 us (11%)
  other arithmetic  54.2 us (7%)
  starting transfers between devices  38.3 us (5%)
  loops' own time  17.3 us (2%)
  between operations  14.7 us (2%)
    unnamed x9, waiting for transfers between devices  185 us
    reduce_scatter x1, waiting for transfers between devices, per_device(): lax.psum_scatter(jnp.stack([wpart_d, wpart_u]).astype(jnp.bfloat16), 'ctx...  159 us
    ppermute x6, starting transfers between devices, swapped(): return lax.ppermute(block, axis, route)  34.5 us
    dot_general x6, matrix products, work(): jnp.einsum('kgtn,tkgd->nkd', prob.astype(jnp.bfloat16), dout, preferred_e...  33.2 us
    all_gather x1, waiting for transfers between devices, gather_all(): lax.all_gather(kv_up, 'ctx', axis=0, tiled=True)  32.7 us
    unnamed x58, local copies, waits for them, and re-layouts  21.5 us
    all_gather x1, waiting for transfers between devices, gather_all(): lax.all_gather(kv_down, 'ctx', axis=0, tiled=True)  20.5 us
    while x6, local copies, waits for them, and re-layouts, per_device(): lax.fori_loop(0, rows // block, forward_step, (start, start))  19.8 us
  transfers between devices with their start and end apart: 14, of which 11 were waited for; matrix products, arithmetic and copies ran while one was open for 17% of the time, Pallas kernels for 0%

commit v1 on v0

v1 whole, which is shorter than its diff:
```python
import functools

import jax
import jax.numpy as jnp
from jax import lax
from jax.experimental import pallas as pl
from jax.experimental.pallas import tpu as pltpu
from jax.sharding import PartitionSpec as P

LOG2E = 1.4426950408889634
NT = (((1,), (1,)), ((), ()))
TN = (((0,), (0,)), ((), ()))
F32 = jnp.float32
BF = jnp.bfloat16


def stack_heads(block):
    return jnp.concatenate([block[:, j * 128:(j + 1) * 128] for j in range(8)], 0)


def spread_heads(rows):
    return jnp.concatenate([rows[j * 128:(j + 1) * 128] for j in range(8)], 1)


def attention_kernel(kf, kb, bvar, tq_ref, inv_ref, q_ref, dy_ref, kv_hbm, mixed_ref, dq_ref, terms_ref,
                     kv_s, dk_s, dv_s, sems):
    nq = q_ref.shape[0]
    head = pl.program_id(0)
    spans = kv_hbm.shape[0]
    scale = 128 ** -0.5
    c = scale * LOG2E

    @pl.when(head == 0)
    def _():
        copies = [pltpu.make_async_copy(kv_hbm.at[inv_ref[t]], kv_s.at[pl.ds(t * 128, 128)], sems.at[t])
                  for t in range(spans)]
        for cp in copies:
            cp.start()
        for cp in copies:
            cp.wait()

    dk_s[...] = jnp.zeros_like(dk_s)
    dv_s[...] = jnp.zeros_like(dv_s)
    kcol = pl.multiple_of(head * 256, 256)
    vcol = pl.multiple_of(head * 256 + 128, 128)

    def span(qi, _):
        t = tq_ref[qi]
        q = stack_heads(q_ref[qi])
        dy = stack_heads(dy_ref[qi])
        rows = q.shape[0]

        def fwd(b, carry, masked):
            m, l, acc = carry
            at = pl.multiple_of(b * kf, kf)
            k = kv_s[pl.ds(at, kf), pl.ds(kcol, 128)]
            v = kv_s[pl.ds(at, kf), pl.ds(vcol, 128)]
            s = lax.dot_general(q, k, NT, preferred_element_type=F32) * c
            if masked:
                kpos = at + lax.broadcasted_iota(jnp.int32, (128, kf), 1)
                qpos = t * 128 + lax.broadcasted_iota(jnp.int32, (128, kf), 0)
                s = jnp.where((kpos <= qpos)[None], s.reshape(8, 128, kf), -1e30).reshape(rows, kf)
            m_new = jnp.maximum(m, jnp.max(s, 1, keepdims=True))
            e = jnp.exp2(s - m_new)
            fade = jnp.exp2(m - m_new)
            l = l * fade + jnp.sum(e, 1, keepdims=True)
            acc = acc * fade + lax.dot_general(e.astype(BF), v, (((1,), (0,)), ((), ())), preferred_element_type=F32)
            return m_new, l, acc

        nf = (t * 128) // kf
        carry = (jnp.full((rows, 1), -1e30, F32), jnp.zeros((rows, 1), F32), jnp.zeros((rows, 128), F32))
        carry = lax.fori_loop(0, nf, lambda b, cr: fwd(b, cr, False), carry)
        m, l, acc = fwd(nf, carry, True)
        mixed = acc / l
        mixed_ref[qi] = spread_heads(mixed).astype(mixed_ref.dtype)
        lse = m + jnp.log2(l)
        delta = jnp.sum(dy.astype(F32) * mixed, 1, keepdims=True)
        lse_r = jnp.transpose(jnp.broadcast_to(lse, (rows, 128)))[0:1]
        delta_r = jnp.transpose(jnp.broadcast_to(delta, (rows, 128)))[0:1]

        def bwd(b, dq, masked):
            at = pl.multiple_of(b * kb, kb)
            k = kv_s[pl.ds(at, kb), pl.ds(kcol, 128)]
            v = kv_s[pl.ds(at, kb), pl.ds(vcol, 128)]
            s = lax.dot_general(k, q, NT, preferred_element_type=F32) * c
            p = jnp.exp2(s - lse_r)
            if masked:
                kpos = at + lax.broadcasted_iota(jnp.int32, (kb, 128), 0)
                qpos = t * 128 + lax.broadcasted_iota(jnp.int32, (kb, 128), 1)
                vis = kpos <= qpos
                p = jnp.concatenate([jnp.where(vis, p[:, j * 128:(j + 1) * 128], 0.0) for j in range(8)], 1)
            dp = lax.dot_general(v, dy, NT, preferred_element_type=F32)
            ds = (p * (dp - delta_r)).astype(BF)
            dv_s[pl.ds(at, kb)] += jnp.dot(p.astype(BF), dy, preferred_element_type=F32)
            dk_s[pl.ds(at, kb)] += jnp.dot(ds, q, preferred_element_type=F32)
            if bvar == 0:
                return dq + lax.dot_general(ds, k, TN, preferred_element_type=F32)
            return dq + lax.dot_general(k, ds, TN, preferred_element_type=F32)

        nb = (t * 128) // kb
        dq = jnp.zeros((rows, 128) if bvar == 0 else (128, rows), F32)
        dq = lax.fori_loop(0, nb, lambda b, cr: bwd(b, cr, False), dq)
        dq = bwd(nb, dq, True)
        if bvar != 0:
            dq = jnp.transpose(dq)
        dq_ref[qi] = spread_heads(dq * scale).astype(dq_ref.dtype)
        return 0

    lax.fori_loop(0, nq, span, 0)
    for t in range(spans):
        at = pl.ds(pl.multiple_of(inv_ref[t] * 128, 128), 128)
        terms_ref[at, 0:128] = (dk_s[t * 128:(t + 1) * 128] * scale).astype(BF)
        terms_ref[at, 128:256] = dv_s[t * 128:(t + 1) * 128].astype(BF)


def attention(q, dy, kv, tq, inv, kf=512, kb=256, bvar=0, vmem=50 << 20):
    nq, tok, width = q.shape
    nh = width // 1024
    spans = kv.shape[0]
    smem = pl.BlockSpec(memory_space=pltpu.SMEM)
    qspec = pl.BlockSpec((nq, tok, 1024), lambda h: (0, 0, h))
    flops = 2 * 7 * nq * nh * 1024 * spans * 128 * 128
    return pl.pallas_call(
        functools.partial(attention_kernel, kf, kb, bvar),
        grid=(nh,),
        in_specs=[smem, smem, qspec, qspec, pl.BlockSpec(memory_space=pl.ANY)],
        out_specs=[qspec, qspec, pl.BlockSpec((spans * 128, 256), lambda h: (0, h))],
        out_shape=[jax.ShapeDtypeStruct(q.shape, BF), jax.ShapeDtypeStruct(q.shape, BF),
                   jax.ShapeDtypeStruct((spans * 128, nh * 256), BF)],
        scratch_shapes=[pltpu.VMEM((spans * 128, nh * 256), BF), pltpu.VMEM((spans * 128, 128), F32),
                        pltpu.VMEM((spans * 128, 128), F32), pltpu.SemaphoreType.DMA((spans,))],
        compiler_params=pltpu.CompilerParams(vmem_limit_bytes=vmem),
        cost_estimate=pl.CostEstimate(flops=flops, bytes_accessed=16 << 20, transcendentals=0),
        name="attention",
    )(tq, inv, q, dy, kv)


MESH_ID = pl.DeviceIdType.MESH
EPS = 1e-05
DOWN, UP = 0, 1
OWN, PAIR = 0, 1
UNITS = [(UP, OWN), (UP, PAIR), (DOWN, OWN), (DOWN, PAIR)]


class Place:
    def __init__(self):
        self.me = lax.axis_index("ctx")
        self.core = self.me % 2
        self.chip = self.me // 2
        beside = self.chip % 2
        self.partner = self.me + 1 - 2 * self.core
        self.across = self.me + 2 - 4 * beside
        self.above = (self.me + 4) % 16
        self.below = (self.me + 12) % 16
        self.chip_x = self.chip + 1 - 2 * beside

    def greet(self, barrier):
        for dev in (self.partner, self.across, self.above, self.below):
            pl.semaphore_signal(barrier, inc=1, device_id={"ctx": dev}, device_id_type=MESH_ID)
        pl.semaphore_wait(barrier, 4)

    def span(self, chip, kind):
        return 2 * chip + (self.core if kind == OWN else 1 - self.core)

    def up(self, chip, by):
        return (chip + 2 * by) % 8


class Wires:
    def __init__(self, send_sem, recv_sem):
        self.send_sem, self.recv_sem, self.started = send_sem, recv_sem, []

    def copy(self, index, src, dst, dev):
        return pltpu.make_async_remote_copy(
            src_ref=src, dst_ref=dst, send_sem=self.send_sem.at[index], recv_sem=self.recv_sem.at[index],
            device_id={"ctx": dev}, device_id_type=MESH_ID)

    def send(self, index, src, dst, dev):
        copy = self.copy(index, src, dst, dev)
        copy.start()
        self.started.append(copy)

    def arrive(self, index, ref, dev):
        self.copy(index, ref, ref, dev).wait_recv()

    def finish(self):
        for copy in self.started:
            copy.wait_send()


X, ZM, ZP, XZM, XZP, AN, XA = range(7)


def gather_first(place, wires, base, unit, src, slot):
    kind = unit[1]
    at = base + 7 * UNITS.index(unit)
    here = slot(unit, place.chip)
    wires.send(at + X, src, here, place.across)
    wires.send(at + ZM, src, here, place.above)
    wires.send(at + ZP, src, here, place.below)


def gather_second(place, wires, base, unit, slot, landed):
    kind = unit[1]
    at = base + 7 * UNITS.index(unit)
    cx = slot(unit, place.chip_x)
    wires.arrive(at + X, cx, place.across)
    wires.send(at + XZM, cx, cx, place.above)
    wires.send(at + XZP, cx, cx, place.below)
    landed(unit, place.chip_x)
    lo, hi = slot(unit, place.up(place.chip, 3)), slot(unit, place.up(place.chip, 1))
    wires.arrive(at + ZM, lo, place.below)
    if kind == OWN:
        wires.send(at + AN, lo, lo, place.above)
    wires.arrive(at + ZP, hi, place.above)
    if kind == PAIR:
        wires.send(at + AN, hi, hi, place.below)
    landed(unit, place.up(place.chip, 3))
    landed(unit, place.up(place.chip, 1))


def gather_third(place, wires, base, unit, slot, landed):
    at = base + 7 * UNITS.index(unit)
    far = slot(unit, place.up(place.chip, 2))
    wires.arrive(at + AN, far, place.below if unit[1] == OWN else place.above)
    wires.send(at + XA, far, far, place.across)
    landed(unit, place.up(place.chip, 2))
    for kind, by, dev in ((XZM, 3, place.below), (XZP, 1, place.above)):
        chip = place.up(place.chip_x, by)
        wires.arrive(at + kind, slot(unit, chip), dev)
        landed(unit, chip)


def gather_last(place, wires, base, unit, slot, landed):
    at = base + 7 * UNITS.index(unit)
    chip = place.up(place.chip_x, 2)
    wires.arrive(at + XA, slot(unit, chip), place.across)
    landed(unit, chip)


def nothing(unit, chip):
    pass


def spread_kernel(act_d, act_u, cot_d, cot_u, kv_d, kv_u, q_d, q_u, dy_d, dy_u, all_d, all_u,
                  send_sem, recv_sem, local_sem):
    place = Place()
    wires = Wires(send_sem, recv_sem)
    place.greet(pltpu.get_barrier_semaphore())
    all_kv, kv = (all_d, all_u), (kv_d, kv_u)
    tok = act_d.shape[0]
    mine = lambda width: pl.ds(pl.multiple_of(place.core * width, width), width)
    other = lambda width: pl.ds(pl.multiple_of((1 - place.core) * width, width), width)
    slot = lambda unit, chip: all_kv[unit[0]].at[place.span(chip, unit[1])]
    local = []

    def keep(src, dst):
        copy = pltpu.make_async_copy(src, dst, local_sem.at[len(local)])
        copy.start()
        local.append(copy)

    for layer in (UP, DOWN):
        wires.send(28 + layer, kv[layer].at[:, other(512)], all_kv[layer].at[place.me], place.partner)
    for layer in (UP, DOWN):
        gather_first(place, wires, 0, (layer, OWN), kv[layer].at[:, mine(512)], slot)
        keep(kv[layer].at[:, mine(512)], all_kv[layer].at[place.me])
    at = 30
    for src, dst in ((act_u, q_u), (cot_u, dy_u), (act_d, q_d), (cot_d, dy_d)):
        wires.send(at, src.at[:, other(2048)], dst.at[place.core], place.partner)
        keep(src.at[:, mine(2048)], dst.at[place.core])
        at += 1
    for layer in (UP, DOWN):
        wires.arrive(28 + layer, all_kv[layer].at[place.partner], place.partner)
        gather_first(place, wires, 0, (layer, PAIR), slot((layer, PAIR), place.chip), slot)
    for unit in UNITS:
        gather_second(place, wires, 0, unit, slot, nothing)
    for unit in UNITS:
        gather_third(place, wires, 0, unit, slot, nothing)
    for unit in UNITS:
        gather_last(place, wires, 0, unit, slot, nothing)
    at = 30
    for dst in (q_u, dy_u, q_d, dy_d):
        wires.arrive(at, dst.at[1 - place.core], place.partner)
        at += 1
    for copy in local:
        copy.wait()
    wires.finish()


def spread(act_d, act_u, cot_d, cot_u, kv_d, kv_u):
    half = jax.ShapeDtypeStruct((2, 128, 2048), BF)
    whole = jax.ShapeDtypeStruct((16, 128, 512), BF)
    hbm = pl.BlockSpec(memory_space=pl.ANY)
    return pl.pallas_call(
        spread_kernel,
        in_specs=[hbm] * 6,
        out_specs=[hbm] * 6,
        out_shape=[half] * 4 + [whole] * 2,
        scratch_shapes=[pltpu.SemaphoreType.DMA((34,)), pltpu.SemaphoreType.DMA((34,)), pltpu.SemaphoreType.DMA((6,))],
        compiler_params=pltpu.CompilerParams(collective_id=1, has_side_effects=True),
        name="spread",
    )(act_d, act_u, cot_d, cot_u, kv_d, kv_u)


R0, RA, RB, R1, RU, RD, RX = range(7)


def reduce_kernel(terms_d, terms_u, mix_d, mix_u, dq_d, dq_u, mixed_d, mixed_u, dquery_d, dquery_u, all_d, all_u,
                  slots, stage, total, send_sem, recv_sem, local_sem):
    place = Place()
    wires = Wires(send_sem, recv_sem)
    place.greet(pltpu.get_barrier_semaphore())
    terms, all_kv = (terms_d, terms_u), (all_d, all_u)
    mine = pl.ds(pl.multiple_of(place.core * 512, 512), 512)
    wide = pl.ds(pl.multiple_of(place.core * 2048, 2048), 2048)
    chip, chip_x = place.chip, place.chip_x
    local = []

    def term(unit, at):
        return terms[unit[0]].at[pl.ds(pl.multiple_of(place.span(at, unit[1]) * 128, 128), 128)]

    def plus(*refs):
        value = refs[0][...].astype(F32)
        for ref in refs[1:]:
            value = value + ref[...].astype(F32)
        return value.astype(BF)

    for n, unit in enumerate(UNITS):
        at = 7 * n
        wires.send(at + R0, term(unit, place.up(chip_x, 2)), slots.at[at + R0], place.across)
        wires.send(at + RA, term(unit, place.up(chip_x, 1)), slots.at[at + RA], place.above)
        wires.send(at + RB, term(unit, place.up(chip_x, 3)), slots.at[at + RB], place.below)
        if unit[1] == OWN:
            wires.send(at + RD, term(unit, place.up(chip, 1)), slots.at[at + RD], place.above)
        else:
            wires.send(at + RU, term(unit, place.up(chip, 3)), slots.at[at + RU], place.below)
    index = 56 + 32
    for src, dst in ((mix_u, mixed_u), (mix_d, mixed_d), (dq_u, dquery_u), (dq_d, dquery_d)):
        wires.send(index, src.at[1 - place.core], dst.at[:, wide], place.partner)
        copy = pltpu.make_async_copy(src.at[place.core], dst.at[:, wide], local_sem.at[len(local)])
        copy.start()
        local.append(copy)
        index += 1
    for n, unit in enumerate(UNITS):
        at = 7 * n
        wires.arrive(at + R0, slots.at[at + R0], place.across)
        stage[3 * n] = plus(slots.at[at + R0], term(unit, place.up(chip, 2)))
        wires.send(at + R1, stage.at[3 * n], slots.at[at + R1], place.below if unit[1] == OWN else place.above)
    for n, unit in enumerate(UNITS):
        at = 7 * n
        wires.arrive(at + RA, slots.at[at + RA], place.below)
        wires.arrive(at + RB, slots.at[at + RB], place.above)
        stage[3 * n + 1] = plus(slots.at[at + RA], slots.at[at + RB], term(unit, chip_x))
        wires.send(at + RX, stage.at[3 * n + 1], slots.at[at + RX], place.across)
        if unit[1] == OWN:
            wires.arrive(at + R1, slots.at[at + R1], place.above)
            stage[3 * n + 2] = plus(slots.at[at + R1], term(unit, place.up(chip, 3)))
            wires.send(at + RU, stage.at[3 * n + 2], slots.at[at + RU], place.below)
        else:
            wires.arrive(at + R1, slots.at[at + R1], place.below)
            stage[3 * n + 2] = plus(slots.at[at + R1], term(unit, place.up(chip, 1)))
            wires.send(at + RD, stage.at[3 * n + 2], slots.at[at + RD], place.above)

    slot = lambda unit, at: all_kv[unit[0]].at[place.span(at, unit[1]), :, mine]
    passed = [0]

    def hand_over(unit, at):
        ref = slot(unit, at)
        wires.send(56 + passed[0], ref, ref, place.partner)
        passed[0] += 1

    order = []

    def landed(unit, at):
        order.append((unit, at))
        hand_over(unit, at)

    for n, unit in enumerate(UNITS):
        at = 7 * n
        wires.arrive(at + RX, slots.at[at + RX], place.across)
        wires.arrive(at + RU, slots.at[at + RU], place.above)
        wires.arrive(at + RD, slots.at[at + RD], place.below)
        total[n] = plus(slots.at[at + RX], slots.at[at + RU], slots.at[at + RD], term(unit, chip))
        gather_first(place, wires, 28, unit, total.at[n], slot)
        copy = pltpu.make_async_copy(total.at[n], slot(unit, chip), local_sem.at[len(local)])
        copy.start()
        local.append(copy)
        wires.send(56 + passed[0], total.at[n], slot(unit, chip), place.partner)
        order.append((unit, chip))
        passed[0] += 1
    for unit in UNITS:
        gather_second(place, wires, 28, unit, slot, landed)
    for unit in UNITS:
        gather_third(place, wires, 28, unit, slot, landed)
    for unit in UNITS:
        gather_last(place, wires, 28, unit, slot, landed)
    theirs = pl.ds(pl.multiple_of((1 - place.core) * 512, 512), 512)
    for n, (unit, at) in enumerate(order):
        span = place.span(at, 1 - unit[1])
        wires.arrive(56 + n, all_kv[unit[0]].at[span, :, theirs], place.partner)
    index = 56 + 32
    others = pl.ds(pl.multiple_of((1 - place.core) * 2048, 2048), 2048)
    for dst in (mixed_u, mixed_d, dquery_u, dquery_d):
        wires.arrive(index, dst.at[:, others], place.partner)
        index += 1
    for copy in local:
        copy.wait()
    wires.finish()


def reduce_terms(terms_d, terms_u, mix_d, mix_u, dq_d, dq_u):
    hbm = pl.BlockSpec(memory_space=pl.ANY)
    vmem = pl.BlockSpec(memory_space=pltpu.VMEM)
    row = jax.ShapeDtypeStruct((128, 4096), BF)
    whole = jax.ShapeDtypeStruct((16, 128, 1024), BF)
    return pl.pallas_call(
        reduce_kernel,
        in_specs=[vmem] * 2 + [hbm] * 4,
        out_specs=[hbm] * 6,
        out_shape=[row] * 4 + [whole] * 2,
        scratch_shapes=[pltpu.VMEM((28, 128, 512), BF), pltpu.VMEM((12, 128, 512), BF), pltpu.VMEM((4, 128, 512), BF),
                        pltpu.SemaphoreType.DMA((92,)), pltpu.SemaphoreType.DMA((92,)), pltpu.SemaphoreType.DMA((8,))],
        compiler_params=pltpu.CompilerParams(collective_id=2, has_side_effects=True, vmem_limit_bytes=32 << 20),
        name="reduce_terms",
    )(terms_d, terms_u, mix_d, mix_u, dq_d, dq_u)


def mirror_kernel(wu_ref, g_ref, w_out, gd_out, gu_out, parts, mine, send_sem, recv_sem, local_sem):
    me = lax.axis_index("ctx")
    section = lax.axis_index("section")
    barrier = pltpu.get_barrier_semaphore()
    pl.semaphore_signal(barrier, inc=1, device_id={"section": 7 - section}, device_id_type=MESH_ID)
    for step in range(1, 16):
        pl.semaphore_signal(barrier, inc=1, device_id={"ctx": (me + step) % 16}, device_id_type=MESH_ID)
    pl.semaphore_wait(barrier, 16)
    far = pltpu.make_async_remote_copy(src_ref=wu_ref, dst_ref=w_out, send_sem=send_sem.at[0], recv_sem=recv_sem.at[0],
                                       device_id={"section": 7 - section}, device_id_type=MESH_ID)
    far.start()
    copies = []
    for step in range(1, 16):
        to = (me + step) % 16
        copy = pltpu.make_async_remote_copy(
            src_ref=g_ref.at[to], dst_ref=parts.at[step], send_sem=send_sem.at[step], recv_sem=recv_sem.at[step],
            device_id={"ctx": to}, device_id_type=MESH_ID)
        copy.start()
        copies.append(copy)
    value = g_ref[me]
    for step in range(1, 16):
        copies[step - 1].wait_recv()
        value = value + parts[step]
    mine[...] = value
    gd_out[...] = value
    last = pltpu.make_async_remote_copy(src_ref=mine, dst_ref=gu_out, send_sem=send_sem.at[16], recv_sem=recv_sem.at[16],
                                        device_id={"section": 7 - section}, device_id_type=MESH_ID)
    last.start()
    for copy in copies:
        copy.wait_send()
    last.wait()
    far.wait()


def mirror(wu, gains):
    hbm = pl.BlockSpec(memory_space=pl.ANY)
    vmem = pl.BlockSpec(memory_space=pltpu.VMEM)
    small = jax.ShapeDtypeStruct((8, 256), F32)
    return pl.pallas_call(
        mirror_kernel,
        in_specs=[hbm, vmem],
        out_specs=[hbm, vmem, vmem],
        out_shape=[jax.ShapeDtypeStruct(wu.shape, BF), small, small],
        scratch_shapes=[pltpu.VMEM((16, 8, 256), F32), pltpu.VMEM((8, 256), F32),
                        pltpu.SemaphoreType.DMA((17,)), pltpu.SemaphoreType.DMA((17,)), pltpu.SemaphoreType.DMA((1,))],
        compiler_params=pltpu.CompilerParams(collective_id=3, has_side_effects=True),
        name="mirror",
    )(wu, gains)


def by_head(kv):
    return kv.reshape(-1, 2, 4, 128).transpose(0, 2, 1, 3).reshape(-1, 1024)


def by_kind(kv):
    return kv.reshape(-1, 4, 2, 128).transpose(0, 2, 1, 3).reshape(-1, 1024)


def prepare(x, gain, weight):
    xf = x.astype(F32)
    recip = lax.rsqrt(jnp.mean(xf * xf, -1, keepdims=True) + EPS)
    normed = xf * recip
    act = (normed * gain[None, :]).astype(BF)
    kv = jnp.dot(act, weight, preferred_element_type=F32).astype(BF)
    return recip, act, by_head(kv)


def complete(x, recip, cot, gain, weight, dquery, dkv):
    normed = x.astype(F32) * recip
    dact = dquery.astype(F32) + lax.dot_general(by_kind(dkv), weight, NT, preferred_element_type=F32)
    gpart = jnp.sum(dact * normed, 0)
    dnormed = dact * gain[None, :]
    dx = cot.astype(F32) + recip * (dnormed - normed * jnp.mean(dnormed * normed, -1, keepdims=True))
    return dx.astype(BF), gpart


def weight_grad(features, dkv):
    return lax.dot_general(features, dkv, TN, preferred_element_type=F32)


def shifted(array, by):
    size = lax.axis_size("section")
    return lax.ppermute(array, "section", [(i, (i + by) % size) for i in range(size)])


def per_device(down_in, up_in, down_cot, up_cot, kv_weight, norm_gain, span_ids):
    own = lax.axis_index("ctx")
    x_d, x_u, cot_d, cot_u = down_in[0], up_in[0], down_cot[0], up_cot[0]
    gain_d, gain_u = norm_gain[0, 0], norm_gain[1, 0]
    weight_d, weight_u = kv_weight[0, 0], kv_weight[1, 0]
    recip_u, act_u, kv_u = prepare(x_u, gain_u, weight_u)
    recip_d, act_d, kv_d = prepare(x_d, gain_d, weight_d)
    q_d, q_u, dy_d, dy_u, all_d, all_u = spread(act_d, act_u, cot_d, cot_u, kv_d, kv_u)
    features = jnp.stack([act_d, act_u]).reshape(2, 128, 16, 256).transpose(2, 0, 1, 3)
    features = lax.all_to_all(features, "ctx", 0, 0, tiled=False)
    features = features.transpose(1, 0, 2, 3).reshape(2, 2048, 256)
    times = lax.dynamic_slice_in_dim(span_ids, own // 2 * 2, 2, 0)
    inverse = jnp.argsort(span_ids).astype(jnp.int32)
    mix_u, dq_u, terms_u = attention(q_u, dy_u, all_u, times, inverse)
    mix_d, dq_d, terms_d = attention(q_d, dy_d, all_d, times, inverse)
    mixed_d, mixed_u, dquery_d, dquery_u, dkv_d, dkv_u = reduce_terms(terms_d, terms_u, mix_d, mix_u, dq_d, dq_u)
    y_down = (x_d.astype(F32) + mixed_d.astype(F32)).astype(BF)
    y_up = (x_u.astype(F32) + mixed_u.astype(F32)).astype(BF)
    down_out = shifted(y_down, 1)
    up_out = shifted(y_up, -1)
    wgrad_u = weight_grad(features[1], dkv_u.reshape(2048, 1024)).astype(BF)
    own_dkv = lambda dkv: lax.dynamic_index_in_dim(dkv, own, 0, False)
    grad_u, gpart_u = complete(x_u, recip_u, cot_u, gain_u, weight_u, dquery_u, own_dkv(dkv_u))
    grad_d, gpart_d = complete(x_d, recip_d, cot_d, gain_d, weight_d, dquery_d, own_dkv(dkv_d))
    gains = jnp.stack([gpart_d, gpart_u] + [jnp.zeros_like(gpart_d)] * 6).reshape(8, 16, 256).transpose(1, 0, 2)
    mirror_w, gain_here, gain_there = mirror(wgrad_u, gains)
    wgrad_d = weight_grad(features[0], dkv_d.reshape(2048, 1024))
    kv_grad = by_kind(wgrad_d + mirror_w.astype(F32))[None]
    gain_grad = (gain_here[0] + gain_there[1])[None]
    return (down_out[None], up_out[None], grad_d[None], grad_u[None], kv_grad, gain_grad)


def solution(mesh):
    row = P("section", "ctx", None)
    in_specs = (row, row, row, row, P(None, "section", None, None), P(None, "section", None), P())
    out_specs = (row, row, row, row, row, P("section", "ctx"))
    return jax.shard_map(per_device, mesh=mesh, in_specs=in_specs, out_specs=out_specs, check_vma=False)
```

time: 786 us -> 363 us (0.46); the launches traced: 773 us -> 362 us
  waiting for transfers between devices: 410 us -> 27.3 us
  Pallas kernels: 0 us -> 251 us
  matrix products: 148 us -> 29.4 us
  local copies, waits for them, and re-layouts: 90 us -> 26.6 us
  other arithmetic: 54.2 us -> 14.7 us
  starting transfers between devices: 38.3 us -> 12.7 us
  loops' own time: 17.3 us -> 0 us
  between operations: 14.7 us -> 0.99 us
    pallas_call x0 -> x5, Pallas kernels: none -> 251 us  [the longest x1 79.4 us: reduce_terms(): pl.pallas_call(reduce_kernel, in_specs=[vmem] * 2 + [hbm] * 4, out_specs=...]
    unnamed x9 -> x0, waiting for transfers between devices: 185 us -> none
    reduce_scatter x1 -> x0, waiting for transfers between devices: 159 us -> none  [per_device(): lax.psum_scatter(jnp.stack([wpart_d, wpart_u]).astype(jnp.bfloat16), 'ctx...]
    dot_general x48 -> x6, matrix products: 148 us -> 29.4 us  [the longest x2 14.4 us: complete(): lax.dot_general(by_kind(dkv), weight, NT, preferred_element_type=F32)]
    all_gather x2 -> x0, waiting for transfers between devices: 53.1 us -> none  [the longest x1 32.7 us: gather_all(): lax.all_gather(kv_up, 'ctx', axis=0, tiled=True)]
    ppermute x8 -> x2, starting transfers between devices: 37.8 us -> 4.9 us  [shifted(): lax.ppermute(array, 'section', [(i, (i + by) % size) for i in range(size)])]
    while x8 -> x0, local copies, waits for them, and re-layouts: 25 us -> none  [the longest x6 19.8 us: per_device(): lax.fori_loop(0, rows // block, forward_step, (start, start))]
    another operation x19 -> x0, loops' own time: 17.3 us -> none  [the longest x2 10.3 us: backward_terms(): dquery, terms = lax.fori_loop(0, rows // block, step, start_state)]
  transfers between devices with their start and end apart: 14 -> 3, of which waited for: 11 -> 2; matrix products, arithmetic and copies ran while one was open for 17% -> 11% of each run, Pallas kernels for 0% -> 63%
where the time goes in v1:
time: 363 us; the launch traced here: 362 us
  Pallas kernels  251 us (69%)
  matrix products  29.4 us (8%)
  waiting for transfers between devices  27.3 us (8%)
  local copies, waits for them, and re-layouts  26.6 us (7%)
  other arithmetic  14.7 us (4%)
  starting transfers between devices  12.7 us (3%)
    pallas_call x1, Pallas kernels, reduce_terms(): pl.pallas_call(reduce_kernel, in_specs=[vmem] * 2 + [hbm] * 4, out_specs=...  79.4 us
    pallas_call x1, Pallas kernels, spread(): pl.pallas_call(spread_kernel, in_specs=[hbm] * 6, out_specs=[hbm] * 6, ou...  75.9 us
    pallas_call x2, Pallas kernels, attention(): pl.pallas_call(functools.partial(attention_kernel, kf, kb, bvar), grid=(n...  71.7 us
    ppermute x2, waiting for transfers between devices, shifted(): lax.ppermute(array, 'section', [(i, (i + by) % size) for i in range(size)])  27.3 us
    pallas_call x1, Pallas kernels, mirror(): pl.pallas_call(mirror_kernel, in_specs=[hbm, vmem], out_specs=[hbm, vmem,...  23.8 us
    dot_general x2, matrix products, complete(): lax.dot_general(by_kind(dkv), weight, NT, preferred_element_type=F32)  14.4 us
    unnamed x36, local copies, waits for them, and re-layouts  13.7 us
    dot_general x2, matrix products, prepare(): kv = jnp.dot(act, weight, preferred_element_type=F32).astype(BF)  9.36 us
  transfers between devices with their start and end apart: 3, of which 2 were waited for; matrix products, arithmetic and copies ran while one was open for 11% of the time, Pallas kernels for 63%

profile of v1, /device:TPU:1, one launch (start us, length us, event | category | flops | bytes accessed | tf_op | source)
XLA Modules:
  0.0 362.4 jit_solution(3940715604480247237)
XLA Ops:
  0.6 0.0 copy-start.10
  0.6 0.8 fusion.65
  1.5 1.6 fusion.50
  3.1 1.5 fusion.39
  4.6 0.3 fusion.42
  5.0 0.3 fusion.53
  5.3 0.0 copy-start.12
  5.3 0.2 copy_bitcast_fusion.1
  5.6 0.7 copy-done.12
  6.3 1.5 maximum_bitcast_fusion
  7.8 7.8 %all-to-all-start = ((bf16[16,2,128,256]{3,2,1,0:T(8,128)(2,1)}), bf16[16,2,128,256]{3,2,1,0:T(8,128)(2,1)}, u32[]{:S(2)}, u32[]{:S(2)}) async-start(bf16[16,2,128,256]{3,2,1,0:T(8,128)(2,1)} %maximum_bitcast_fusion), calls=%async_computation | async-start | bytes 4194304 | tf_op jit(solution)/shard_map/all_to_all | solution.py:522
  15.5 2.0 fusion.32
  17.5 4.7 %fusion.54 = bf16[128,1024]{1,0:T(8,128)(2,1)S(1)} fusion(bf16[2,1,4096,1024]{3,2,1,0:T(8,128)(2,1)} %param.11, bf16[1,128,4096]{2,1,0:T(8,128)(2,1)S(1)} %fusion.42), kind=kOutput, calls=%fused_computation.58 | convolution fusion | flops 1073872896 | bytes 9699328 | tf_op jit(solution)/shard_map/dot_general | solution.py:491
  22.2 4.6 %fusion.57 = bf16[128,1024]{1,0:T(8,128)(2,1)S(1)} fusion(bf16[2,1,4096,1024]{3,2,1,0:T(8,128)(2,1)} %param.11, bf16[1,128,4096]{2,1,0:T(8,128)(2,1)S(1)} %copy-done.13), kind=kOutput, calls=%fused_computation.59 | convolution fusion | flops 1073872896 | bytes 9699328 | tf_op jit(solution)/shard_map/dot_general | solution.py:491
  26.9 0.0 copy-start.16
  26.9 0.2 reshape.146
  27.1 0.2 copy.49
  27.3 0.9 reshape.147.kv_d
  28.2 0.2 reshape.148
  28.4 0.2 copy.48
  28.6 0.9 reshape.149.kv_u
  29.4 0.1 dynamic_slice.10.tq_ref
  29.5 1.2 sort.17
  30.8 75.9 %spread.1 = (bf16[2,128,2048]{2,1,0:T(8,128)(2,1)}, bf16[2,128,2048]{2,1,0:T(8,128)(2,1)}, bf16[2,128,2048]{2,1,0:T(8,128)(2,1)}, bf16[2,128,2048]{2,1,0:T(8,128...) custom-call(bf16[128,4096]{1,0:T(8,128)(2,1)} %get-tuple-element.64.act_d, ...), custom_call_target="tpu_custom_call" | custom-call | tf_op jit(solution)/shard_map/spread/pallas_call | solution.py:294
  106.7 1.2 copy-done.7
  107.9 35.7 %attention.3 = (bf16[2,128,2048]{2,1,0:T(8,128)(2,1)S(1)}, bf16[2,128,2048]{2,1,0:T(8,128)(2,1)S(1)}, bf16[2048,512]{1,0:T(8,128)(2,1)}) custom-call(s32[2]{0:T(128)S(1)} %dynamic_slice.10.tq_ref, s32[16]{0:T(128)S(1)} %get-tuple-element.28.inv_ref, bf16[2,128,2048]{2,1,0:T(8,128)(2,1)S(1)} %copy-done.7, bf16[2,128,2048]{2,1,0:T(8,128)(2,1)} %get-tuple-element.34.dy_ref, ...), custom_call_target="tpu_custom_call" | custom-call | flops 15032385536 | bytes 16777216 | tf_op jit(solution)/shard_map/attention/pallas_call | solution.py:123
  143.6 36.0 %attention.2 = (bf16[2,128,2048]{2,1,0:T(8,128)(2,1)S(1)}, bf16[2,128,2048]{2,1,0:T(8,128)(2,1)S(1)}, bf16[2048,512]{1,0:T(8,128)(2,1)}) custom-call(s32[2]{0:T(128)S(1)} %dynamic_slice.10.tq_ref, s32[16]{0:T(128)S(1)} %get-tuple-element.28.inv_ref, bf16[2,128,2048]{2,1,0:T(8,128)(2,1)S(1)} %copy-done.5, bf16[2,128,2048]{2,1,0:T(8,128)(2,1)} %get-tuple-element.30.dy_ref, ...), custom_call_target="tpu_custom_call" | custom-call | flops 15032385536 | bytes 16777216 | tf_op jit(solution)/shard_map/attention/pallas_call | solution.py:123
  179.6 1.6 copy-done.1
  181.2 79.4 %reduce_terms.1 = (bf16[128,4096]{1,0:T(8,128)(2,1)S(1)}, bf16[128,4096]{1,0:T(8,128)(2,1)S(1)}, bf16[128,4096]{1,0:T(8,128)(2,1)S(1)}, bf16[128,4096]{1,0:T(8,1...) custom-call(bf16[2048,512]{1,0:T(8,128)(2,1)S(1)} %copy-done.1, ...), custom_call_target="tpu_custom_call" | custom-call | tf_op jit(solution)/shard_map/reduce_terms/pallas_call | solution.py:416
  260.6 1.9 copy-done.2
  262.5 1.0 copy-done.6
  263.5 2.0 copy-done.3
  265.5 0.8 copy.34
  266.3 1.0 copy.35
  267.3 0.0 copy-start.9
  267.3 0.0 copy-start.14
  267.3 7.4 %fusion.49 = (f32[4096]{0:T(1024)S(1)}, f32[128]{0:T(128)S(1)}, f32[128,4096]{1,0:T(8,128)S(1)}) fusion(bf16[1,128,4096]{2,1,0:T(8,128)(2,1)} %param.8, f32[128]{0:T(128)S(1)} %add_rsqrt_fusion, f32[4096]{0:T(1024)S(1)} %bitcast.173, bf16[128,1024]{0,1:T(8,128)(2,1)S(1)} %bitcast.175, bf16[2,1,4096,1024]{3,2,1,0:T(8,128)(2,1)} %param.11, ...), kind=kOutput, calls=%fused_computation.49 | convolution fusion | flops 1078456192 | bytes 12878848 | tf_op jit(solution)/shard_map/dot_general | solution.py:497
  274.7 2.3 fusion.60
  277.0 4.9 %collective-permute-start.1 = (bf16[128,4096]{1,0:T(8,128)(2,1)}, bf16[128,4096]{1,0:T(8,128)(2,1)S(1)}, u32[]{:S(2)}, u32[]{:S(2)}) collective-permute-start(bf16[128,4096]{1,0:T(8,128)(2,1)} %get-tuple-element.57), channel_id=1, source_target_pairs={{0,112},{16,0},{32,16},{48,32},{64,48},{80,64},{96,80},{112,96},{1... | collective-permute-start | bytes 3145736 | tf_op jit(solution)/shard_map/ppermute | solution.py:510
  281.9 1.0 constant_dynamic-slice_fusion.1
  282.9 0.8 copy.32
  283.7 1.0 copy.33
  284.7 0.0 copy-start.11
  284.7 0.0 copy-start.15
  284.7 7.0 %fusion.38 = (f32[4096]{0:T(1024)S(1)}, f32[128]{0:T(128)S(1)}, f32[128,4096]{1,0:T(8,128)S(1)}) fusion(bf16[1,128,4096]{2,1,0:T(8,128)(2,1)} %param.7, f32[128]{0:T(128)S(1)} %add_rsqrt_fusion.1, f32[4096]{0:T(1024)S(1)} %bitcast.169, bf16[128,1024]{0,1:T(8,128)(2,1)S(1)} %bitcast.176, bf16[2,1,4096,1024]{3,2,1,0:T(8,128)(2,1)} %param.11, ...), kind=kOutput, calls=%fused_computation.38 | convolution fusion | flops 1078456192 | bytes 12878848 | tf_op jit(solution)/shard_map/dot_general | solution.py:497
  291.8 1.9 fusion.61
  293.7 0.0 collective-permute-start
  293.7 0.1 pad.2.clone
  293.7 0.1 pad.3.clone
  293.8 0.7 maximum_bitcast_fusion.1.g_ref
  294.6 10.2 %collective-permute-done.1 = bf16[128,4096]{1,0:T(8,128)(2,1)S(1)} collective-permute-done((bf16[128,4096]{1,0:T(8,128)(2,1)}, bf16[128,4096]{1,0:T(8,128)(2,1)S(1)}, u32[]{:S(2)}, u32[]{:S(2)}) %collective-permute-start.1) | collective-permute-done | bytes 1048608 | tf_op jit(solution)/shard_map/ppermute | solution.py:510
  304.8 17.1 %collective-permute-done = bf16[128,4096]{1,0:T(8,128)(2,1)} collective-permute-done((bf16[128,4096]{1,0:T(8,128)(2,1)S(1)}, bf16[128,4096]{1,0:T(8,128)(2,1)}, u32[]{:S(2)}, u32[]{:S(2)}) %collective-permute-start) | collective-permute-done | bytes 1048608 | tf_op jit(solution)/shard_map/ppermute | solution.py:510
  321.9 1.7 copy.47
  323.6 0.1 fusion.64
  323.8 2.0 copy-done.4
  325.8 2.1 convolution_convert_fusion.wu_ref
  327.9 23.8 %mirror.1 = (bf16[256,1024]{1,0:T(8,128)(2,1)}, f32[8,256]{1,0:T(8,128)}, f32[8,256]{1,0:T(8,128)}) custom-call(bf16[256,1024]{1,0:T(8,128)(2,1)} %convolution_convert_fusion.wu_ref, f32[16,8,256]{2,1,0:T(8,128)} %maximum_bitcast_fusion.1.g_ref), custom_call_target="tpu_custom_call" | custom-call | tf_op jit(solution)/shard_map/mirror/pallas_call | solution.py:466
  351.7 3.6 convolution_add_fusion
  355.3 0.9 reshape.156
  356.2 0.3 copy.39
  356.5 1.4 broadcast_in_dim_reshape.3
  357.8 1.3 slice_add_fusion
  359.1 2.3 copy.52
  361.4 1.0 copy.53
  (29 shorter events, 0.1 us)
Async XLA Ops:
  0.6 4.0 %copy-start.10 = (bf16[1,128,4096]{2,1,0:T(8,128)(2,1)S(1)}, bf16[1,128,4096]{2,1,0:T(8,128)(2,1)}, u32[]{:S(2)}) copy-start(bf16[1,128,4096]{2,1,0:T(8,128)(2,1)} %param.7) | copy-start | bytes 3145732
  1.5 3.5 copy-start.8
  5.3 1.0 copy-start.12
  7.8 314.1 %all-to-all-start = ((bf16[16,2,128,256]{3,2,1,0:T(8,128)(2,1)}), bf16[16,2,128,256]{3,2,1,0:T(8,128)(2,1)}, u32[]{:S(2)}, u32[]{:S(2)}) async-start(bf16[16,2,128,256]{3,2,1,0:T(8,128)(2,1)} %maximum_bitcast_fusion), calls=%async_computation | async-start | bytes 4194304 | tf_op jit(solution)/shard_map/all_to_all | solution.py:522
  17.5 4.7 %copy-start.13 = (bf16[1,128,4096]{2,1,0:T(8,128)(2,1)S(1)}, bf16[1,128,4096]{2,1,0:T(8,128)(2,1)}, u32[]{:S(2)}) copy-start(bf16[1,128,4096]{2,1,0:T(8,128)(2,1)} %copy-done.12) | copy-start | bytes 3145732
  26.9 2.6 copy-start.16
  106.7 1.2 copy-start.7
  107.9 35.7 %copy-start.5 = (bf16[2,128,2048]{2,1,0:T(8,128)(2,1)S(1)}, bf16[2,128,2048]{2,1,0:T(8,128)(2,1)}, u32[]{:S(2)}) copy-start(bf16[2,128,2048]{2,1,0:T(8,128)(2,1)} %get-tuple-element.29.q_ref) | copy-start | bytes 3145732
  143.6 36.0 %copy-start = (bf16[2048,512]{1,0:T(8,128)(2,1)S(1)}, bf16[2048,512]{1,0:T(8,128)(2,1)}, u32[]{:S(2)}) copy-start(bf16[2048,512]{1,0:T(8,128)(2,1)} %get-tuple-element.36.terms_u) | copy-start | bytes 6291460
  179.6 1.6 copy-start.1
  260.6 1.9 copy-start.2
  262.5 1.0 copy-start.6
  263.5 2.0 copy-start.3
  267.3 7.4 %copy-start.9 = (bf16[1,128,4096]{2,1,0:T(8,128)(2,1)S(1)}, bf16[1,128,4096]{2,1,0:T(8,128)(2,1)}, u32[]{:S(2)}) copy-start(bf16[1,128,4096]{2,1,0:T(8,128)(2,1)} %param.8) | copy-start | bytes 3145732
  267.3 7.4 %copy-start.14 = (bf16[1,128,4096]{2,1,0:T(8,128)(2,1)S(1)}, bf16[1,128,4096]{2,1,0:T(8,128)(2,1)}, u32[]{:S(2)}) copy-start(bf16[1,128,4096]{2,1,0:T(8,128)(2,1)} %param.10) | copy-start | bytes 3145732
  277.0 27.8 %collective-permute-start.1 = (bf16[128,4096]{1,0:T(8,128)(2,1)}, bf16[128,4096]{1,0:T(8,128)(2,1)S(1)}, u32[]{:S(2)}, u32[]{:S(2)}) collective-permute-start(bf16[128,4096]{1,0:T(8,128)(2,1)} %get-tuple-element.57), channel_id=1, source_target_pairs={{0,112},{16,0},{32,16},{48,32},{64,48},{80,64},{96,80},{112,96},{1... | collective-permute-start | bytes 3145736 | tf_op jit(solution)/shard_map/ppermute | solution.py:510
  284.7 7.1 %copy-start.11 = (bf16[1,128,4096]{2,1,0:T(8,128)(2,1)S(1)}, bf16[1,128,4096]{2,1,0:T(8,128)(2,1)}, u32[]{:S(2)}) copy-start(bf16[1,128,4096]{2,1,0:T(8,128)(2,1)} %param.7) | copy-start | bytes 3145732
  284.7 7.1 %copy-start.15 = (bf16[1,128,4096]{2,1,0:T(8,128)(2,1)S(1)}, bf16[1,128,4096]{2,1,0:T(8,128)(2,1)}, u32[]{:S(2)}) copy-start(bf16[1,128,4096]{2,1,0:T(8,128)(2,1)} %param.9) | copy-start | bytes 3145732
  293.7 28.2 %collective-permute-start = (bf16[128,4096]{1,0:T(8,128)(2,1)S(1)}, bf16[128,4096]{1,0:T(8,128)(2,1)}, u32[]{:S(2)}, u32[]{:S(2)}) collective-permute-start(bf16[128,4096]{1,0:T(8,128)(2,1)S(1)} %get-tuple-element.59), channel_id=1, source_target_pairs={{0,16},{16,32},{32,48},{48,64},{64,80},{80,96},{96,112},{112,0},{1... | collective-permute-start | bytes 3145736 | tf_op jit(solution)/shard_map/ppermute | solution.py:510
  323.6 2.2 copy-start.4

commit v2 on v1

--- a/solution.py
+++ b/solution.py
@@ -22,7 +22,7 @@
     return jnp.concatenate([rows[j * 128:(j + 1) * 128] for j in range(8)], 1)
 
 
-def attention_kernel(kf, kb, bvar, tq_ref, inv_ref, q_ref, dy_ref, kv_hbm, mixed_ref, dq_ref, terms_ref,
+def attention_kernel(first, kf, kb, tq_ref, inv_ref, q_ref, dy_ref, x_ref, kv_hbm, y_ref, dq_ref, terms_ref,
                      kv_s, dk_s, dv_s, sems):
     nq = q_ref.shape[0]
     head = pl.program_id(0)
@@ -32,7 +32,7 @@
 
     @pl.when(head == 0)
     def _():
-        copies = [pltpu.make_async_copy(kv_hbm.at[inv_ref[t]], kv_s.at[pl.ds(t * 128, 128)], sems.at[t])
+        copies = [pltpu.make_async_copy(kv_hbm.at[inv_ref[t], :, pl.ds(first * 256, kv_s.shape[1])], kv_s.at[pl.ds(t * 128, 128)], sems.at[t])
                   for t in range(spans)]
         for cp in copies:
             cp.start()
@@ -72,7 +72,7 @@
         carry = lax.fori_loop(0, nf, lambda b, cr: fwd(b, cr, False), carry)
         m, l, acc = fwd(nf, carry, True)
         mixed = acc / l
-        mixed_ref[qi] = spread_heads(mixed).astype(mixed_ref.dtype)
+        y_ref[qi] = (x_ref[qi].astype(F32) + spread_heads(mixed)).astype(y_ref.dtype)
         lse = m + jnp.log2(l)
         delta = jnp.sum(dy.astype(F32) * mixed, 1, keepdims=True)
         lse_r = jnp.transpose(jnp.broadcast_to(lse, (rows, 128)))[0:1]
@@ -93,16 +93,12 @@
             ds = (p * (dp - delta_r)).astype(BF)
             dv_s[pl.ds(at, kb)] += jnp.dot(p.astype(BF), dy, preferred_element_type=F32)
             dk_s[pl.ds(at, kb)] += jnp.dot(ds, q, preferred_element_type=F32)
-            if bvar == 0:
-                return dq + lax.dot_general(ds, k, TN, preferred_element_type=F32)
-            return dq + lax.dot_general(k, ds, TN, preferred_element_type=F32)
+            return dq + lax.dot_general(ds, k, TN, preferred_element_type=F32)
 
         nb = (t * 128) // kb
-        dq = jnp.zeros((rows, 128) if bvar == 0 else (128, rows), F32)
+        dq = jnp.zeros((rows, 128), F32)
         dq = lax.fori_loop(0, nb, lambda b, cr: bwd(b, cr, False), dq)
         dq = bwd(nb, dq, True)
-        if bvar != 0:
-            dq = jnp.transpose(dq)
         dq_ref[qi] = spread_heads(dq * scale).astype(dq_ref.dtype)
         return 0
 
@@ -113,33 +109,33 @@
         terms_ref[at, 128:256] = dv_s[t * 128:(t + 1) * 128].astype(BF)
 
 
-def attention(q, dy, kv, tq, inv, kf=512, kb=256, bvar=0, vmem=50 << 20):
-    nq, tok, width = q.shape
-    nh = width // 1024
+def attention(q, dy, x, kv, tq, inv, first, count, kf=1024, kb=512):
+    nq, tok, _ = q.shape
     spans = kv.shape[0]
     smem = pl.BlockSpec(memory_space=pltpu.SMEM)
-    qspec = pl.BlockSpec((nq, tok, 1024), lambda h: (0, 0, h))
-    flops = 2 * 7 * nq * nh * 1024 * spans * 128 * 128
+    qspec = pl.BlockSpec((nq, tok, 1024), lambda h: (0, 0, first + h))
+    ospec = pl.BlockSpec((nq, tok, 1024), lambda h: (0, 0, h))
+    flops = 2 * 7 * nq * count * 1024 * spans * 128 * 128
+    rows = jax.ShapeDtypeStruct((nq, tok, count * 1024), BF)
     return pl.pallas_call(
-        functools.partial(attention_kernel, kf, kb, bvar),
-        grid=(nh,),
-        in_specs=[smem, smem, qspec, qspec, pl.BlockSpec(memory_space=pl.ANY)],
-        out_specs=[qspec, qspec, pl.BlockSpec((spans * 128, 256), lambda h: (0, h))],
-        out_shape=[jax.ShapeDtypeStruct(q.shape, BF), jax.ShapeDtypeStruct(q.shape, BF),
-                   jax.ShapeDtypeStruct((spans * 128, nh * 256), BF)],
-        scratch_shapes=[pltpu.VMEM((spans * 128, nh * 256), BF), pltpu.VMEM((spans * 128, 128), F32),
+        functools.partial(attention_kernel, first, kf, kb),
+        grid=(count,),
+        in_specs=[smem, smem, qspec, qspec, qspec, pl.BlockSpec(memory_space=pl.ANY)],
+        out_specs=[ospec, ospec, pl.BlockSpec((spans * 128, 256), lambda h: (0, h))],
+        out_shape=[rows, rows, jax.ShapeDtypeStruct((spans * 128, count * 256), BF)],
+        scratch_shapes=[pltpu.VMEM((spans * 128, count * 256), BF), pltpu.VMEM((spans * 128, 128), F32),
                         pltpu.VMEM((spans * 128, 128), F32), pltpu.SemaphoreType.DMA((spans,))],
-        compiler_params=pltpu.CompilerParams(vmem_limit_bytes=vmem),
+        compiler_params=pltpu.CompilerParams(vmem_limit_bytes=50 << 20),
         cost_estimate=pl.CostEstimate(flops=flops, bytes_accessed=16 << 20, transcendentals=0),
         name="attention",
-    )(tq, inv, q, dy, kv)
+    )(tq, inv, q, dy, x, kv)
 
 
 MESH_ID = pl.DeviceIdType.MESH
 EPS = 1e-05
 DOWN, UP = 0, 1
 OWN, PAIR = 0, 1
-UNITS = [(UP, OWN), (UP, PAIR), (DOWN, OWN), (DOWN, PAIR)]
+UNITS = [(0, OWN), (0, PAIR), (1, OWN), (1, PAIR)]
 
 
 class Place:
@@ -242,16 +238,15 @@
     pass
 
 
-def spread_kernel(act_d, act_u, cot_d, cot_u, kv_d, kv_u, q_d, q_u, dy_d, dy_u, all_d, all_u,
-                  send_sem, recv_sem, local_sem):
+def spread_kernel(act_d, act_u, cot_d, cot_u, x_d, x_u, kv_d, kv_u,
+                  q_d, q_u, dy_d, dy_u, xh_d, xh_u, pair_d, all_u, send_sem, recv_sem, local_sem):
     place = Place()
     wires = Wires(send_sem, recv_sem)
     place.greet(pltpu.get_barrier_semaphore())
-    all_kv, kv = (all_d, all_u), (kv_d, kv_u)
-    tok = act_d.shape[0]
     mine = lambda width: pl.ds(pl.multiple_of(place.core * width, width), width)
     other = lambda width: pl.ds(pl.multiple_of((1 - place.core) * width, width), width)
-    slot = lambda unit, chip: all_kv[unit[0]].at[place.span(chip, unit[1])]
+    slot = lambda unit, chip: all_u.at[place.span(chip, unit[1]), :, pl.ds(unit[0] * 256, 256)]
+    part = lambda head: pl.ds(pl.multiple_of(place.core * 512 + head * 256, 256), 256)
     local = []
 
     def keep(src, dst):
@@ -259,60 +254,66 @@
         copy.start()
         local.append(copy)
 
-    for layer in (UP, DOWN):
-        wires.send(28 + layer, kv[layer].at[:, other(512)], all_kv[layer].at[place.me], place.partner)
-    for layer in (UP, DOWN):
-        gather_first(place, wires, 0, (layer, OWN), kv[layer].at[:, mine(512)], slot)
-        keep(kv[layer].at[:, mine(512)], all_kv[layer].at[place.me])
-    at = 30
-    for src, dst in ((act_u, q_u), (cot_u, dy_u), (act_d, q_d), (cot_d, dy_d)):
-        wires.send(at, src.at[:, other(2048)], dst.at[place.core], place.partner)
+    wires.send(28, kv_u.at[:, other(512)], all_u.at[place.me], place.partner)
+    for head in range(2):
+        gather_first(place, wires, 0, (head, OWN), kv_u.at[:, part(head)], slot)
+    keep(kv_u.at[:, mine(512)], all_u.at[place.me])
+    wires.arrive(28, all_u.at[place.partner], place.partner)
+    for head in range(2):
+        gather_first(place, wires, 0, (head, PAIR), slot((head, PAIR), place.chip), slot)
+    wires.send(29, kv_d.at[:, other(512)], pair_d.at[place.core], place.partner)
+    keep(kv_d.at[:, mine(512)], pair_d.at[place.core])
+    halves = ((act_u, q_u), (cot_u, dy_u), (x_u, xh_u), (act_d, q_d), (cot_d, dy_d), (x_d, xh_d))
+    for n, (src, dst) in enumerate(halves):
+        wires.send(30 + n, src.at[:, other(2048)], dst.at[place.core], place.partner)
         keep(src.at[:, mine(2048)], dst.at[place.core])
-        at += 1
-    for layer in (UP, DOWN):
-        wires.arrive(28 + layer, all_kv[layer].at[place.partner], place.partner)
-        gather_first(place, wires, 0, (layer, PAIR), slot((layer, PAIR), place.chip), slot)
     for unit in UNITS:
         gather_second(place, wires, 0, unit, slot, nothing)
     for unit in UNITS:
         gather_third(place, wires, 0, unit, slot, nothing)
     for unit in UNITS:
         gather_last(place, wires, 0, unit, slot, nothing)
-    at = 30
-    for dst in (q_u, dy_u, q_d, dy_d):
-        wires.arrive(at, dst.at[1 - place.core], place.partner)
-        at += 1
+    wires.arrive(29, pair_d.at[1 - place.core], place.partner)
+    for n, (src, dst) in enumerate(halves):
+        wires.arrive(30 + n, dst.at[1 - place.core], place.partner)
     for copy in local:
         copy.wait()
     wires.finish()
 
 
-def spread(act_d, act_u, cot_d, cot_u, kv_d, kv_u):
+def spread(*operands):
     half = jax.ShapeDtypeStruct((2, 128, 2048), BF)
-    whole = jax.ShapeDtypeStruct((16, 128, 512), BF)
     hbm = pl.BlockSpec(memory_space=pl.ANY)
     return pl.pallas_call(
         spread_kernel,
-        in_specs=[hbm] * 6,
-        out_specs=[hbm] * 6,
-        out_shape=[half] * 4 + [whole] * 2,
-        scratch_shapes=[pltpu.SemaphoreType.DMA((34,)), pltpu.SemaphoreType.DMA((34,)), pltpu.SemaphoreType.DMA((6,))],
+        in_specs=[hbm] * 8,
+        out_specs=[hbm] * 8,
+        out_shape=[half] * 6 + [jax.ShapeDtypeStruct((2, 128, 512), BF), jax.ShapeDtypeStruct((16, 128, 512), BF)],
+        scratch_shapes=[pltpu.SemaphoreType.DMA((36,)), pltpu.SemaphoreType.DMA((36,)), pltpu.SemaphoreType.DMA((8,))],
         compiler_params=pltpu.CompilerParams(collective_id=1, has_side_effects=True),
         name="spread",
-    )(act_d, act_u, cot_d, cot_u, kv_d, kv_u)
+    )(*operands)
 
 
 R0, RA, RB, R1, RU, RD, RX = range(7)
 
 
-def reduce_kernel(terms_d, terms_u, mix_d, mix_u, dq_d, dq_u, mixed_d, mixed_u, dquery_d, dquery_u, all_d, all_u,
+def reduce_kernel(terms_0, terms_1, y_0, y_1, dq_0, dq_1, wgrad_u, down_out, dquery, all_kv, mirror_w,
                   slots, stage, total, send_sem, recv_sem, local_sem):
     place = Place()
     wires = Wires(send_sem, recv_sem)
-    place.greet(pltpu.get_barrier_semaphore())
-    terms, all_kv = (terms_d, terms_u), (all_d, all_u)
-    mine = pl.ds(pl.multiple_of(place.core * 512, 512), 512)
-    wide = pl.ds(pl.multiple_of(place.core * 2048, 2048), 2048)
+    section = lax.axis_index("section")
+    after, before, mirrored = (section + 1) % 8, (section + 7) % 8, 7 - section
+    barrier = pltpu.get_barrier_semaphore()
+    for there in (after, before):
+        for dev in (place.me, place.partner):
+            pl.semaphore_signal(barrier, inc=1, device_id={"section": there, "ctx": dev}, device_id_type=MESH_ID)
+    pl.semaphore_signal(barrier, inc=1, device_id={"section": mirrored}, device_id_type=MESH_ID)
+    for dev in (place.partner, place.across, place.above, place.below):
+        pl.semaphore_signal(barrier, inc=1, device_id={"ctx": dev}, device_id_type=MESH_ID)
+    pl.semaphore_wait(barrier, 9)
+    terms = (terms_0, terms_1)
+    part = lambda core, head, width: pl.ds(pl.multiple_of(core * 2 * width + head * width, width), width)
     chip, chip_x = place.chip, place.chip_x
     local = []
 
@@ -335,12 +336,24 @@
         else:
             wires.send(at + RU, term(unit, place.up(chip, 3)), slots.at[at + RU], place.below)
     index = 56 + 32
-    for src, dst in ((mix_u, mixed_u), (mix_d, mixed_d), (dq_u, dquery_u), (dq_d, dquery_d)):
-        wires.send(index, src.at[1 - place.core], dst.at[:, wide], place.partner)
-        copy = pltpu.make_async_copy(src.at[place.core], dst.at[:, wide], local_sem.at[len(local)])
+    far = []
+
+    def far_send(src, dst, dev):
+        copy = pltpu.make_async_remote_copy(
+            src_ref=src, dst_ref=dst, send_sem=send_sem.at[index + len(far)], recv_sem=recv_sem.at[index + len(far)],
+            device_id=dev, device_id_type=MESH_ID)
+        copy.start()
+        far.append(copy)
+
+    for head, (y, dq) in enumerate(((y_0, dq_0), (y_1, dq_1))):
+        here = part(place.core, head, 1024)
+        far_send(dq.at[1 - place.core], dquery.at[:, here], {"ctx": place.partner})
+        far_send(y.at[place.core], down_out.at[:, here], {"section": after})
+        far_send(y.at[1 - place.core], down_out.at[:, here], {"section": after, "ctx": place.partner})
+        copy = pltpu.make_async_copy(dq.at[place.core], dquery.at[:, here], local_sem.at[len(local)])
         copy.start()
         local.append(copy)
-        index += 1
+    far_send(wgrad_u, mirror_w, {"section": mirrored})
     for n, unit in enumerate(UNITS):
         at = 7 * n
         wires.arrive(at + R0, slots.at[at + R0], place.across)
@@ -361,7 +374,7 @@
             stage[3 * n + 2] = plus(slots.at[at + R1], term(unit, place.up(chip, 1)))
             wires.send(at + RD, stage.at[3 * n + 2], slots.at[at + RD], place.above)
 
-    slot = lambda unit, at: all_kv[unit[0]].at[place.span(at, unit[1]), :, mine]
+    slot = lambda unit, at: all_kv.at[place.span(at, unit[1]), :, part(place.core, unit[0], 256)]
     passed = [0]
 
     def hand_over(unit, at):
@@ -394,38 +407,33 @@
         gather_third(place, wires, 28, unit, slot, landed)
     for unit in UNITS:
         gather_last(place, wires, 28, unit, slot, landed)
-    theirs = pl.ds(pl.multiple_of((1 - place.core) * 512, 512), 512)
     for n, (unit, at) in enumerate(order):
-        span = place.span(at, 1 - unit[1])
-        wires.arrive(56 + n, all_kv[unit[0]].at[span, :, theirs], place.partner)
-    index = 56 + 32
-    others = pl.ds(pl.multiple_of((1 - place.core) * 2048, 2048), 2048)
-    for dst in (mixed_u, mixed_d, dquery_u, dquery_d):
-        wires.arrive(index, dst.at[:, others], place.partner)
-        index += 1
+        ref = all_kv.at[place.span(at, 1 - unit[1]), :, part(1 - place.core, unit[0], 256)]
+        wires.arrive(56 + n, ref, place.partner)
+    for copy in far:
+        copy.wait()
     for copy in local:
         copy.wait()
     wires.finish()
 
 
-def reduce_terms(terms_d, terms_u, mix_d, mix_u, dq_d, dq_u):
+def reduce_terms(*operands):
     hbm = pl.BlockSpec(memory_space=pl.ANY)
     vmem = pl.BlockSpec(memory_space=pltpu.VMEM)
     row = jax.ShapeDtypeStruct((128, 4096), BF)
-    whole = jax.ShapeDtypeStruct((16, 128, 1024), BF)
     return pl.pallas_call(
         reduce_kernel,
-        in_specs=[vmem] * 2 + [hbm] * 4,
-        out_specs=[hbm] * 6,
-        out_shape=[row] * 4 + [whole] * 2,
-        scratch_shapes=[pltpu.VMEM((28, 128, 512), BF), pltpu.VMEM((12, 128, 512), BF), pltpu.VMEM((4, 128, 512), BF),
-                        pltpu.SemaphoreType.DMA((92,)), pltpu.SemaphoreType.DMA((92,)), pltpu.SemaphoreType.DMA((8,))],
+        in_specs=[vmem] * 2 + [hbm] * 5,
+        out_specs=[hbm] * 4,
+        out_shape=[row] * 2 + [jax.ShapeDtypeStruct((16, 128, 1024), BF), jax.ShapeDtypeStruct((256, 1024), BF)],
+        scratch_shapes=[pltpu.VMEM((28, 128, 256), BF), pltpu.VMEM((12, 128, 256), BF), pltpu.VMEM((4, 128, 256), BF),
+                        pltpu.SemaphoreType.DMA((95,)), pltpu.SemaphoreType.DMA((95,)), pltpu.SemaphoreType.DMA((6,))],
         compiler_params=pltpu.CompilerParams(collective_id=2, has_side_effects=True, vmem_limit_bytes=32 << 20),
         name="reduce_terms",
-    )(terms_d, terms_u, mix_d, mix_u, dq_d, dq_u)
-
-
-def mirror_kernel(wu_ref, g_ref, w_out, gd_out, gu_out, parts, mine, send_sem, recv_sem, local_sem):
+    )(*operands)
+
+
+def gains_kernel(g_ref, gd_out, gu_out, parts, mine, send_sem, recv_sem):
     me = lax.axis_index("ctx")
     section = lax.axis_index("section")
     barrier = pltpu.get_barrier_semaphore()
@@ -433,9 +441,6 @@
     for step in range(1, 16):
         pl.semaphore_signal(barrier, inc=1, device_id={"ctx": (me + step) % 16}, device_id_type=MESH_ID)
     pl.semaphore_wait(barrier, 16)
-    far = pltpu.make_async_remote_copy(src_ref=wu_ref, dst_ref=w_out, send_sem=send_sem.at[0], recv_sem=recv_sem.at[0],
-                                       device_id={"section": 7 - section}, device_id_type=MESH_ID)
-    far.start()
     copies = []
     for step in range(1, 16):
         to = (me + step) % 16
@@ -450,29 +455,27 @@
         value = value + parts[step]
     mine[...] = value
     gd_out[...] = value
-    last = pltpu.make_async_remote_copy(src_ref=mine, dst_ref=gu_out, send_sem=send_sem.at[16], recv_sem=recv_sem.at[16],
+    last = pltpu.make_async_remote_copy(src_ref=mine, dst_ref=gu_out, send_sem=send_sem.at[0], recv_sem=recv_sem.at[0],
                                         device_id={"section": 7 - section}, device_id_type=MESH_ID)
     last.start()
     for copy in copies:
         copy.wait_send()
     last.wait()
-    far.wait()
-
-
-def mirror(wu, gains):
-    hbm = pl.BlockSpec(memory_space=pl.ANY)
+
+
+def sum_gains(gains):
     vmem = pl.BlockSpec(memory_space=pltpu.VMEM)
     small = jax.ShapeDtypeStruct((8, 256), F32)
     return pl.pallas_call(
-        mirror_kernel,
-        in_specs=[hbm, vmem],
-        out_specs=[hbm, vmem, vmem],
-        out_shape=[jax.ShapeDtypeStruct(wu.shape, BF), small, small],
+        gains_kernel,
+        in_specs=[vmem],
+        out_specs=[vmem, vmem],
+        out_shape=[small, small],
         scratch_shapes=[pltpu.VMEM((16, 8, 256), F32), pltpu.VMEM((8, 256), F32),
-                        pltpu.SemaphoreType.DMA((17,)), pltpu.SemaphoreType.DMA((17,)), pltpu.SemaphoreType.DMA((1,))],
+                        pltpu.SemaphoreType.DMA((16,)), pltpu.SemaphoreType.DMA((16,))],
         compiler_params=pltpu.CompilerParams(collective_id=3, has_side_effects=True),
-        name="mirror",
-    )(wu, gains)
+        name="sum_gains",
+    )(gains)
 
 
 def by_head(kv):
@@ -501,42 +504,62 @@
     return dx.astype(BF), gpart
 
 
-def weight_grad(features, dkv):
-    return lax.dot_general(features, dkv, TN, preferred_element_type=F32)
-
-
-def shifted(array, by):
-    size = lax.axis_size("section")
-    return lax.ppermute(array, "section", [(i, (i + by) % size) for i in range(size)])
+def exchanged(array):
+    return lax.ppermute(array, "ctx", [(i, i ^ 1) for i in range(lax.axis_size("ctx"))])
+
+
+def halves_joined(core, mine, other):
+    return jnp.where(core == 0, jnp.concatenate([mine, other], 1), jnp.concatenate([other, mine], 1))
+
+
+def relayed(halves, core, by):
+    sections, spans = lax.axis_size("section"), lax.axis_size("ctx")
+    to = lambda flip: [(s * spans + i, (s + by) % sections * spans + (i ^ flip)) for s in range(sections) for i in range(spans)]
+    pick = lambda which: lax.dynamic_index_in_dim(halves, which, 0, False)
+    mine = lax.ppermute(pick(core), ("section", "ctx"), to(0))
+    other = lax.ppermute(pick(1 - core), ("section", "ctx"), to(1))
+    return halves_joined(core, mine, other)
 
 
 def per_device(down_in, up_in, down_cot, up_cot, kv_weight, norm_gain, span_ids):
     own = lax.axis_index("ctx")
+    core = own % 2
     x_d, x_u, cot_d, cot_u = down_in[0], up_in[0], down_cot[0], up_cot[0]
     gain_d, gain_u = norm_gain[0, 0], norm_gain[1, 0]
     weight_d, weight_u = kv_weight[0, 0], kv_weight[1, 0]
+    same_core = [[i for i in range(16) if i % 2 == c] for c in range(2)]
+    times = lax.dynamic_slice_in_dim(span_ids, own // 2 * 2, 2, 0)
+    inverse = jnp.argsort(span_ids).astype(jnp.int32)
     recip_u, act_u, kv_u = prepare(x_u, gain_u, weight_u)
     recip_d, act_d, kv_d = prepare(x_d, gain_d, weight_d)
-    q_d, q_u, dy_d, dy_u, all_d, all_u = spread(act_d, act_u, cot_d, cot_u, kv_d, kv_u)
+    q_d, q_u, dy_d, dy_u, xh_d, xh_u, pair_d, all_u = spread(act_d, act_u, cot_d, cot_u, x_d, x_u, kv_d, kv_u)
+    all_d = lax.all_gather(pair_d.reshape(256, 512), "ctx", axis=0, axis_index_groups=same_core).reshape(16, 128, 512)
+    act_d, act_u, _ = lax.optimization_barrier((act_d, act_u, pair_d))
     features = jnp.stack([act_d, act_u]).reshape(2, 128, 16, 256).transpose(2, 0, 1, 3)
     features = lax.all_to_all(features, "ctx", 0, 0, tiled=False)
-    features = features.transpose(1, 0, 2, 3).reshape(2, 2048, 256)
-    times = lax.dynamic_slice_in_dim(span_ids, own // 2 * 2, 2, 0)
-    inverse = jnp.argsort(span_ids).astype(jnp.int32)
-    mix_u, dq_u, terms_u = attention(q_u, dy_u, all_u, times, inverse)
-    mix_d, dq_d, terms_d = attention(q_d, dy_d, all_d, times, inverse)
-    mixed_d, mixed_u, dquery_d, dquery_u, dkv_d, dkv_u = reduce_terms(terms_d, terms_u, mix_d, mix_u, dq_d, dq_u)
-    y_down = (x_d.astype(F32) + mixed_d.astype(F32)).astype(BF)
-    y_up = (x_u.astype(F32) + mixed_u.astype(F32)).astype(BF)
-    down_out = shifted(y_down, 1)
-    up_out = shifted(y_up, -1)
-    wgrad_u = weight_grad(features[1], dkv_u.reshape(2048, 1024)).astype(BF)
-    own_dkv = lambda dkv: lax.dynamic_index_in_dim(dkv, own, 0, False)
-    grad_u, gpart_u = complete(x_u, recip_u, cot_u, gain_u, weight_u, dquery_u, own_dkv(dkv_u))
-    grad_d, gpart_d = complete(x_d, recip_d, cot_d, gain_d, weight_d, dquery_d, own_dkv(dkv_d))
+    yh_u, dq_u, terms_u = attention(q_u, dy_u, xh_u, all_u, times, inverse, 0, 2)
+    got_u = lax.all_to_all(terms_u.reshape(8, 256, 512), "ctx", 0, 0, axis_index_groups=same_core, tiled=False)
+    up_out = relayed(yh_u, core, -1)
+    dq_there = exchanged(lax.dynamic_index_in_dim(dq_u, 1 - core, 0, False))
+    yh_d0, dq_d0, terms_d0 = attention(q_d, dy_d, xh_d, all_d, times, inverse, 0, 1)
+    got_u, all_d, terms_d0 = lax.optimization_barrier((got_u, all_d, terms_d0))
+    pair_u = jnp.sum(got_u.astype(F32), 0).astype(BF)
+    dkv_u = lax.all_gather(pair_u, "ctx", axis=0)
+    yh_d1, dq_d1, terms_d1 = attention(q_d, dy_d, xh_d, all_d, times, inverse, 1, 1)
+    dkv_u, terms_d1 = lax.optimization_barrier((dkv_u, terms_d1))
+    dkv_u = dkv_u.reshape(8, 2, 256, 512)
+    wgrad_u = jnp.einsum("ctf,ckth->fkh", features[:, 1].reshape(8, 256, 256), dkv_u, preferred_element_type=F32)
+    wgrad_u = wgrad_u.reshape(256, 1024).astype(BF)
+    down_out, dquery_d, dkv_d, mirror_w = reduce_terms(terms_d0, terms_d1, yh_d0, yh_d1, dq_d0, dq_d1, wgrad_u)
+    dquery_u = halves_joined(core, lax.dynamic_index_in_dim(dq_u, core, 0, False), dq_there)
+    own_u = lax.dynamic_index_in_dim(dkv_u, own // 2, 0, False)
+    own_u = lax.dynamic_slice_in_dim(own_u, core * 128, 128, 1).transpose(1, 0, 2).reshape(128, 1024)
+    own_d = lax.dynamic_index_in_dim(dkv_d, own, 0, False)
+    grad_u, gpart_u = complete(x_u, recip_u, cot_u, gain_u, weight_u, dquery_u, own_u)
+    grad_d, gpart_d = complete(x_d, recip_d, cot_d, gain_d, weight_d, dquery_d, own_d)
     gains = jnp.stack([gpart_d, gpart_u] + [jnp.zeros_like(gpart_d)] * 6).reshape(8, 16, 256).transpose(1, 0, 2)
-    mirror_w, gain_here, gain_there = mirror(wgrad_u, gains)
-    wgrad_d = weight_grad(features[0], dkv_d.reshape(2048, 1024))
+    gain_here, gain_there = sum_gains(gains)
+    wgrad_d = lax.dot_general(features[:, 0].reshape(2048, 256), dkv_d.reshape(2048, 1024), TN, preferred_element_type=F32)
     kv_grad = by_kind(wgrad_d + mirror_w.astype(F32))[None]
     gain_grad = (gain_here[0] + gain_there[1])[None]
     return (down_out[None], up_out[None], grad_d[None], grad_u[None], kv_grad, gain_grad)

time: 363 us -> 469 us (1.29); the launches traced: 362 us -> 464 us
  Pallas kernels: 251 us -> 287 us
  waiting for transfers between devices: 27.3 us -> 57.2 us
  between operations: 0.99 us -> 14.7 us
  local copies, waits for them, and re-layouts: 26.6 us -> 35.6 us
  other arithmetic: 14.7 us -> 20.6 us
    pallas_call x5 -> x6, Pallas kernels: 251 us -> 287 us  [the longest x1 110 us: spread(): pl.pallas_call(spread_kernel, in_specs=[hbm] * 8, out_specs=[hbm] * 8, ou...]
    ppermute x2 -> x3, waiting for transfers between devices: 27.3 us -> 57.2 us  [the longest x1 45.9 us: relayed(): mine = lax.ppermute(pick(core), ('section', 'ctx'), to(0))]
    dot_general x0 -> x1, local copies, waits for them, and re-layouts: none -> 6.75 us  [per_device(): jnp.einsum('ctf,ckth->fkh', features[:, 1].reshape(8, 256, 256), dkv_u, p...]
    unnamed x36 -> x55, local copies, waits for them, and re-layouts: 13.7 us -> 11.4 us
  transfers between devices with their start and end apart: 3 -> 7, of which waited for: 2 -> 2; matrix products, arithmetic and copies ran while one was open for 11% -> 3% of each run, Pallas kernels for 63% -> 21%
where the time goes in v2:
time: 469 us; the launch traced here: 464 us
  Pallas kernels  287 us (61%)
  waiting for transfers between devices  57.2 us (12%)
  local copies, waits for them, and re-layouts  35.6 us (8%)
  matrix products  31.1 us (7%)
  other arithmetic  20.6 us (4%)
  starting transfers between devices  17 us (4%)
  between operations  14.7 us (3%)
    pallas_call x1, Pallas kernels, spread(): pl.pallas_call(spread_kernel, in_specs=[hbm] * 8, out_specs=[hbm] * 8, ou...  110 us
    pallas_call x3, Pallas kernels, attention(): pl.pallas_call(functools.partial(attention_kernel, first, kf, kb), grid=(...  95.6 us
    pallas_call x1, Pallas kernels, reduce_terms(): pl.pallas_call(reduce_kernel, in_specs=[vmem] * 2 + [hbm] * 5, out_specs=...  48.4 us
    ppermute x1, waiting for transfers between devices, relayed(): mine = lax.ppermute(pick(core), ('section', 'ctx'), to(0))  45.9 us
    pallas_call x1, Pallas kernels, sum_gains(): pl.pallas_call(gains_kernel, in_specs=[vmem], out_specs=[vmem, vmem], out...  33.4 us
    dot_general x2, matrix products, complete(): lax.dot_general(by_kind(dkv), weight, NT, preferred_element_type=F32)  16.8 us
    unnamed x55, local copies, waits for them, and re-layouts  11.4 us
    ppermute x1, waiting for transfers between devices, relayed(): other = lax.ppermute(pick(1 - core), ('section', 'ctx'), to(1))  11.2 us
  transfers between devices with their start and end apart: 7, of which 2 were waited for; matrix products, arithmetic and copies ran while one was open for 3% of the time, Pallas kernels for 21%

profile of v2, /device:TPU:1, one launch (start us, length us, event | category | flops | bytes accessed | tf_op | source)
XLA Modules:
  0.0 463.5 jit_solution(17149444619151724119)
XLA Ops:
  7.2 1.6 fusion.30
  8.8 1.5 fusion.38
  10.4 4.8 %fusion.40 = bf16[128,1024]{1,0:T(8,128)(2,1)S(1)} fusion(bf16[2,1,4096,1024]{3,2,1,0:T(8,128)(2,1)} %param.11, bf16[1,128,4096]{2,1,0:T(8,128)(2,1)S(1)} %copy-done.14, f32[4096]{0:T(1024)S(1)} %bitcast.145, f32[128]{0:T(128)S(1)} %add_rsqrt_fusion.1), kind=kOutput, calls=%fused_computation.48 | convolution fusion | flops 1075970048 | bytes 9716224 | tf_op jit(solution)/shard_map/dot_general | solution.py:494
  15.2 4.7 %fusion.43 = bf16[128,1024]{1,0:T(8,128)(2,1)S(1)} fusion(bf16[2,1,4096,1024]{3,2,1,0:T(8,128)(2,1)} %param.11, bf16[1,128,4096]{2,1,0:T(8,128)(2,1)S(1)} %copy-done.16, f32[4096]{0:T(1024)S(1)} %bitcast.141, f32[128]{0:T(128)S(1)} %add_rsqrt_fusion), kind=kOutput, calls=%fused_computation.49 | convolution fusion | flops 1075970048 | bytes 9716224 | tf_op jit(solution)/shard_map/dot_general | solution.py:494
  19.9 2.0 fusion.23
  21.8 0.2 reshape.173
  22.0 0.2 copy.55
  22.2 0.9 reshape.174.kv_d
  23.1 0.2 reshape.175
  23.3 0.2 copy.54
  23.5 0.9 reshape.176.kv_u
  24.4 109.7 %spread.1 = (bf16[2,128,2048]{2,1,0:T(8,128)(2,1)}, bf16[2,128,2048]{2,1,0:T(8,128)(2,1)}, bf16[2,128,2048]{2,1,0:T(8,128)(2,1)}, bf16[2,128,2048]{2,1,0:T(8,128...) custom-call(bf16[128,4096]{1,0:T(8,128)(2,1)} %get-tuple-element.57., ...), custom_call_target="tpu_custom_call" | custom-call | tf_op jit(solution)/shard_map/spread/pallas_call | solution.py:287
  134.1 0.1 dynamic_slice.27.tq_ref
  134.2 1.2 sort.17
  135.5 1.2 copy-done.11
  136.7 47.1 %attention.3 = (bf16[2,128,2048]{2,1,0:T(8,128)(2,1)S(1)}, bf16[2,128,2048]{2,1,0:T(8,128)(2,1)S(1)}, bf16[2048,512]{1,0:T(8,128)(2,1)}) custom-call(s32[2]{0:T(128)S(1)} %dynamic_slice.27.tq_ref, s32[16]{0:T(128)S(1)} %get-tuple-element.37.inv_ref, bf16[2,128,2048]{2,1,0:T(8,128)(2,1)S(1)} %copy-done.11, bf16[2,128,2048]{2,1,0:T(8,128)(2,1)} %get-tuple-element.39.dy_ref, ...), custom_call_target="tpu_custom_call" | custom-call | flops 15032385536 | bytes 16777216 | tf_op jit(solution)/shard_map/attention/pallas_call | solution.py:120
  183.8 4.4 all-to-all-start
  188.3 1.2 copy-done.9
  189.5 24.1 %attention.4 = (bf16[2,128,1024]{2,1,0:T(8,128)(2,1)S(1)}, bf16[2,128,1024]{2,1,0:T(8,128)(2,1)S(1)}, bf16[2048,256]{1,0:T(8,128)(2,1)S(1)}) custom-call(s32[2]{0:T(128)S(1)} %dynamic_slice.27.tq_ref, s32[16]{0:T(128)S(1)} %get-tuple-element.37.inv_ref, bf16[2,128,2048]{2,1,0:T(8,128)(2,1)S(1)} %copy-done.9, bf16[2,128,2048]{2,1,0:T(8,128)(2,1)} %get-tuple-element.45.dy_ref, ...), custom_call_target="tpu_custom_call" | custom-call | flops 7516192768 | bytes 16777216 | tf_op jit(solution)/shard_map/attention/pallas_call | solution.py:120
  213.6 0.8 copy-done
  214.4 0.8 copy-done.2
  215.2 2.6 reduce_sum.68
  217.9 1.6 copy.50
  219.5 0.3 copy.36
  219.8 0.2 copy.51
  220.1 0.3 copy.37
  220.4 1.6 maximum_bitcast_fusion
  222.0 6.5 %all-to-all-start.1 = ((bf16[16,2,128,256]{3,2,1,0:T(8,128)(2,1)}), bf16[16,2,128,256]{3,2,1,0:T(8,128)(2,1)}, u32[]{:S(2)}, u32[]{:S(2)}) async-start(bf16[16,2,128,256]{3,2,1,0:T(8,128)(2,1)} %maximum_bitcast_fusion), calls=%async_computation.1 | async-start | bytes 4194304 | tf_op jit(solution)/shard_map/all_to_all | solution.py:539
  228.5 1.0 dynamic-slice_bitcast_fusion.3
  229.5 5.2 %collective-permute-start = (bf16[128,2048]{1,0:T(8,128)(2,1)}, bf16[128,2048]{1,0:T(8,128)(2,1)S(1)}, u32[]{:S(2)}, u32[]{:S(2)}) collective-permute-start(bf16[128,2048]{1,0:T(8,128)(2,1)} %get-tuple-element.76), channel_id=1, source_target_pairs={{0,112},{1,113},{2,114},{3,115},{4,116},{5,117},{6,118},{7,119},{8... | collective-permute-start | bytes 1572872 | tf_op jit(solution)/shard_map/ppermute | solution.py:519
  234.7 0.8 collective-permute-start.1
  235.6 1.0 dynamic-slice_bitcast_fusion
  236.6 0.1 collective-permute-start.2
  236.6 0.1 pad.3.clone
  236.7 0.1 pad.2.clone
  236.8 45.9 %collective-permute-done = bf16[128,2048]{1,0:T(8,128)(2,1)S(1)} collective-permute-done((bf16[128,2048]{1,0:T(8,128)(2,1)}, bf16[128,2048]{1,0:T(8,128)(2,1)S(1)}, u32[]{:S(2)}, u32[]{:S(2)}) %collective-permute-start) | collective-permute-done | bytes 524320 | tf_op jit(solution)/shard_map/ppermute | solution.py:519
  282.8 11.2 %collective-permute-done.1 = bf16[128,2048]{1,0:T(8,128)(2,1)S(1)} collective-permute-done((bf16[128,2048]{1,0:T(8,128)(2,1)}, bf16[128,2048]{1,0:T(8,128)(2,1)S(1)}, u32[]{:S(2)}, u32[]{:S(2)}) %collective-permute-start.1) | collective-permute-done | bytes 524320 | tf_op jit(solution)/shard_map/ppermute | solution.py:520
  294.0 1.2 maximum_select_fusion
  295.2 3.2 fusion.56
  298.4 24.3 %attention.5 = (bf16[2,128,1024]{2,1,0:T(8,128)(2,1)S(1)}, bf16[2,128,1024]{2,1,0:T(8,128)(2,1)S(1)}, bf16[2048,256]{1,0:T(8,128)(2,1)S(1)}) custom-call(s32[2]{0:T(128)S(1)} %dynamic_slice.27.tq_ref, s32[16]{0:T(128)S(1)} %get-tuple-element.37.inv_ref, bf16[2,128,2048]{2,1,0:T(8,128)(2,1)S(1)} %copy-done.10, ...), custom_call_target="tpu_custom_call" | custom-call | flops 7516192768 | bytes 16777216 | tf_op jit(solution)/shard_map/attention/pallas_call | solution.py:120
  322.7 0.8 copy-done.4
  323.5 0.8 copy-done.6
  324.3 1.0 constant_dynamic-slice_fusion
  325.3 0.2 copy.43
  325.5 8.9 %fusion.37 = (f32[4096]{0:T(1024)S(1)}, f32[128]{0:T(128)S(1)}, f32[128,4096]{1,0:T(8,128)}) fusion(f32[128]{0:T(128)S(1)} %add_rsqrt_fusion, bf16[1,128,4096]{2,1,0:T(8,128)(2,1)} %param.8, bf16[128,2048]{1,0:T(8,128)(2,1)} %get-tuple-element.75, bf16[128,2048]{1,0:T(8,128)(2,1)} %collective-permute-done.2, pred[]{:T(512)S(6)} %eq.6, ...), kind=kOutput, calls=%fused_computation.39 | convolution fusion | flops 1083174784 | bytes 12878849 | tf_op jit(solution)/shard_map/dot_general | solution.py:500
  334.4 6.8 %copy.39 = bf16[2,512,8,256]{3,1,0,2:T(8,128)(2,1)} copy(bf16[2,512,8,256]{1,3,0,2:T(8,128)(2,1)} %bitcast.122) | data formatting | bytes 8388608 | tf_op jit(solution)/shard_map/ctf,ckth->fkh/dot_general | solution.py:551
  341.2 3.6 fusion.39.wgrad_u
  344.9 48.4 %reduce_terms.1 = (bf16[128,4096]{1,0:T(8,128)(2,1)S(1)}, bf16[128,4096]{1,0:T(8,128)(2,1)S(1)}, bf16[16,128,1024]{2,1,0:T(8,128)(2,1)S(1)}, bf16[256,1024]{1,0:T(8,128)(2,1)S(1)}) custom-call(bf16[2048,256]{1,0:T(8,128)(2,1)S(1)} %get-tuple-element.48.terms_0, bf16[2048,256]{1,0:T(8,128)(2,1)S(1)} %get-tuple-element.52.terms_1, ...), custom_call_target="tpu_custom_call" | custom-call | tf_op jit(solution)/shard_map/reduce_terms/pallas_call | solution.py:424
  393.4 1.0 copy-done.12
  394.3 1.9 copy-done.8
  396.3 1.3 convolution_add_fusion
  397.5 0.9 reshape.184
  398.4 1.2 copy.46
  399.7 2.8 broadcast_in_dim_reshape.3
  402.4 1.0 constant_dynamic-slice_fusion.1
  403.4 0.8 copy.41
  404.2 1.0 copy.42
  405.2 7.9 %fusion.29 = (f32[4096]{0:T(1024)S(1)}, f32[128]{0:T(128)S(1)}, f32[128,4096]{1,0:T(8,128)}) fusion(f32[128]{0:T(128)S(1)} %add_rsqrt_fusion.1, bf16[1,128,4096]{2,1,0:T(8,128)(2,1)S(1)} %copy-done.15, f32[4096]{0:T(1024)S(1)} %bitcast.147, bf16[128,1024]{0,1:T(8,128)(2,1)S(1)} %bitcast.140, bf16[2,1,4096,1024]{3,2,1,0:T(8,128)(2,1)} %param.11, ...), kind=kOutput, calls=%fused_computation.31 | convolution fusion | flops 1078456192 | bytes 12878848 | tf_op jit(solution)/shard_map/dot_general | solution.py:500
  413.2 0.7 maximum_bitcast_fusion.1.g_ref
  413.9 33.4 %sum_gains.1 = (f32[8,256]{1,0:T(8,128)}, f32[8,256]{1,0:T(8,128)}) custom-call(f32[16,8,256]{2,1,0:T(8,128)} %maximum_bitcast_fusion.1.g_ref), custom_call_target="tpu_custom_call" | custom-call | tf_op jit(solution)/shard_map/sum_gains/pallas_call | solution.py:469
  447.4 3.7 fusion.51
  451.0 1.3 slice_add_fusion
  452.3 3.2 fusion.50
  455.5 1.0 copy.57
  (62 shorter events, 0.3 us)
Async XLA Ops:
  7.2 3.2 copy-start.14
  7.2 3.2 copy-start.24
  7.2 181.1 %all-gather.4.cloned.1.call-start = ((), (), s32[]{:S(2)}) async-start(), calls=%async_computation.2 | async-start | bytes 2359296 | tf_op jit(solution)/shard_map/all_gather | solution.py:536
  10.4 4.8 %copy-start.16 = (bf16[1,128,4096]{2,1,0:T(8,128)(2,1)S(1)}, bf16[1,128,4096]{2,1,0:T(8,128)(2,1)}, u32[]{:S(2)}) copy-start(bf16[1,128,4096]{2,1,0:T(8,128)(2,1)} %param.8) | copy-start | bytes 3145732
  24.4 109.8 %copy-start.25 = (s32[16]{0:T(128)S(1)}, s32[16]{0:T(128)}, u32[]{:S(2)}) copy-start(s32[16]{0:T(128)} %param.13) | copy-start | bytes 196
  135.5 1.2 copy-start.11
  183.8 31.4 %all-to-all-start = ((bf16[8,256,512]{2,1,0:T(8,128)(2,1)}), bf16[8,256,512]{2,1,0:T(8,128)(2,1)}, u32[]{:S(2)}, u32[]{:S(2)}) async-start(bf16[8,256,512]{2,1,0:T(8,128)(2,1)} %bitcast.129), calls=%async_computation | async-start | bytes 4194304 | tf_op jit(solution)/shard_map/all_to_all | solution.py:541
  188.2 136.1 %all-gather.6.cloned.1.call-start = ((), (), s32[]{:S(2)}) async-start(), calls=%async_computation.3 | async-start | bytes 4456448 | tf_op jit(solution)/shard_map/all_gather | solution.py:547
  188.3 1.2 copy-start.9
  213.6 0.8 copy-start
  214.4 0.8 copy-start.2
  217.9 1.9 copy-start.18
  222.0 73.2 %all-to-all-start.1 = ((bf16[16,2,128,256]{3,2,1,0:T(8,128)(2,1)}), bf16[16,2,128,256]{3,2,1,0:T(8,128)(2,1)}, u32[]{:S(2)}, u32[]{:S(2)}) async-start(bf16[16,2,128,256]{3,2,1,0:T(8,128)(2,1)} %maximum_bitcast_fusion), calls=%async_computation.1 | async-start | bytes 4194304 | tf_op jit(solution)/shard_map/all_to_all | solution.py:539
  229.5 53.2 %collective-permute-start = (bf16[128,2048]{1,0:T(8,128)(2,1)}, bf16[128,2048]{1,0:T(8,128)(2,1)S(1)}, u32[]{:S(2)}, u32[]{:S(2)}) collective-permute-start(bf16[128,2048]{1,0:T(8,128)(2,1)} %get-tuple-element.76), channel_id=1, source_target_pairs={{0,112},{1,113},{2,114},{3,115},{4,116},{5,117},{6,118},{7,119},{8... | collective-permute-start | bytes 1572872 | tf_op jit(solution)/shard_map/ppermute | solution.py:519
  234.7 59.2 %collective-permute-start.1 = (bf16[128,2048]{1,0:T(8,128)(2,1)}, bf16[128,2048]{1,0:T(8,128)(2,1)S(1)}, u32[]{:S(2)}, u32[]{:S(2)}) collective-permute-start(bf16[128,2048]{1,0:T(8,128)(2,1)} %get-tuple-element.77), channel_id=1, source_target_pairs={{0,113},{1,112},{2,115},{3,114},{4,117},{5,116},{6,119},{7,118},{8... | collective-permute-start | bytes 1572872 | tf_op jit(solution)/shard_map/ppermute | solution.py:520
  236.6 88.9 %collective-permute-start.2 = (bf16[128,2048]{1,0:T(8,128)(2,1)}, bf16[128,2048]{1,0:T(8,128)(2,1)}, u32[]{:S(2)}, u32[]{:S(2)}) collective-permute-start(bf16[128,2048]{1,0:T(8,128)(2,1)} %get-tuple-element.74), channel_id=1, source_target_pairs={{0,1},{1,0},{2,3},{3,2},{4,5},{5,4},{6,7},{7,6},{8,9},{9,8},{10,11... | collective-permute-start | bytes 1572872 | tf_op jit(solution)/shard_map/ppermute | solution.py:508
  295.2 3.2 copy-start.10
  322.7 0.8 copy-start.4
  323.5 0.8 copy-start.6
  334.4 6.8 %copy-start.23 = (bf16[16,1,128,256]{3,2,1,0:T(8,128)(2,1)S(1)}, bf16[16,1,128,256]{3,2,1,0:T(8,128)(2,1)}, u32[]{:S(2)}) copy-start(bf16[16,1,128,256]{3,2,1,0:T(8,128)(2,1)} %get-tuple-element.73) | copy-start | bytes 3145732
  341.2 3.7 copy-start.1
  341.2 3.7 copy-start.3
  341.2 3.7 copy-start.5
  341.2 3.7 copy-start.7
  344.9 51.4 %copy-start.22 = (bf16[16,1,128,256]{3,2,1,0:T(8,128)(2,1)S(1)}, bf16[16,1,128,256]{3,2,1,0:T(8,128)(2,1)}, u32[]{:S(2)}) copy-start(bf16[16,1,128,256]{3,2,1,0:T(8,128)(2,1)} %get-tuple-element.72) | copy-start | bytes 3145732
  393.3 1.0 copy-start.12
  394.3 1.9 copy-start.8
  399.7 5.6 %copy-start.13 = (bf16[128,4096]{1,0:T(8,128)(2,1)S(1)}, bf16[128,4096]{1,0:T(8,128)(2,1)}, u32[]{:S(2)}) copy-start(bf16[128,4096]{1,0:T(8,128)(2,1)} %copy-done.12) | copy-start | bytes 3145732
  399.7 5.6 %copy-start.15 = (bf16[1,128,4096]{2,1,0:T(8,128)(2,1)S(1)}, bf16[1,128,4096]{2,1,0:T(8,128)(2,1)}, u32[]{:S(2)}) copy-start(bf16[1,128,4096]{2,1,0:T(8,128)(2,1)} %param.7) | copy-start | bytes 3145732
  447.3 5.0 %copy-start.17 = (bf16[1,128,4096]{2,1,0:T(8,128)(2,1)S(1)}, bf16[1,128,4096]{2,1,0:T(8,128)(2,1)}, u32[]{:S(2)}) copy-start(bf16[1,128,4096]{2,1,0:T(8,128)(2,1)} %param.8) | copy-start | bytes 3145732
  447.3 5.0 %copy-start.19 = (bf16[1,128,4096]{2,1,0:T(8,128)(2,1)S(1)}, bf16[1,128,4096]{2,1,0:T(8,128)(2,1)}, u32[]{:S(2)}) copy-start(bf16[1,128,4096]{2,1,0:T(8,128)(2,1)} %param.10) | copy-start | bytes 3145732
  447.4 5.0 %copy-start.20 = (f32[128,4096]{1,0:T(8,128)S(1)}, f32[128,4096]{1,0:T(8,128)}, u32[]{:S(2)}) copy-start(f32[128,4096]{1,0:T(8,128)} %get-tuple-element.81) | copy-start | bytes 6291460
  447.4 5.0 %copy-start.21 = (bf16[128,2048]{1,0:T(8,128)(2,1)S(1)}, bf16[128,2048]{1,0:T(8,128)(2,1)}, u32[]{:S(2)}) copy-start(bf16[128,2048]{1,0:T(8,128)(2,1)} %get-tuple-element.75) | copy-start | bytes 1572868
Sparse Core Ops, SparseCore 0:
  134.2 52.1 all-gather.3
  218.0 68.3 all-gather.5

commit v3 on v2

--- a/solution.py
+++ b/solution.py
@@ -22,9 +22,8 @@
     return jnp.concatenate([rows[j * 128:(j + 1) * 128] for j in range(8)], 1)
 
 
-def attention_kernel(first, kf, kb, tq_ref, inv_ref, q_ref, dy_ref, x_ref, kv_hbm, y_ref, dq_ref, terms_ref,
-                     kv_s, dk_s, dv_s, sems):
-    nq = q_ref.shape[0]
+def attention_kernel(kf, kb, tq_ref, inv_ref, q_own, q_got, dy_own, dy_got, x_own, x_got, kv_hbm,
+                     y_own, y_got, dq_own, dq_got, terms_ref, kv_s, dk_s, dv_s, sems):
     head = pl.program_id(0)
     spans = kv_hbm.shape[0]
     scale = 128 ** -0.5
@@ -32,7 +31,7 @@
 
     @pl.when(head == 0)
     def _():
-        copies = [pltpu.make_async_copy(kv_hbm.at[inv_ref[t], :, pl.ds(first * 256, kv_s.shape[1])], kv_s.at[pl.ds(t * 128, 128)], sems.at[t])
+        copies = [pltpu.make_async_copy(kv_hbm.at[inv_ref[t]], kv_s.at[pl.ds(t * 128, 128)], sems.at[t])
                   for t in range(spans)]
         for cp in copies:
             cp.start()
@@ -44,10 +43,10 @@
     kcol = pl.multiple_of(head * 256, 256)
     vcol = pl.multiple_of(head * 256 + 128, 128)
 
-    def span(qi, _):
+    def span(qi, q_ref, dy_ref, x_ref, y_ref, dq_ref):
         t = tq_ref[qi]
-        q = stack_heads(q_ref[qi])
-        dy = stack_heads(dy_ref[qi])
+        q = stack_heads(q_ref[...])
+        dy = stack_heads(dy_ref[...])
         rows = q.shape[0]
 
         def fwd(b, carry, masked):
@@ -72,7 +71,7 @@
         carry = lax.fori_loop(0, nf, lambda b, cr: fwd(b, cr, False), carry)
         m, l, acc = fwd(nf, carry, True)
         mixed = acc / l
-        y_ref[qi] = (x_ref[qi].astype(F32) + spread_heads(mixed)).astype(y_ref.dtype)
+        y_ref[...] = (x_ref[...].astype(F32) + spread_heads(mixed)).astype(y_ref.dtype)
         lse = m + jnp.log2(l)
         delta = jnp.sum(dy.astype(F32) * mixed, 1, keepdims=True)
         lse_r = jnp.transpose(jnp.broadcast_to(lse, (rows, 128)))[0:1]
@@ -99,43 +98,45 @@
         dq = jnp.zeros((rows, 128), F32)
         dq = lax.fori_loop(0, nb, lambda b, cr: bwd(b, cr, False), dq)
         dq = bwd(nb, dq, True)
-        dq_ref[qi] = spread_heads(dq * scale).astype(dq_ref.dtype)
-        return 0
-
-    lax.fori_loop(0, nq, span, 0)
+        dq_ref[...] = spread_heads(dq * scale).astype(dq_ref.dtype)
+
+    span(0, q_own, dy_own, x_own, y_own, dq_own)
+    span(1, q_got, dy_got, x_got, y_got, dq_got)
     for t in range(spans):
         at = pl.ds(pl.multiple_of(inv_ref[t] * 128, 128), 128)
         terms_ref[at, 0:128] = (dk_s[t * 128:(t + 1) * 128] * scale).astype(BF)
         terms_ref[at, 128:256] = dv_s[t * 128:(t + 1) * 128].astype(BF)
 
 
-def attention(q, dy, x, kv, tq, inv, first, count, kf=1024, kb=512):
-    nq, tok, _ = q.shape
+def attention(q, dy, x, kv, tq, inv, kf=1024, kb=512):
     spans = kv.shape[0]
-    smem = pl.BlockSpec(memory_space=pltpu.SMEM)
-    qspec = pl.BlockSpec((nq, tok, 1024), lambda h: (0, 0, first + h))
-    ospec = pl.BlockSpec((nq, tok, 1024), lambda h: (0, 0, h))
-    flops = 2 * 7 * nq * count * 1024 * spans * 128 * 128
-    rows = jax.ShapeDtypeStruct((nq, tok, count * 1024), BF)
+    count = kv.shape[2] // 256
+    own = pl.BlockSpec((128, 1024), lambda h, tq, inv: (0, tq[2] * count + h))
+    got = pl.BlockSpec((128, 1024), lambda h, tq, inv: (0, h))
+    flops = 2 * 7 * 2 * count * 1024 * spans * 128 * 128
+    rows = jax.ShapeDtypeStruct((128, count * 1024), BF)
     return pl.pallas_call(
-        functools.partial(attention_kernel, first, kf, kb),
-        grid=(count,),
-        in_specs=[smem, smem, qspec, qspec, qspec, pl.BlockSpec(memory_space=pl.ANY)],
-        out_specs=[ospec, ospec, pl.BlockSpec((spans * 128, 256), lambda h: (0, h))],
-        out_shape=[rows, rows, jax.ShapeDtypeStruct((spans * 128, count * 256), BF)],
-        scratch_shapes=[pltpu.VMEM((spans * 128, count * 256), BF), pltpu.VMEM((spans * 128, 128), F32),
-                        pltpu.VMEM((spans * 128, 128), F32), pltpu.SemaphoreType.DMA((spans,))],
+        functools.partial(attention_kernel, kf, kb),
+        grid_spec=pltpu.PrefetchScalarGridSpec(
+            num_scalar_prefetch=2,
+            grid=(count,),
+            in_specs=[own, got] * 3 + [pl.BlockSpec(memory_space=pl.ANY)],
+            out_specs=[got] * 4 + [pl.BlockSpec((spans * 128, 256), lambda h, tq, inv: (0, h))],
+            scratch_shapes=[pltpu.VMEM((spans * 128, count * 256), BF), pltpu.VMEM((spans * 128, 128), F32),
+                            pltpu.VMEM((spans * 128, 128), F32), pltpu.SemaphoreType.DMA((spans,))],
+        ),
+        out_shape=[rows] * 4 + [jax.ShapeDtypeStruct((spans * 128, count * 256), BF)],
         compiler_params=pltpu.CompilerParams(vmem_limit_bytes=50 << 20),
         cost_estimate=pl.CostEstimate(flops=flops, bytes_accessed=16 << 20, transcendentals=0),
         name="attention",
-    )(tq, inv, q, dy, x, kv)
+    )(tq, inv, *q, *dy, *x, kv)
 
 
 MESH_ID = pl.DeviceIdType.MESH
 EPS = 1e-05
 DOWN, UP = 0, 1
 OWN, PAIR = 0, 1
-UNITS = [(0, OWN), (0, PAIR), (1, OWN), (1, PAIR)]
+UNITS = [(UP, OWN), (UP, PAIR), (DOWN, OWN), (DOWN, PAIR)]
 
 
 class Place:
@@ -239,57 +240,50 @@
 
 
 def spread_kernel(act_d, act_u, cot_d, cot_u, x_d, x_u, kv_d, kv_u,
-                  q_d, q_u, dy_d, dy_u, xh_d, xh_u, pair_d, all_u, send_sem, recv_sem, local_sem):
+                  q_d, q_u, dy_d, dy_u, xh_d, xh_u, all_d, all_u, send_sem, recv_sem, local_sem):
     place = Place()
     wires = Wires(send_sem, recv_sem)
     place.greet(pltpu.get_barrier_semaphore())
-    mine = lambda width: pl.ds(pl.multiple_of(place.core * width, width), width)
+    all_kv, kv = (all_d, all_u), (kv_d, kv_u)
+    mine = pl.ds(pl.multiple_of(place.core * 512, 512), 512)
     other = lambda width: pl.ds(pl.multiple_of((1 - place.core) * width, width), width)
-    slot = lambda unit, chip: all_u.at[place.span(chip, unit[1]), :, pl.ds(unit[0] * 256, 256)]
-    part = lambda head: pl.ds(pl.multiple_of(place.core * 512 + head * 256, 256), 256)
+    slot = lambda unit, chip: all_kv[unit[0]].at[place.span(chip, unit[1])]
     local = []
-
-    def keep(src, dst):
-        copy = pltpu.make_async_copy(src, dst, local_sem.at[len(local)])
+    for layer in (UP, DOWN):
+        wires.send(28 + layer, kv[layer].at[:, other(512)], all_kv[layer].at[place.me], place.partner)
+    for layer in (UP, DOWN):
+        gather_first(place, wires, 0, (layer, OWN), kv[layer].at[:, mine], slot)
+        copy = pltpu.make_async_copy(kv[layer].at[:, mine], all_kv[layer].at[place.me], local_sem.at[layer])
         copy.start()
         local.append(copy)
-
-    wires.send(28, kv_u.at[:, other(512)], all_u.at[place.me], place.partner)
-    for head in range(2):
-        gather_first(place, wires, 0, (head, OWN), kv_u.at[:, part(head)], slot)
-    keep(kv_u.at[:, mine(512)], all_u.at[place.me])
-    wires.arrive(28, all_u.at[place.partner], place.partner)
-    for head in range(2):
-        gather_first(place, wires, 0, (head, PAIR), slot((head, PAIR), place.chip), slot)
-    wires.send(29, kv_d.at[:, other(512)], pair_d.at[place.core], place.partner)
-    keep(kv_d.at[:, mine(512)], pair_d.at[place.core])
+    for layer in (UP, DOWN):
+        wires.arrive(28 + layer, all_kv[layer].at[place.partner], place.partner)
+        gather_first(place, wires, 0, (layer, PAIR), slot((layer, PAIR), place.chip), slot)
     halves = ((act_u, q_u), (cot_u, dy_u), (x_u, xh_u), (act_d, q_d), (cot_d, dy_d), (x_d, xh_d))
     for n, (src, dst) in enumerate(halves):
-        wires.send(30 + n, src.at[:, other(2048)], dst.at[place.core], place.partner)
-        keep(src.at[:, mine(2048)], dst.at[place.core])
+        wires.send(30 + n, src.at[:, other(2048)], dst, place.partner)
     for unit in UNITS:
         gather_second(place, wires, 0, unit, slot, nothing)
     for unit in UNITS:
         gather_third(place, wires, 0, unit, slot, nothing)
     for unit in UNITS:
         gather_last(place, wires, 0, unit, slot, nothing)
-    wires.arrive(29, pair_d.at[1 - place.core], place.partner)
     for n, (src, dst) in enumerate(halves):
-        wires.arrive(30 + n, dst.at[1 - place.core], place.partner)
+        wires.arrive(30 + n, dst, place.partner)
     for copy in local:
         copy.wait()
     wires.finish()
 
 
 def spread(*operands):
-    half = jax.ShapeDtypeStruct((2, 128, 2048), BF)
+    half = jax.ShapeDtypeStruct((128, 2048), BF)
     hbm = pl.BlockSpec(memory_space=pl.ANY)
     return pl.pallas_call(
         spread_kernel,
-        in_specs=[hbm] * 8,
+        in_specs=[hbm] * 6 + [pl.BlockSpec(memory_space=pltpu.VMEM)] * 2,
         out_specs=[hbm] * 8,
-        out_shape=[half] * 6 + [jax.ShapeDtypeStruct((2, 128, 512), BF), jax.ShapeDtypeStruct((16, 128, 512), BF)],
-        scratch_shapes=[pltpu.SemaphoreType.DMA((36,)), pltpu.SemaphoreType.DMA((36,)), pltpu.SemaphoreType.DMA((8,))],
+        out_shape=[half] * 6 + [jax.ShapeDtypeStruct((16, 128, 512), BF)] * 2,
+        scratch_shapes=[pltpu.SemaphoreType.DMA((36,)), pltpu.SemaphoreType.DMA((36,)), pltpu.SemaphoreType.DMA((2,))],
         compiler_params=pltpu.CompilerParams(collective_id=1, has_side_effects=True),
         name="spread",
     )(*operands)
@@ -298,22 +292,22 @@
 R0, RA, RB, R1, RU, RD, RX = range(7)
 
 
-def reduce_kernel(terms_0, terms_1, y_0, y_1, dq_0, dq_1, wgrad_u, down_out, dquery, all_kv, mirror_w,
+def reduce_kernel(terms_d, terms_u, yo_d, yg_d, yo_u, yg_u, dqg_d, dqg_u, down_out, up_out, dq_d, dq_u, all_d, all_u,
                   slots, stage, total, send_sem, recv_sem, local_sem):
     place = Place()
     wires = Wires(send_sem, recv_sem)
     section = lax.axis_index("section")
-    after, before, mirrored = (section + 1) % 8, (section + 7) % 8, 7 - section
+    after, before = (section + 1) % 8, (section + 7) % 8
     barrier = pltpu.get_barrier_semaphore()
     for there in (after, before):
         for dev in (place.me, place.partner):
             pl.semaphore_signal(barrier, inc=1, device_id={"section": there, "ctx": dev}, device_id_type=MESH_ID)
-    pl.semaphore_signal(barrier, inc=1, device_id={"section": mirrored}, device_id_type=MESH_ID)
     for dev in (place.partner, place.across, place.above, place.below):
         pl.semaphore_signal(barrier, inc=1, device_id={"ctx": dev}, device_id_type=MESH_ID)
-    pl.semaphore_wait(barrier, 9)
-    terms = (terms_0, terms_1)
-    part = lambda core, head, width: pl.ds(pl.multiple_of(core * 2 * width + head * width, width), width)
+    pl.semaphore_wait(barrier, 8)
+    terms, all_kv = (terms_d, terms_u), (all_d, all_u)
+    mine = pl.ds(pl.multiple_of(place.core * 512, 512), 512)
+    wide = pl.ds(pl.multiple_of(place.core * 2048, 2048), 2048)
     chip, chip_x = place.chip, place.chip_x
     local = []
 
@@ -345,15 +339,11 @@
         copy.start()
         far.append(copy)
 
-    for head, (y, dq) in enumerate(((y_0, dq_0), (y_1, dq_1))):
-        here = part(place.core, head, 1024)
-        far_send(dq.at[1 - place.core], dquery.at[:, here], {"ctx": place.partner})
-        far_send(y.at[place.core], down_out.at[:, here], {"section": after})
-        far_send(y.at[1 - place.core], down_out.at[:, here], {"section": after, "ctx": place.partner})
-        copy = pltpu.make_async_copy(dq.at[place.core], dquery.at[:, here], local_sem.at[len(local)])
-        copy.start()
-        local.append(copy)
-    far_send(wgrad_u, mirror_w, {"section": mirrored})
+    far_send(dqg_u, dq_u, {"ctx": place.partner})
+    far_send(dqg_d, dq_d, {"ctx": place.partner})
+    for there, mine_y, other_y, out in ((before, yo_u, yg_u, up_out), (after, yo_d, yg_d, down_out)):
+        far_send(mine_y, out.at[:, wide], {"section": there})
+        far_send(other_y, out.at[:, wide], {"section": there, "ctx": place.partner})
     for n, unit in enumerate(UNITS):
         at = 7 * n
         wires.arrive(at + R0, slots.at[at + R0], place.across)
@@ -374,7 +364,7 @@
             stage[3 * n + 2] = plus(slots.at[at + R1], term(unit, place.up(chip, 1)))
             wires.send(at + RD, stage.at[3 * n + 2], slots.at[at + RD], place.above)
 
-    slot = lambda unit, at: all_kv.at[place.span(at, unit[1]), :, part(place.core, unit[0], 256)]
+    slot = lambda unit, at: all_kv[unit[0]].at[place.span(at, unit[1]), :, mine]
     passed = [0]
 
     def hand_over(unit, at):
@@ -407,11 +397,21 @@
         gather_third(place, wires, 28, unit, slot, landed)
     for unit in UNITS:
         gather_last(place, wires, 28, unit, slot, landed)
+    theirs = pl.ds(pl.multiple_of((1 - place.core) * 512, 512), 512)
     for n, (unit, at) in enumerate(order):
-        ref = all_kv.at[place.span(at, 1 - unit[1]), :, part(1 - place.core, unit[0], 256)]
-        wires.arrive(56 + n, ref, place.partner)
+        span = place.span(at, 1 - unit[1])
+        wires.arrive(56 + n, all_kv[unit[0]].at[span, :, theirs], place.partner)
     for copy in far:
-        copy.wait()
+        copy.wait_send()
+    wires.arrive(index, dq_u, place.partner)
+    wires.arrive(index + 1, dq_d, place.partner)
+    for n, (out, there) in enumerate(((up_out, after), (down_out, before))):
+        for flip, dev in ((0, place.me), (1, place.partner)):
+            half = pl.ds(pl.multiple_of((place.core + flip * (1 - 2 * place.core)) * 2048, 2048), 2048)
+            pltpu.make_async_remote_copy(
+                src_ref=out.at[:, half], dst_ref=out.at[:, half], send_sem=send_sem.at[index + 2 + 2 * n + flip],
+                recv_sem=recv_sem.at[index + 2 + 2 * n + flip], device_id={"section": there, "ctx": dev},
+                device_id_type=MESH_ID).wait_recv()
     for copy in local:
         copy.wait()
     wires.finish()
@@ -421,13 +421,15 @@
     hbm = pl.BlockSpec(memory_space=pl.ANY)
     vmem = pl.BlockSpec(memory_space=pltpu.VMEM)
     row = jax.ShapeDtypeStruct((128, 4096), BF)
+    half = jax.ShapeDtypeStruct((128, 2048), BF)
+    whole = jax.ShapeDtypeStruct((16, 128, 1024), BF)
     return pl.pallas_call(
         reduce_kernel,
-        in_specs=[vmem] * 2 + [hbm] * 5,
-        out_specs=[hbm] * 4,
-        out_shape=[row] * 2 + [jax.ShapeDtypeStruct((16, 128, 1024), BF), jax.ShapeDtypeStruct((256, 1024), BF)],
-        scratch_shapes=[pltpu.VMEM((28, 128, 256), BF), pltpu.VMEM((12, 128, 256), BF), pltpu.VMEM((4, 128, 256), BF),
-                        pltpu.SemaphoreType.DMA((95,)), pltpu.SemaphoreType.DMA((95,)), pltpu.SemaphoreType.DMA((6,))],
+        in_specs=[vmem] * 2 + [hbm] * 6,
+        out_specs=[hbm] * 6,
+        out_shape=[row] * 2 + [half] * 2 + [whole] * 2,
+        scratch_shapes=[pltpu.VMEM((28, 128, 512), BF), pltpu.VMEM((12, 128, 512), BF), pltpu.VMEM((4, 128, 512), BF),
+                        pltpu.SemaphoreType.DMA((94,)), pltpu.SemaphoreType.DMA((94,)), pltpu.SemaphoreType.DMA((4,))],
         compiler_params=pltpu.CompilerParams(collective_id=2, has_side_effects=True, vmem_limit_bytes=32 << 20),
         name="reduce_terms",
     )(*operands)
@@ -504,21 +506,8 @@
     return dx.astype(BF), gpart
 
 
-def exchanged(array):
-    return lax.ppermute(array, "ctx", [(i, i ^ 1) for i in range(lax.axis_size("ctx"))])
-
-
 def halves_joined(core, mine, other):
     return jnp.where(core == 0, jnp.concatenate([mine, other], 1), jnp.concatenate([other, mine], 1))
-
-
-def relayed(halves, core, by):
-    sections, spans = lax.axis_size("section"), lax.axis_size("ctx")
-    to = lambda flip: [(s * spans + i, (s + by) % sections * spans + (i ^ flip)) for s in range(sections) for i in range(spans)]
-    pick = lambda which: lax.dynamic_index_in_dim(halves, which, 0, False)
-    mine = lax.ppermute(pick(core), ("section", "ctx"), to(0))
-    other = lax.ppermute(pick(1 - core), ("section", "ctx"), to(1))
-    return halves_joined(core, mine, other)
 
 
 def per_device(down_in, up_in, down_cot, up_cot, kv_weight, norm_gain, span_ids):
@@ -527,40 +516,27 @@
     x_d, x_u, cot_d, cot_u = down_in[0], up_in[0], down_cot[0], up_cot[0]
     gain_d, gain_u = norm_gain[0, 0], norm_gain[1, 0]
     weight_d, weight_u = kv_weight[0, 0], kv_weight[1, 0]
-    same_core = [[i for i in range(16) if i % 2 == c] for c in range(2)]
-    times = lax.dynamic_slice_in_dim(span_ids, own // 2 * 2, 2, 0)
+    scalars = jnp.stack([span_ids[own], span_ids[own + 1 - 2 * core], core]).astype(jnp.int32)
     inverse = jnp.argsort(span_ids).astype(jnp.int32)
     recip_u, act_u, kv_u = prepare(x_u, gain_u, weight_u)
     recip_d, act_d, kv_d = prepare(x_d, gain_d, weight_d)
-    q_d, q_u, dy_d, dy_u, xh_d, xh_u, pair_d, all_u = spread(act_d, act_u, cot_d, cot_u, x_d, x_u, kv_d, kv_u)
-    all_d = lax.all_gather(pair_d.reshape(256, 512), "ctx", axis=0, axis_index_groups=same_core).reshape(16, 128, 512)
-    act_d, act_u, _ = lax.optimization_barrier((act_d, act_u, pair_d))
+    q_d, q_u, dy_d, dy_u, xh_d, xh_u, all_d, all_u = spread(act_d, act_u, cot_d, cot_u, x_d, x_u, kv_d, kv_u)
     features = jnp.stack([act_d, act_u]).reshape(2, 128, 16, 256).transpose(2, 0, 1, 3)
     features = lax.all_to_all(features, "ctx", 0, 0, tiled=False)
-    yh_u, dq_u, terms_u = attention(q_u, dy_u, xh_u, all_u, times, inverse, 0, 2)
-    got_u = lax.all_to_all(terms_u.reshape(8, 256, 512), "ctx", 0, 0, axis_index_groups=same_core, tiled=False)
-    up_out = relayed(yh_u, core, -1)
-    dq_there = exchanged(lax.dynamic_index_in_dim(dq_u, 1 - core, 0, False))
-    yh_d0, dq_d0, terms_d0 = attention(q_d, dy_d, xh_d, all_d, times, inverse, 0, 1)
-    got_u, all_d, terms_d0 = lax.optimization_barrier((got_u, all_d, terms_d0))
-    pair_u = jnp.sum(got_u.astype(F32), 0).astype(BF)
-    dkv_u = lax.all_gather(pair_u, "ctx", axis=0)
-    yh_d1, dq_d1, terms_d1 = attention(q_d, dy_d, xh_d, all_d, times, inverse, 1, 1)
-    dkv_u, terms_d1 = lax.optimization_barrier((dkv_u, terms_d1))
-    dkv_u = dkv_u.reshape(8, 2, 256, 512)
-    wgrad_u = jnp.einsum("ctf,ckth->fkh", features[:, 1].reshape(8, 256, 256), dkv_u, preferred_element_type=F32)
-    wgrad_u = wgrad_u.reshape(256, 1024).astype(BF)
-    down_out, dquery_d, dkv_d, mirror_w = reduce_terms(terms_d0, terms_d1, yh_d0, yh_d1, dq_d0, dq_d1, wgrad_u)
-    dquery_u = halves_joined(core, lax.dynamic_index_in_dim(dq_u, core, 0, False), dq_there)
-    own_u = lax.dynamic_index_in_dim(dkv_u, own // 2, 0, False)
-    own_u = lax.dynamic_slice_in_dim(own_u, core * 128, 128, 1).transpose(1, 0, 2).reshape(128, 1024)
-    own_d = lax.dynamic_index_in_dim(dkv_d, own, 0, False)
-    grad_u, gpart_u = complete(x_u, recip_u, cot_u, gain_u, weight_u, dquery_u, own_u)
-    grad_d, gpart_d = complete(x_d, recip_d, cot_d, gain_d, weight_d, dquery_d, own_d)
+    yo_u, yg_u, dqo_u, dqg_u, terms_u = attention((act_u, q_u), (cot_u, dy_u), (x_u, xh_u), all_u, scalars, inverse)
+    yo_d, yg_d, dqo_d, dqg_d, terms_d = attention((act_d, q_d), (cot_d, dy_d), (x_d, xh_d), all_d, scalars, inverse)
+    down_out, up_out, dq_d, dq_u, dkv_d, dkv_u = reduce_terms(
+        terms_d, terms_u, yo_d, yg_d, yo_u, yg_u, dqg_d, dqg_u)
+    wgrad = lambda which, dkv: lax.dot_general(
+        features[:, which].reshape(2048, 256), dkv.reshape(2048, 1024), TN, preferred_element_type=F32)
+    sections = lax.axis_size("section")
+    mirror_w = lax.ppermute(wgrad(1, dkv_u).astype(BF), "section", [(i, sections - 1 - i) for i in range(sections)])
+    own_dkv = lambda dkv: lax.dynamic_index_in_dim(dkv, own, 0, False)
+    grad_u, gpart_u = complete(x_u, recip_u, cot_u, gain_u, weight_u, halves_joined(core, dqo_u, dq_u), own_dkv(dkv_u))
+    grad_d, gpart_d = complete(x_d, recip_d, cot_d, gain_d, weight_d, halves_joined(core, dqo_d, dq_d), own_dkv(dkv_d))
     gains = jnp.stack([gpart_d, gpart_u] + [jnp.zeros_like(gpart_d)] * 6).reshape(8, 16, 256).transpose(1, 0, 2)
     gain_here, gain_there = sum_gains(gains)
-    wgrad_d = lax.dot_general(features[:, 0].reshape(2048, 256), dkv_d.reshape(2048, 1024), TN, preferred_element_type=F32)
-    kv_grad = by_kind(wgrad_d + mirror_w.astype(F32))[None]
+    kv_grad = by_kind(wgrad(0, dkv_d) + mirror_w.astype(F32))[None]
     gain_grad = (gain_here[0] + gain_there[1])[None]
     return (down_out[None], up_out[None], grad_d[None], grad_u[None], kv_grad, gain_grad)
 

time: 469 us -> 355 us (0.76)
  the two profiles are of different devices: /device:TPU:1 before, /device:TPU:2 now
where the time goes in v3:
time: 355 us; the launch traced here: 348 us
  Pallas kernels  254 us (72%)
  matrix products  36.1 us (10%)
  local copies, waits for them, and re-layouts  34.3 us (10%)
  other arithmetic  14.1 us (4%)
  starting transfers between devices  8.07 us (2%)
    pallas_call x1, Pallas kernels, reduce_terms(): pl.pallas_call(reduce_kernel, in_specs=[vmem] * 2 + [hbm] * 6, out_specs=...  105 us
    pallas_call x2, Pallas kernels, attention(): pl.pallas_call(functools.partial(attention_kernel, kf, kb), grid_spec=plt...  84.5 us
    pallas_call x1, Pallas kernels, spread(): pl.pallas_call(spread_kernel, in_specs=[hbm] * 6 + [pl.BlockSpec(memory_s...  41.6 us
    pallas_call x1, Pallas kernels, sum_gains(): pl.pallas_call(gains_kernel, in_specs=[vmem], out_specs=[vmem, vmem], out...  22.8 us
    unnamed x60, local copies, waits for them, and re-layouts  16.4 us
    dot_general x2, matrix products, complete(): lax.dot_general(by_kind(dkv), weight, NT, preferred_element_type=F32)  15.6 us
    dot_general x2, matrix products, prepare(): kv = jnp.dot(act, weight, preferred_element_type=F32).astype(BF)  10.9 us
    dot_general x2, matrix products, per_device(): lax.dot_general(features[:, which].reshape(2048, 256), dkv.reshape(2048,...  9.59 us
  transfers between devices with their start and end apart: 2, of which 0 were waited for; matrix products, arithmetic and copies ran while one was open for 13% of the time, Pallas kernels for 73%

profile of v3, /device:TPU:2, one launch (start us, length us, event | category | flops | bytes accessed | tf_op | source)
XLA Modules:
  0.0 348.2 jit_solution(15262234806954640959)
XLA Ops:
  0.6 0.0 copy-start.13
  0.6 1.6 fusion.33
  2.2 1.6 copy.30
  3.9 0.0 copy-start.25
  3.9 0.3 fusion.41
  4.2 0.7 copy.32
  4.9 0.7 multiply_convert_fusion.1
  5.6 0.0 copy-start.18
  5.6 0.7 multiply_convert_fusion
  6.3 0.2 maximum_bitcast_fusion
  6.5 0.0 copy-done.18
  6.6 1.5 copy.38
  8.1 6.9 %all-to-all-start = ((bf16[16,2,128,256]{2,3,1,0:T(8,128)(2,1)}), bf16[16,2,128,256]{2,3,1,0:T(8,128)(2,1)}, u32[]{:S(2)}, u32[]{:S(2)}) async-start(bf16[16,2,128,256]{2,3,1,0:T(8,128)(2,1)} %copy.38), calls=%async_computation | async-start | bytes 4194304 | tf_op jit(solution)/shard_map/all_to_all | solution.py:525
  15.0 5.4 %fusion.42 = bf16[128,1024]{1,0:T(8,128)(2,1)} fusion(bf16[2,1,4096,1024]{3,2,1,0:T(8,128)(2,1)} %param.11, bf16[1,128,4096]{1,2,0:T(8,128)(2,1)S(1)} %copy-done.19), kind=kOutput, calls=%fused_computation.46 | convolution fusion | flops 1073872896 | bytes 9699328 | tf_op jit(solution)/shard_map/dot_general | solution.py:496
  20.4 5.5 %fusion.45 = bf16[128,1024]{1,0:T(8,128)(2,1)} fusion(bf16[2,1,4096,1024]{3,2,1,0:T(8,128)(2,1)} %param.11, bf16[1,128,4096]{1,2,0:T(8,128)(2,1)S(1)} %multiply_convert_fusion), kind=kOutput, calls=%fused_computation.47 | convolution fusion | flops 1073872896 | bytes 9699328 | tf_op jit(solution)/shard_map/dot_general | solution.py:496
  25.9 1.3 fusion.26.act_d.q_own
  27.2 1.3 fusion.34.act_u.q_own
  28.5 0.2 reshape.137
  28.7 0.2 copy.47
  28.9 0.9 reshape.138.kv_d
  29.8 0.2 reshape.139
  30.0 0.2 copy.46
  30.2 0.9 reshape.140.kv_u
  31.1 1.2 sort.17
  32.3 0.6 fusion.54
  32.9 1.3 pad_add_fusion.tq_ref
  34.3 41.6 %spread.1 = (bf16[128,2048]{1,0:T(8,128)(2,1)}, bf16[128,2048]{1,0:T(8,128)(2,1)}, bf16[128,2048]{1,0:T(8,128)(2,1)}, bf16[128,2048]{1,0:T(8,128)(2,1)}, bf16[12...) custom-call(bf16[128,4096]{1,0:T(8,128)(2,1)} %fusion.26.act_d.q_own, ...), custom_call_target="tpu_custom_call" | custom-call | tf_op jit(solution)/shard_map/spread/pallas_call | solution.py:281
  75.9 1.0 copy-done.7
  77.0 1.0 copy-done.8
  78.0 1.0 copy-done.9
  79.1 36.7 %attention.3 = (bf16[128,2048]{1,0:T(8,128)(2,1)S(1)}, bf16[128,2048]{1,0:T(8,128)(2,1)S(1)}, bf16[128,2048]{1,0:T(8,128)(2,1)S(1)}, bf16[128,2048]{1,0:T(8,128)(2,1)S(1)}, bf16[2048,512]{1,0:T(8,128)(2,1)}) custom-call(s32[3]{0:T(128)S(1)} %pad_add_fusion.tq_ref, s32[16]{0:T(128)S(1)} %get-tuple-element.33.inv_ref, bf16[128,4096]{1,0:T(8,128)(2,1)} %fusion.34.act_u.q_own, ...), custom_call_target="tpu_custom_call" | custom-call | flops 15032385536 | bytes 16777216 | tf_op jit(solution)/shard_map/attention/pallas_call | solution.py:118
  115.7 0.0 copy-start.10
  115.7 0.8 copy-done.10
  116.5 47.9 %attention.2 = (bf16[128,2048]{1,0:T(8,128)(2,1)S(1)}, bf16[128,2048]{1,0:T(8,128)(2,1)S(1)}, bf16[128,2048]{1,0:T(8,128)(2,1)S(1)}, bf16[128,2048]{1,0:T(8,128)(2,1)S(1)}, bf16[2048,512]{1,0:T(8,128)(2,1)}) custom-call(s32[3]{0:T(128)S(1)} %pad_add_fusion.tq_ref, s32[16]{0:T(128)S(1)} %get-tuple-element.33.inv_ref, bf16[128,4096]{1,0:T(8,128)(2,1)} %fusion.26.act_d.q_own, ...), custom_call_target="tpu_custom_call" | custom-call | flops 15032385536 | bytes 16777216 | tf_op jit(solution)/shard_map/attention/pallas_call | solution.py:118
  164.4 0.8 copy-done.11
  165.2 1.6 copy-done.1
  166.8 105.3 %reduce_terms.1 = (bf16[128,4096]{1,0:T(8,128)(2,1)S(1)}, bf16[128,4096]{1,0:T(8,128)(2,1)S(1)}, bf16[128,2048]{1,0:T(8,128)(2,1)S(1)}, bf16[128,2048]{1,0:T(8,1...) custom-call(bf16[2048,512]{1,0:T(8,128)(2,1)S(1)} %copy-done.1, ...), custom_call_target="tpu_custom_call" | custom-call | tf_op jit(solution)/shard_map/reduce_terms/pallas_call | solution.py:426
  272.1 1.9 copy-done.2
  274.0 1.4 constant_dynamic-slice_fusion
  275.5 0.1 copy-done.3
  275.6 1.1 copy.36
  276.7 0.7 copy.37
  277.4 1.1 copy.34
  278.5 0.0 copy-start.12
  278.6 7.4 %fusion.40 = (f32[4096]{0:T(1024)S(1)}, f32[128]{0:T(128)S(1)}, f32[128,4096]{1,0:T(8,128)S(1)}) fusion(f32[128]{0:T(128)S(1)} %add_rsqrt_fusion, bf16[1,128,4096]{2,1,0:T(8,128)(2,1)} %param.8, f32[4096]{0:T(1024)S(1)} %bitcast.113, bf16[128,1024]{0,1:T(8,128)(2,1)} %bitcast.116, bf16[2,1,4096,1024]{3,2,1,0:T(8,128)(2,1)} %param.11, ...), kind=kOutput, calls=%fused_computation.40 | convolution fusion | flops 1083174784 | bytes 12878849 | tf_op jit(solution)/shard_map/dot_general | solution.py:502
  286.0 8.2 %fusion.32 = (f32[4096]{0:T(1024)S(1)}, f32[128]{0:T(128)S(1)}, f32[128,4096]{1,0:T(8,128)}) fusion(f32[128]{0:T(128)S(1)} %add_rsqrt_fusion.1, bf16[1,128,4096]{2,1,0:T(8,128)(2,1)S(1)} %copy-done.16, f32[4096]{0:T(1024)S(1)} %bitcast.109, bf16[128,1024]{0,1:T(8,128)(2,1)S(1)} %bitcast.115, bf16[2,1,4096,1024]{3,2,1,0:T(8,128)(2,1)} %param.11, ...), kind=kOutput, calls=%fused_computation.32 | convolution fusion | flops 1083174784 | bytes 12878849 | tf_op jit(solution)/shard_map/dot_general | solution.py:502
  294.2 1.7 fusion.48
  295.9 2.7 fusion.52
  298.6 2.3 copy.43
  300.9 4.7 %convolution_convert_fusion = bf16[256,1024]{1,0:T(8,128)(2,1)} fusion(bf16[2048,256]{1,0:T(8,128)(2,1)} %bitcast.102, bf16[2048,1024]{1,0:T(8,128)(2,1)} %bitcast.89), kind=kOutput, calls=%fused_computation.45 | convolution fusion | flops 1074003968 | bytes 5767168 | tf_op jit(solution)/shard_map/dot_general | solution.py:530
  305.6 1.2 collective-permute-start
  306.8 1.7 fusion.49
  308.5 0.1 pad.2.clone
  308.6 0.1 pad.3.clone
  308.6 0.7 maximum_bitcast_fusion.1.g_ref
  309.4 22.8 %sum_gains.1 = (f32[8,256]{1,0:T(8,128)}, f32[8,256]{1,0:T(8,128)}) custom-call(f32[16,8,256]{2,1,0:T(8,128)} %maximum_bitcast_fusion.1.g_ref), custom_call_target="tpu_custom_call" | custom-call | tf_op jit(solution)/shard_map/sum_gains/pallas_call | solution.py:471
  332.2 1.3 slice_add_fusion
  333.4 1.5 copy.42
  335.0 4.9 %convert_add_fusion = f32[256,1024]{1,0:T(8,128)} fusion(bf16[256,1024]{1,0:T(8,128)(2,1)} %collective-permute-done, bf16[2048,256]{1,0:T(8,128)(2,1)} %bitcast.101, bf16[2048,1024]{1,0:T(8,128)(2,1)} %bitcast.88), kind=kOutput, calls=%fused_computation.54 | convolution fusion | flops 1074266112 | bytes 6815744 | tf_op jit(solution)/shard_map/dot_general | solution.py:530
  339.9 2.1 reshape.147
  342.0 1.2 copy.41
  343.2 2.6 broadcast_in_dim_reshape.3
  345.8 1.0 copy.50
  346.8 1.0 copy.51
  (51 shorter events, 0.1 us)
Async XLA Ops:
  0.6 3.2 copy-start.13
  3.9 1.0 copy-start.25
  5.6 1.0 copy-start.18
  8.0 6.9 %copy-start.19 = (bf16[1,128,4096]{1,2,0:T(8,128)(2,1)S(1)}, bf16[1,128,4096]{1,2,0:T(8,128)(2,1)}, u32[]{:S(2)}) copy-start(bf16[1,128,4096]{1,2,0:T(8,128)(2,1)} %copy-done.18) | copy-start | bytes 3145732
  8.1 287.9 %all-to-all-start = ((bf16[16,2,128,256]{2,3,1,0:T(8,128)(2,1)}), bf16[16,2,128,256]{2,3,1,0:T(8,128)(2,1)}, u32[]{:S(2)}, u32[]{:S(2)}) async-start(bf16[16,2,128,256]{2,3,1,0:T(8,128)(2,1)} %copy.38), calls=%async_computation | async-start | bytes 4194304 | tf_op jit(solution)/shard_map/all_to_all | solution.py:525
  20.4 5.5 %copy-start.15 = (bf16[1,128,4096]{2,1,0:T(8,128)(2,1)S(1)}, bf16[1,128,4096]{2,1,0:T(8,128)(2,1)}, u32[]{:S(2)}) copy-start(bf16[1,128,4096]{2,1,0:T(8,128)(2,1)} %param.7) | copy-start | bytes 3145732
  25.9 2.6 copy-start.24
  27.2 2.6 copy-start.23
  28.5 2.5 copy-start.26
  75.9 1.0 copy-start.7
  77.0 1.0 copy-start.8
  78.0 1.0 copy-start.9
  79.1 37.5 %copy-start.4 = (bf16[128,2048]{1,0:T(8,128)(2,1)S(1)}, bf16[128,2048]{1,0:T(8,128)(2,1)}, u32[]{:S(2)}) copy-start(bf16[128,2048]{1,0:T(8,128)(2,1)} %get-tuple-element.34.q_got) | copy-start | bytes 1572868
  79.1 37.5 %copy-start.5 = (bf16[128,2048]{1,0:T(8,128)(2,1)S(1)}, bf16[128,2048]{1,0:T(8,128)(2,1)}, u32[]{:S(2)}) copy-start(bf16[128,2048]{1,0:T(8,128)(2,1)} %get-tuple-element.35.dy_got) | copy-start | bytes 1572868
  79.1 37.5 %copy-start.6 = (bf16[128,2048]{1,0:T(8,128)(2,1)S(1)}, bf16[128,2048]{1,0:T(8,128)(2,1)}, u32[]{:S(2)}) copy-start(bf16[128,2048]{1,0:T(8,128)(2,1)} %get-tuple-element.36.x_got) | copy-start | bytes 1572868
  115.7 0.8 copy-start.10
  116.5 48.7 %copy-start = (bf16[2048,512]{1,0:T(8,128)(2,1)S(1)}, bf16[2048,512]{1,0:T(8,128)(2,1)}, u32[]{:S(2)}) copy-start(bf16[2048,512]{1,0:T(8,128)(2,1)} %get-tuple-element.43.terms_u) | copy-start | bytes 6291460
  164.4 0.8 copy-start.11
  165.2 1.6 copy-start.1
  272.1 2.0 copy-start.2
  272.1 3.5 copy-start.3
  278.5 7.5 %copy-start.12 = (bf16[128,2048]{1,0:T(8,128)(2,1)S(1)}, bf16[128,2048]{1,0:T(8,128)(2,1)}, u32[]{:S(2)}) copy-start(bf16[128,2048]{1,0:T(8,128)(2,1)} %copy-done.11) | copy-start | bytes 1572868
  278.6 7.5 %copy-start.16 = (bf16[1,128,4096]{2,1,0:T(8,128)(2,1)S(1)}, bf16[1,128,4096]{2,1,0:T(8,128)(2,1)}, u32[]{:S(2)}) copy-start(bf16[1,128,4096]{2,1,0:T(8,128)(2,1)} %param.7) | copy-start | bytes 3145732
  286.0 8.2 %copy-start.14 = (bf16[1,128,4096]{2,1,0:T(8,128)(2,1)S(1)}, bf16[1,128,4096]{2,1,0:T(8,128)(2,1)}, u32[]{:S(2)}) copy-start(bf16[1,128,4096]{2,1,0:T(8,128)(2,1)} %param.8) | copy-start | bytes 3145732
  286.0 8.2 %copy-start.20 = (bf16[1,128,4096]{2,1,0:T(8,128)(2,1)S(1)}, bf16[1,128,4096]{2,1,0:T(8,128)(2,1)}, u32[]{:S(2)}) copy-start(bf16[1,128,4096]{2,1,0:T(8,128)(2,1)} %param.10) | copy-start | bytes 3145732
  300.9 5.9 %copy-start.17 = (bf16[1,128,4096]{2,1,0:T(8,128)(2,1)S(1)}, bf16[1,128,4096]{2,1,0:T(8,128)(2,1)}, u32[]{:S(2)}) copy-start(bf16[1,128,4096]{2,1,0:T(8,128)(2,1)} %param.7) | copy-start | bytes 3145732
  300.9 5.9 %copy-start.21 = (bf16[1,128,4096]{2,1,0:T(8,128)(2,1)S(1)}, bf16[1,128,4096]{2,1,0:T(8,128)(2,1)}, u32[]{:S(2)}) copy-start(bf16[1,128,4096]{2,1,0:T(8,128)(2,1)} %param.9) | copy-start | bytes 3145732
  300.9 5.9 %copy-start.22 = (f32[128,4096]{1,0:T(8,128)S(1)}, f32[128,4096]{1,0:T(8,128)}, u32[]{:S(2)}) copy-start(f32[128,4096]{1,0:T(8,128)} %get-tuple-element.70) | copy-start | bytes 6291460
  305.6 29.3 %collective-permute-start = (bf16[256,1024]{1,0:T(8,128)(2,1)}, bf16[256,1024]{1,0:T(8,128)(2,1)}, u32[]{:S(2)}, u32[]{:S(2)}) collective-permute-start(bf16[256,1024]{1,0:T(8,128)(2,1)} %convolution_convert_fusion), channel_id=1, source_target_pairs={{0,112},{16,96},{32,80},{48,64},{64,48},{80,32},{96,16},{112,0},{1... | collective-permute-start | bytes 1572872 | tf_op jit(solution)/shard_map/ppermute | solution.py:533

commit v4 on v3

--- a/solution.py
+++ b/solution.py
@@ -151,6 +151,13 @@
         self.below = (self.me + 12) % 16
         self.chip_x = self.chip + 1 - 2 * beside
 
+    def greet_all(self, barrier):
+        for step in range(1, 16):
+            pl.semaphore_signal(barrier, inc=1, device_id={"ctx": (self.me + step) % 16}, device_id_type=MESH_ID)
+        mirrored = 7 - lax.axis_index("section")
+        pl.semaphore_signal(barrier, inc=1, device_id={"section": mirrored}, device_id_type=MESH_ID)
+        pl.semaphore_wait(barrier, 16)
+
     def greet(self, barrier):
         for dev in (self.partner, self.across, self.above, self.below):
             pl.semaphore_signal(barrier, inc=1, device_id={"ctx": dev}, device_id_type=MESH_ID)
@@ -176,6 +183,14 @@
         copy = self.copy(index, src, dst, dev)
         copy.start()
         self.started.append(copy)
+
+    def far_send(self, index, src, dst, section):
+        copy = pltpu.make_async_remote_copy(
+            src_ref=src, dst_ref=dst, send_sem=self.send_sem.at[index], recv_sem=self.recv_sem.at[index],
+            device_id={"section": section}, device_id_type=MESH_ID)
+        copy.start()
+        self.started.append(copy)
+        return copy
 
     def arrive(self, index, ref, dev):
         self.copy(index, ref, ref, dev).wait_recv()
@@ -292,24 +307,29 @@
 R0, RA, RB, R1, RU, RD, RX = range(7)
 
 
-def reduce_kernel(terms_d, terms_u, yo_d, yg_d, yo_u, yg_u, dqg_d, dqg_u, down_out, up_out, dq_d, dq_u, all_d, all_u,
-                  slots, stage, total, send_sem, recv_sem, local_sem):
+HANDED, DQ, GAINS, FAR = 56, 88, 90, 120
+
+
+def finish_kernel(terms_d, terms_u, dqo_d, dqo_u, dqg_d, dqg_u, x_d, x_u, cot_d, cot_u, gains, features, w_d, w_u,
+                  grad_d, grad_u, kv_grad, gain_grad,
+                  slots, stage, total, all_kv, dquery, weight, dact, gparts, ggot, gsum, acc, wsend, wgot, ggot_far,
+                  send_sem, recv_sem, local_sem):
     place = Place()
     wires = Wires(send_sem, recv_sem)
-    section = lax.axis_index("section")
-    after, before = (section + 1) % 8, (section + 7) % 8
-    barrier = pltpu.get_barrier_semaphore()
-    for there in (after, before):
-        for dev in (place.me, place.partner):
-            pl.semaphore_signal(barrier, inc=1, device_id={"section": there, "ctx": dev}, device_id_type=MESH_ID)
-    for dev in (place.partner, place.across, place.above, place.below):
-        pl.semaphore_signal(barrier, inc=1, device_id={"ctx": dev}, device_id_type=MESH_ID)
-    pl.semaphore_wait(barrier, 8)
-    terms, all_kv = (terms_d, terms_u), (all_d, all_u)
-    mine = pl.ds(pl.multiple_of(place.core * 512, 512), 512)
+    mirrored = 7 - lax.axis_index("section")
+    terms = (terms_d, terms_u)
+    chip, chip_x = place.chip, place.chip_x
     wide = pl.ds(pl.multiple_of(place.core * 2048, 2048), 2048)
-    chip, chip_x = place.chip, place.chip_x
     local = []
+
+    def keep(src, dst):
+        copy = pltpu.make_async_copy(src, dst, local_sem.at[len(local)])
+        copy.start()
+        local.append(copy)
+        return copy
+
+    loads = {UP: keep(w_u, weight.at[UP]), DOWN: keep(w_d, weight.at[DOWN])}
+    place.greet_all(pltpu.get_barrier_semaphore())
 
     def term(unit, at):
         return terms[unit[0]].at[pl.ds(pl.multiple_of(place.span(at, unit[1]) * 128, 128), 128)]
@@ -329,21 +349,9 @@
             wires.send(at + RD, term(unit, place.up(chip, 1)), slots.at[at + RD], place.above)
         else:
             wires.send(at + RU, term(unit, place.up(chip, 3)), slots.at[at + RU], place.below)
-    index = 56 + 32
-    far = []
-
-    def far_send(src, dst, dev):
-        copy = pltpu.make_async_remote_copy(
-            src_ref=src, dst_ref=dst, send_sem=send_sem.at[index + len(far)], recv_sem=recv_sem.at[index + len(far)],
-            device_id=dev, device_id_type=MESH_ID)
-        copy.start()
-        far.append(copy)
-
-    far_send(dqg_u, dq_u, {"ctx": place.partner})
-    far_send(dqg_d, dq_d, {"ctx": place.partner})
-    for there, mine_y, other_y, out in ((before, yo_u, yg_u, up_out), (after, yo_d, yg_d, down_out)):
-        far_send(mine_y, out.at[:, wide], {"section": there})
-        far_send(other_y, out.at[:, wide], {"section": there, "ctx": place.partner})
+    for layer, own_part, sent in ((UP, dqo_u, dqg_u), (DOWN, dqo_d, dqg_d)):
+        wires.send(DQ + layer, sent, dquery.at[layer, :, wide], place.partner)
+        loads[layer + 2] = keep(own_part, dquery.at[layer, :, wide])
     for n, unit in enumerate(UNITS):
         at = 7 * n
         wires.arrive(at + R0, slots.at[at + R0], place.across)
@@ -364,19 +372,13 @@
             stage[3 * n + 2] = plus(slots.at[at + R1], term(unit, place.up(chip, 1)))
             wires.send(at + RD, stage.at[3 * n + 2], slots.at[at + RD], place.above)
 
-    slot = lambda unit, at: all_kv[unit[0]].at[place.span(at, unit[1]), :, mine]
-    passed = [0]
-
-    def hand_over(unit, at):
+    slot = lambda unit, at: all_kv.at[unit[0], place.core, place.span(at, unit[1])]
+    order = []
+
+    def landed(unit, at):
         ref = slot(unit, at)
-        wires.send(56 + passed[0], ref, ref, place.partner)
-        passed[0] += 1
-
-    order = []
-
-    def landed(unit, at):
+        wires.send(HANDED + len(order), ref, ref, place.partner)
         order.append((unit, at))
-        hand_over(unit, at)
 
     for n, unit in enumerate(UNITS):
         at = 7 * n
@@ -385,107 +387,137 @@
         wires.arrive(at + RD, slots.at[at + RD], place.below)
         total[n] = plus(slots.at[at + RX], slots.at[at + RU], slots.at[at + RD], term(unit, chip))
         gather_first(place, wires, 28, unit, total.at[n], slot)
-        copy = pltpu.make_async_copy(total.at[n], slot(unit, chip), local_sem.at[len(local)])
-        copy.start()
-        local.append(copy)
-        wires.send(56 + passed[0], total.at[n], slot(unit, chip), place.partner)
+        loads[4 + n] = keep(total.at[n], slot(unit, chip))
+        wires.send(HANDED + n, total.at[n], slot(unit, chip), place.partner)
         order.append((unit, chip))
-        passed[0] += 1
+
+    waited = set()
+
+    def handed(chosen):
+        for n, (unit, at) in enumerate(order):
+            if chosen(unit, at) and n not in waited:
+                waited.add(n)
+                ref = all_kv.at[unit[0], 1 - place.core, place.span(at, 1 - unit[1])]
+                wires.arrive(HANDED + n, ref, place.partner)
+
+    def complete(layer, x_ref, cot_ref, grad_ref):
+        for n, unit in enumerate(UNITS):
+            if unit[0] == layer:
+                loads[4 + n].wait()
+        handed(lambda unit, at: unit[0] == layer and at is chip)
+        loads[layer].wait()
+        loads[layer + 2].wait()
+        wires.arrive(DQ + layer, dquery.at[layer, :, pl.ds(pl.multiple_of((1 - place.core) * 2048, 2048), 2048)], place.partner)
+        halves = [all_kv[layer, half, place.me] for half in range(2)]
+        dkv = jnp.concatenate([halves[h // 2][:, (h % 2) * 256 + kind * 128:(h % 2) * 256 + kind * 128 + 128]
+                               for kind in range(2) for h in range(4)], 1)
+        total_sq = jnp.zeros((128, 1), F32)
+        for tile in range(8):
+            part = x_ref[:, tile * 512:(tile + 1) * 512].astype(F32)
+            total_sq = total_sq + jnp.sum(part * part, 1, keepdims=True)
+        recip = lax.rsqrt(total_sq / 4096 + EPS)
+
+        def first(tile, dots):
+            cols = pl.ds(pl.multiple_of(tile * 512, 512), 512)
+            normed = x_ref[:, cols].astype(F32) * recip
+            value = dquery[layer, :, cols].astype(F32) + lax.dot_general(
+                dkv, weight[layer, cols, :], NT, preferred_element_type=F32)
+            dact[:, cols] = value
+            product = value * normed
+            column = jnp.sum(product, 0, keepdims=True)
+            for half in range(2):
+                gparts[layer, 2 * tile + half] = jnp.broadcast_to(column[:, half * 256:(half + 1) * 256], (8, 256))
+            return dots + jnp.sum(product * gains[layer:layer + 1, cols], 1, keepdims=True)
+
+        dots = lax.fori_loop(0, 8, first, jnp.zeros((128, 1), F32))
+        for step in range(1, 16):
+            to = (place.me + step) % 16
+            wires.send(GAINS + 15 * layer + step - 1, gparts.at[layer, to], ggot.at[layer, step], to)
+        mean = dots / 4096
+
+        def second(tile, _):
+            cols = pl.ds(pl.multiple_of(tile * 512, 512), 512)
+            normed = x_ref[:, cols].astype(F32) * recip
+            dnormed = dact[:, cols] * gains[layer:layer + 1, cols]
+            grad_ref[:, cols] = (cot_ref[:, cols].astype(F32) + recip * (dnormed - normed * mean)).astype(BF)
+            return 0
+
+        lax.fori_loop(0, 8, second, 0)
+
+    def gain_total(layer):
+        value = gparts[layer, place.me]
+        for step in range(1, 16):
+            wires.arrive(GAINS + 15 * layer + step - 1, ggot.at[layer, step], (place.me + step) % 16)
+            value = value + ggot[layer, step]
+        return value
+
+    def weight_grad(layer):
+        acc[...] = jnp.zeros_like(acc)
+
+        def step(n, _):
+            two = pl.ds(2 * n, 2)
+            act = features[two, layer].reshape(256, 256)
+            for half in range(2):
+                dkv = all_kv[layer, half, two].reshape(256, 512)
+                acc[:, half * 512:(half + 1) * 512] += lax.dot_general(act, dkv, TN, preferred_element_type=F32)
+            return 0
+
+        lax.fori_loop(0, 8, step, 0)
+
+    up, down = UNITS[:2], UNITS[2:]
+    complete(UP, x_u, cot_u, grad_u)
     for unit in UNITS:
         gather_second(place, wires, 28, unit, slot, landed)
+    complete(DOWN, x_d, cot_d, grad_d)
     for unit in UNITS:
         gather_third(place, wires, 28, unit, slot, landed)
-    for unit in UNITS:
+    for unit in up:
         gather_last(place, wires, 28, unit, slot, landed)
-    theirs = pl.ds(pl.multiple_of((1 - place.core) * 512, 512), 512)
-    for n, (unit, at) in enumerate(order):
-        span = place.span(at, 1 - unit[1])
-        wires.arrive(56 + n, all_kv[unit[0]].at[span, :, theirs], place.partner)
-    for copy in far:
-        copy.wait_send()
-    wires.arrive(index, dq_u, place.partner)
-    wires.arrive(index + 1, dq_d, place.partner)
-    for n, (out, there) in enumerate(((up_out, after), (down_out, before))):
-        for flip, dev in ((0, place.me), (1, place.partner)):
-            half = pl.ds(pl.multiple_of((place.core + flip * (1 - 2 * place.core)) * 2048, 2048), 2048)
-            pltpu.make_async_remote_copy(
-                src_ref=out.at[:, half], dst_ref=out.at[:, half], send_sem=send_sem.at[index + 2 + 2 * n + flip],
-                recv_sem=recv_sem.at[index + 2 + 2 * n + flip], device_id={"section": there, "ctx": dev},
-                device_id_type=MESH_ID).wait_recv()
-    for copy in local:
-        copy.wait()
+    handed(lambda unit, at: unit[0] == UP)
+    weight_grad(UP)
+    wsend[...] = acc[...].astype(BF)
+    far_w = wires.far_send(FAR, wsend, wgot, mirrored)
+    gsum[...] = gain_total(UP)
+    far_g = wires.far_send(FAR + 1, gsum, ggot_far, mirrored)
+    for unit in down:
+        gather_last(place, wires, 28, unit, slot, landed)
+    handed(lambda unit, at: True)
+    weight_grad(DOWN)
+    mine = gain_total(DOWN)
+    far_g.wait_recv()
+    gain_grad[...] = mine + ggot_far[...]
+    far_w.wait_recv()
+    for h in range(4):
+        for kind in range(2):
+            came = slice(h * 256 + kind * 128, h * 256 + kind * 128 + 128)
+            goes = slice(kind * 512 + h * 128, kind * 512 + h * 128 + 128)
+            kv_grad[:, goes] = acc[:, came] + wgot[:, came].astype(F32)
     wires.finish()
 
 
-def reduce_terms(*operands):
+def finish(terms_d, terms_u, dqo_d, dqo_u, dqg_d, dqg_u, x_d, x_u, cot_d, cot_u, gains, features, w_d, w_u):
     hbm = pl.BlockSpec(memory_space=pl.ANY)
     vmem = pl.BlockSpec(memory_space=pltpu.VMEM)
     row = jax.ShapeDtypeStruct((128, 4096), BF)
-    half = jax.ShapeDtypeStruct((128, 2048), BF)
-    whole = jax.ShapeDtypeStruct((16, 128, 1024), BF)
+    operands = (terms_d, terms_u, dqo_d, dqo_u, dqg_d, dqg_u, x_d, x_u, cot_d, cot_u, gains, features, w_d, w_u)
+    unit = lambda count: pltpu.VMEM((count, 128, 512), BF)
     return pl.pallas_call(
-        reduce_kernel,
-        in_specs=[vmem] * 2 + [hbm] * 6,
-        out_specs=[hbm] * 6,
-        out_shape=[row] * 2 + [half] * 2 + [whole] * 2,
-        scratch_shapes=[pltpu.VMEM((28, 128, 512), BF), pltpu.VMEM((12, 128, 512), BF), pltpu.VMEM((4, 128, 512), BF),
-                        pltpu.SemaphoreType.DMA((94,)), pltpu.SemaphoreType.DMA((94,)), pltpu.SemaphoreType.DMA((4,))],
-        compiler_params=pltpu.CompilerParams(collective_id=2, has_side_effects=True, vmem_limit_bytes=32 << 20),
-        name="reduce_terms",
+        finish_kernel,
+        in_specs=[vmem] * 12 + [hbm] * 2,
+        out_specs=[vmem] * 4,
+        out_shape=[row, row, jax.ShapeDtypeStruct((256, 1024), F32), jax.ShapeDtypeStruct((8, 256), F32)],
+        scratch_shapes=[unit(28), unit(12), unit(4), pltpu.VMEM((2, 2, 16, 128, 512), BF), pltpu.VMEM((2, 128, 4096), BF),
+                        pltpu.VMEM((2, 4096, 1024), BF), pltpu.VMEM((128, 4096), F32), pltpu.VMEM((2, 16, 8, 256), F32),
+                        pltpu.VMEM((2, 16, 8, 256), F32), pltpu.VMEM((8, 256), F32), pltpu.VMEM((256, 1024), F32),
+                        pltpu.VMEM((256, 1024), BF), pltpu.VMEM((256, 1024), BF), pltpu.VMEM((8, 256), F32),
+                        pltpu.SemaphoreType.DMA((122,)), pltpu.SemaphoreType.DMA((122,)), pltpu.SemaphoreType.DMA((8,))],
+        compiler_params=pltpu.CompilerParams(collective_id=2, has_side_effects=True, vmem_limit_bytes=60 << 20),
+        name="finish",
     )(*operands)
-
-
-def gains_kernel(g_ref, gd_out, gu_out, parts, mine, send_sem, recv_sem):
-    me = lax.axis_index("ctx")
-    section = lax.axis_index("section")
-    barrier = pltpu.get_barrier_semaphore()
-    pl.semaphore_signal(barrier, inc=1, device_id={"section": 7 - section}, device_id_type=MESH_ID)
-    for step in range(1, 16):
-        pl.semaphore_signal(barrier, inc=1, device_id={"ctx": (me + step) % 16}, device_id_type=MESH_ID)
-    pl.semaphore_wait(barrier, 16)
-    copies = []
-    for step in range(1, 16):
-        to = (me + step) % 16
-        copy = pltpu.make_async_remote_copy(
-            src_ref=g_ref.at[to], dst_ref=parts.at[step], send_sem=send_sem.at[step], recv_sem=recv_sem.at[step],
-            device_id={"ctx": to}, device_id_type=MESH_ID)
-        copy.start()
-        copies.append(copy)
-    value = g_ref[me]
-    for step in range(1, 16):
-        copies[step - 1].wait_recv()
-        value = value + parts[step]
-    mine[...] = value
-    gd_out[...] = value
-    last = pltpu.make_async_remote_copy(src_ref=mine, dst_ref=gu_out, send_sem=send_sem.at[0], recv_sem=recv_sem.at[0],
-                                        device_id={"section": 7 - section}, device_id_type=MESH_ID)
-    last.start()
-    for copy in copies:
-        copy.wait_send()
-    last.wait()
-
-
-def sum_gains(gains):
-    vmem = pl.BlockSpec(memory_space=pltpu.VMEM)
-    small = jax.ShapeDtypeStruct((8, 256), F32)
-    return pl.pallas_call(
-        gains_kernel,
-        in_specs=[vmem],
-        out_specs=[vmem, vmem],
-        out_shape=[small, small],
-        scratch_shapes=[pltpu.VMEM((16, 8, 256), F32), pltpu.VMEM((8, 256), F32),
-                        pltpu.SemaphoreType.DMA((16,)), pltpu.SemaphoreType.DMA((16,))],
-        compiler_params=pltpu.CompilerParams(collective_id=3, has_side_effects=True),
-        name="sum_gains",
-    )(gains)
 
 
 def by_head(kv):
     return kv.reshape(-1, 2, 4, 128).transpose(0, 2, 1, 3).reshape(-1, 1024)
-
-
-def by_kind(kv):
-    return kv.reshape(-1, 4, 2, 128).transpose(0, 2, 1, 3).reshape(-1, 1024)
 
 
 def prepare(x, gain, weight):
@@ -494,20 +526,19 @@
     normed = xf * recip
     act = (normed * gain[None, :]).astype(BF)
     kv = jnp.dot(act, weight, preferred_element_type=F32).astype(BF)
-    return recip, act, by_head(kv)
-
-
-def complete(x, recip, cot, gain, weight, dquery, dkv):
-    normed = x.astype(F32) * recip
-    dact = dquery.astype(F32) + lax.dot_general(by_kind(dkv), weight, NT, preferred_element_type=F32)
-    gpart = jnp.sum(dact * normed, 0)
-    dnormed = dact * gain[None, :]
-    dx = cot.astype(F32) + recip * (dnormed - normed * jnp.mean(dnormed * normed, -1, keepdims=True))
-    return dx.astype(BF), gpart
+    return act, by_head(kv)
 
 
 def halves_joined(core, mine, other):
     return jnp.where(core == 0, jnp.concatenate([mine, other], 1), jnp.concatenate([other, mine], 1))
+
+
+def relayed(own, got, core, by):
+    sections, spans = lax.axis_size("section"), lax.axis_size("ctx")
+    to = lambda flip: [(s * spans + i, (s + by) % sections * spans + (i ^ flip)) for s in range(sections) for i in range(spans)]
+    mine = lax.ppermute(own, ("section", "ctx"), to(0))
+    other = lax.ppermute(got, ("section", "ctx"), to(1))
+    return halves_joined(core, mine, other)
 
 
 def per_device(down_in, up_in, down_cot, up_cot, kv_weight, norm_gain, span_ids):
@@ -517,28 +548,21 @@
     gain_d, gain_u = norm_gain[0, 0], norm_gain[1, 0]
     weight_d, weight_u = kv_weight[0, 0], kv_weight[1, 0]
     scalars = jnp.stack([span_ids[own], span_ids[own + 1 - 2 * core], core]).astype(jnp.int32)
-    inverse = jnp.argsort(span_ids).astype(jnp.int32)
-    recip_u, act_u, kv_u = prepare(x_u, gain_u, weight_u)
-    recip_d, act_d, kv_d = prepare(x_d, gain_d, weight_d)
+    order = jnp.arange(16, dtype=jnp.int32)
+    inverse = jnp.sum(jnp.where(span_ids[:, None] == order[None, :], order[:, None], 0), 0).astype(jnp.int32)
+    act_u, kv_u = prepare(x_u, gain_u, weight_u)
+    act_d, kv_d = prepare(x_d, gain_d, weight_d)
     q_d, q_u, dy_d, dy_u, xh_d, xh_u, all_d, all_u = spread(act_d, act_u, cot_d, cot_u, x_d, x_u, kv_d, kv_u)
-    features = jnp.stack([act_d, act_u]).reshape(2, 128, 16, 256).transpose(2, 0, 1, 3)
+    after_d, after_u, _ = lax.optimization_barrier((act_d, act_u, q_d))
+    features = jnp.stack([after_d, after_u]).reshape(2, 128, 16, 256).transpose(2, 0, 1, 3)
     features = lax.all_to_all(features, "ctx", 0, 0, tiled=False)
     yo_u, yg_u, dqo_u, dqg_u, terms_u = attention((act_u, q_u), (cot_u, dy_u), (x_u, xh_u), all_u, scalars, inverse)
+    up_out = relayed(yo_u, yg_u, core, -1)
     yo_d, yg_d, dqo_d, dqg_d, terms_d = attention((act_d, q_d), (cot_d, dy_d), (x_d, xh_d), all_d, scalars, inverse)
-    down_out, up_out, dq_d, dq_u, dkv_d, dkv_u = reduce_terms(
-        terms_d, terms_u, yo_d, yg_d, yo_u, yg_u, dqg_d, dqg_u)
-    wgrad = lambda which, dkv: lax.dot_general(
-        features[:, which].reshape(2048, 256), dkv.reshape(2048, 1024), TN, preferred_element_type=F32)
-    sections = lax.axis_size("section")
-    mirror_w = lax.ppermute(wgrad(1, dkv_u).astype(BF), "section", [(i, sections - 1 - i) for i in range(sections)])
-    own_dkv = lambda dkv: lax.dynamic_index_in_dim(dkv, own, 0, False)
-    grad_u, gpart_u = complete(x_u, recip_u, cot_u, gain_u, weight_u, halves_joined(core, dqo_u, dq_u), own_dkv(dkv_u))
-    grad_d, gpart_d = complete(x_d, recip_d, cot_d, gain_d, weight_d, halves_joined(core, dqo_d, dq_d), own_dkv(dkv_d))
-    gains = jnp.stack([gpart_d, gpart_u] + [jnp.zeros_like(gpart_d)] * 6).reshape(8, 16, 256).transpose(1, 0, 2)
-    gain_here, gain_there = sum_gains(gains)
-    kv_grad = by_kind(wgrad(0, dkv_d) + mirror_w.astype(F32))[None]
-    gain_grad = (gain_here[0] + gain_there[1])[None]
-    return (down_out[None], up_out[None], grad_d[None], grad_u[None], kv_grad, gain_grad)
+    down_out = relayed(yo_d, yg_d, core, 1)
+    grad_d, grad_u, kv_grad, gain_grad = finish(
+        terms_d, terms_u, dqo_d, dqo_u, dqg_d, dqg_u, x_d, x_u, cot_d, cot_u, norm_gain[:, 0], features, weight_d, weight_u)
+    return (down_out[None], up_out[None], grad_d[None], grad_u[None], kv_grad[None], gain_grad[:1])
 
 
 def solution(mesh):

time: 355 us -> 310 us (0.87)
  the two profiles are of different devices: /device:TPU:2 before, /device:TPU:1 now
where the time goes in v4:
time: 310 us; the launch traced here: 304 us
  Pallas kernels  231 us (75%)
  local copies, waits for them, and re-layouts  27.4 us (9%)
  starting transfers between devices  13.8 us (4%)
  other arithmetic  13 us (4%)
  matrix products  9.55 us (3%)
  waiting for transfers between devices  7.66 us (2%)
    pallas_call x1, Pallas kernels, finish(): pl.pallas_call(finish_kernel, in_specs=[vmem] * 12 + [hbm] * 2, out_specs...  125 us
    pallas_call x2, Pallas kernels, attention(): pl.pallas_call(functools.partial(attention_kernel, kf, kb), grid_spec=plt...  67 us
    pallas_call x1, Pallas kernels, spread(): pl.pallas_call(spread_kernel, in_specs=[hbm] * 6 + [pl.BlockSpec(memory_s...  39.5 us
    squeeze x1, local copies, waits for them, and re-layouts, per_device(): weight_d, weight_u = (kv_weight[0, 0], kv_weight[1, 0])  11.6 us
    dot_general x2, matrix products, prepare(): kv = jnp.dot(act, weight, preferred_element_type=F32).astype(BF)  9.55 us
    unnamed x42, local copies, waits for them, and re-layouts  8.21 us
    ppermute x2, waiting for transfers between devices, relayed(): other = lax.ppermute(got, ('section', 'ctx'), to(1))  7.65 us
    all_to_all x1, starting transfers between devices, per_device(): features = lax.all_to_all(features, 'ctx', 0, 0, tiled=False)  6.69 us
  transfers between devices with their start and end apart: 5, of which 1 were waited for; matrix products, arithmetic and copies ran while one was open for 6% of the time, Pallas kernels for 22%

profile of v4, /device:TPU:1, one launch (start us, length us, event | category | flops | bytes accessed | tf_op | source)
XLA Modules:
  0.0 303.8 jit_solution(5603399616630620868)
XLA Ops:
  0.6 0.0 copy-start.10
  0.6 0.0 copy-start.17
  0.7 1.6 fusion
  2.3 1.5 fusion.3
  3.8 0.0 copy-done.17
  3.8 0.0 copy-done.10
  3.8 0.0 copy-start.11
  3.8 4.8 %convolution_convert_fusion.1 = bf16[128,1024]{1,0:T(8,128)(2,1)S(1)} fusion(bf16[1,128,4096]{2,1,0:T(8,128)(2,1)S(1)} %copy-done.10, f32[4096]{0:T(1024)S(1)} %bitcast.67, f32[128]{0:T(128)S(1)} %add_rsqrt_fusion.1, bf16[2,1,4096,1024]{3,2,1,0:T(8,128)(2,1)} %param.11), kind=kOutput, calls=%fused_computation.16 | convolution fusion | flops 1075970048 | bytes 9716224 | tf_op jit(solution)/shard_map/dot_general | solution.py:528
  8.7 0.0 copy-done.11
  8.7 4.7 %convolution_convert_fusion = bf16[128,1024]{1,0:T(8,128)(2,1)S(1)} fusion(bf16[1,128,4096]{2,1,0:T(8,128)(2,1)S(1)} %copy-done.11, f32[4096]{0:T(1024)S(1)} %bitcast.65, f32[128]{0:T(128)S(1)} %add_rsqrt_fusion, bf16[2,1,4096,1024]{3,2,1,0:T(8,128)(2,1)} %param.11), kind=kOutput, calls=%fused_computation.15 | convolution fusion | flops 1075970048 | bytes 9716224 | tf_op jit(solution)/shard_map/dot_general | solution.py:528
  13.4 2.0 fusion.2
  15.4 0.2 reshape.186
  15.6 0.2 copy.32
  15.8 0.9 reshape.187.kv_d
  16.6 0.2 reshape.188
  16.8 0.2 copy.31
  17.0 0.9 reshape.189.kv_u
  17.9 39.5 %spread.1 = (bf16[128,2048]{1,0:T(8,128)(2,1)}, bf16[128,2048]{1,0:T(8,128)(2,1)}, bf16[128,2048]{1,0:T(8,128)(2,1)}, bf16[128,2048]{1,0:T(8,128)(2,1)}, bf16[12...) custom-call(bf16[128,4096]{1,0:T(8,128)(2,1)} %get-tuple-element.48., ...), custom_call_target="tpu_custom_call" | custom-call | tf_op jit(solution)/shard_map/spread/pallas_call | solution.py:296
  57.4 0.0 copy-done.13
  57.4 0.0 copy-start.12
  57.4 0.7 copy.23
  58.1 1.3 copy.25
  59.4 0.0 copy-done.12
  59.4 0.7 copy.24
  60.0 0.5 copy.26
  60.6 0.0 copy-done.14
  60.6 1.5 maximum_bitcast_fusion
  62.1 6.7 %all-to-all-start = ((bf16[16,2,128,256]{3,2,1,0:T(8,128)(2,1)}), bf16[16,2,128,256]{3,2,1,0:T(8,128)(2,1)}, u32[]{:S(2)}, u32[]{:S(2)}) async-start(bf16[16,2,128,256]{3,2,1,0:T(8,128)(2,1)} %maximum_bitcast_fusion), calls=%async_computation | async-start | bytes 4194304 | tf_op jit(solution)/shard_map/all_to_all | solution.py:558
  68.8 0.0 copy-done.18
  68.8 0.1 select_reduce_fusion.inv_ref
  68.9 0.6 fusion.15
  69.5 1.4 pad_add_fusion.tq_ref
  70.9 0.0 copy-done.7
  70.9 0.0 copy-done.8
  70.9 0.0 copy-done.9
  70.9 33.3 %attention.2 = (bf16[128,2048]{1,0:T(8,128)(2,1)S(1)}, bf16[128,2048]{1,0:T(8,128)(2,1)S(1)}, bf16[128,2048]{1,0:T(8,128)(2,1)S(1)}, bf16[128,2048]{1,0:T(8,128)(2,1)S(1)}, bf16[2048,512]{1,0:T(8,128)(2,1)}) custom-call(s32[3]{0:T(128)S(1)} %pad_add_fusion.tq_ref, s32[16]{0:T(128)S(1)} %select_reduce_fusion.inv_ref, ...), custom_call_target="tpu_custom_call" | custom-call | flops 15032385536 | bytes 16777216 | tf_op jit(solution)/shard_map/attention/pallas_call | solution.py:118
  104.2 0.0 copy-start
  104.3 0.8 copy-done
  105.0 0.8 copy-done.1
  105.8 1.3 collective-permute-start
  107.1 1.8 collective-permute-start.1
  108.9 0.0 copy-done.4
  108.9 0.0 copy-done.6
  108.9 33.7 %attention.3 = (bf16[128,2048]{1,0:T(8,128)(2,1)S(1)}, bf16[128,2048]{1,0:T(8,128)(2,1)S(1)}, bf16[128,2048]{1,0:T(8,128)(2,1)S(1)}, bf16[128,2048]{1,0:T(8,128)(2,1)S(1)}, bf16[2048,512]{1,0:T(8,128)(2,1)}) custom-call(s32[3]{0:T(128)S(1)} %pad_add_fusion.tq_ref, s32[16]{0:T(128)S(1)} %select_reduce_fusion.inv_ref, ...), custom_call_target="tpu_custom_call" | custom-call | flops 15032385536 | bytes 16777216 | tf_op jit(solution)/shard_map/attention/pallas_call | solution.py:118
  142.6 0.0 copy-start.2
  142.7 0.8 copy-done.2
  143.4 0.8 copy-done.3
  144.2 3.8 %collective-permute-start.2 = (bf16[128,2048]{1,0:T(8,128)(2,1)S(1)}, bf16[128,2048]{1,0:T(8,128)(2,1)S(1)}, u32[]{:S(2)}, u32[]{:S(2)}) collective-permute-start(bf16[128,2048]{1,0:T(8,128)(2,1)S(1)} %get-tuple-element.40), channel_id=1, source_target_pairs={{0,112},{1,113},{2,114},{3,115},{4,116},{5,117},{6,118},{7,119},{8... | collective-permute-start | bytes 1572872 | tf_op jit(solution)/shard_map/ppermute | solution.py:539
  148.0 0.3 collective-permute-start.3
  148.3 11.6 %slice_bitcast_fusion = (bf16[4096,1024]{1,0:T(8,128)(2,1)}, bf16[4096,1024]{1,0:T(8,128)(2,1)}) fusion(bf16[2,1,4096,1024]{3,2,1,0:T(8,128)(2,1)} %param.11), kind=kLoop, calls=%fused_computation | loop fusion | bytes 33554432 | tf_op jit(solution)/shard_map/squeeze | solution.py:549
  159.9 0.6 copy.33
  160.5 0.0 collective-permute-done
  160.5 0.0 collective-permute-done.1
  160.6 2.5 maximum_select_fusion
  163.0 0.0 collective-permute-done.2
  163.0 7.7 %collective-permute-done.3 = bf16[128,2048]{1,0:T(8,128)(2,1)} collective-permute-done((bf16[128,2048]{1,0:T(8,128)(2,1)S(1)}, bf16[128,2048]{1,0:T(8,128)(2,1)}, u32[]{:S(2)}, u32[]{:S(2)}) %collective-permute-start.3) | collective-permute-done | bytes 524320 | tf_op jit(solution)/shard_map/ppermute | solution.py:540
  170.7 2.4 maximum_select_fusion.1
  173.1 0.0 all-to-all-done.features
  173.1 124.8 %finish.1 = (bf16[128,4096]{1,0:T(8,128)(2,1)}, bf16[128,4096]{1,0:T(8,128)(2,1)}, f32[256,1024]{1,0:T(8,128)}, f32[8,256]{1,0:T(8,128)}) custom-call(bf16[2048,512]{1,0:T(8,128)(2,1)} %get-tuple-element.42.terms_d, bf16[2048,512]{1,0:T(8,128)(2,1)} %get-tuple-element.43.terms_u, bf16[128,2048]{1,0:T(8,128)(2,1)} %copy-done, bf16[128,2048]{1,0:T(8,128)(2,1)} %copy-done.2, ...), custom_call_target="tpu_custom_call" | custom-call | tf_op jit(solution)/shard_map/finish/pallas_call | solution.py:504
  298.0 1.3 slice.19
  299.3 2.4 copy.37
  301.7 1.0 copy.38
  302.7 0.0 copy-done.15
  302.7 1.0 copy.39
  (18 shorter events, 0.0 us)
Async XLA Ops:
  0.6 3.2 %copy-start.10 = (bf16[1,128,4096]{2,1,0:T(8,128)(2,1)S(1)}, bf16[1,128,4096]{2,1,0:T(8,128)(2,1)}, u32[]{:S(2)}) copy-start(bf16[1,128,4096]{2,1,0:T(8,128)(2,1)} %param.7) | copy-start | bytes 3145732
  0.6 3.2 %copy-start.17 = (f32[2,1,4096]{2,1,0:T(1,128)S(1)}, f32[2,1,4096]{2,1,0:T(1,128)}, u32[]{:S(2)}) copy-start(f32[2,1,4096]{2,1,0:T(1,128)} %param.12) | copy-start | bytes 98308
  3.8 4.8 %copy-start.11 = (bf16[1,128,4096]{2,1,0:T(8,128)(2,1)S(1)}, bf16[1,128,4096]{2,1,0:T(8,128)(2,1)}, u32[]{:S(2)}) copy-start(bf16[1,128,4096]{2,1,0:T(8,128)(2,1)} %param.8) | copy-start | bytes 3145732
  17.9 39.5 %copy-start.13 = (bf16[128,4096]{1,0:T(8,128)(2,1)S(1)}, bf16[128,4096]{1,0:T(8,128)(2,1)}, u32[]{:S(2)}) copy-start(bf16[128,4096]{1,0:T(8,128)(2,1)} %get-tuple-element.48.act_d.q_own) | copy-start | bytes 3145732
  57.4 2.0 copy-start.12
  59.4 1.2 copy-start.14
  62.1 6.7 %copy-start.18 = (s32[16]{0:T(128)S(1)}, s32[16]{0:T(128)}, u32[]{:S(2)}) copy-start(s32[16]{0:T(128)} %param.13) | copy-start | bytes 196
  62.1 8.8 %copy-start.7 = (bf16[128,2048]{1,0:T(8,128)(2,1)S(1)}, bf16[128,2048]{1,0:T(8,128)(2,1)}, u32[]{:S(2)}) copy-start(bf16[128,2048]{1,0:T(8,128)(2,1)} %get-tuple-element.30.q_got) | copy-start | bytes 1572868
  62.1 8.8 %copy-start.8 = (bf16[128,2048]{1,0:T(8,128)(2,1)S(1)}, bf16[128,2048]{1,0:T(8,128)(2,1)}, u32[]{:S(2)}) copy-start(bf16[128,2048]{1,0:T(8,128)(2,1)} %get-tuple-element.31.dy_got) | copy-start | bytes 1572868
  62.1 8.8 %copy-start.9 = (bf16[128,2048]{1,0:T(8,128)(2,1)S(1)}, bf16[128,2048]{1,0:T(8,128)(2,1)}, u32[]{:S(2)}) copy-start(bf16[128,2048]{1,0:T(8,128)(2,1)} %get-tuple-element.32.x_got) | copy-start | bytes 1572868
  62.1 111.0 %all-to-all-start = ((bf16[16,2,128,256]{3,2,1,0:T(8,128)(2,1)}), bf16[16,2,128,256]{3,2,1,0:T(8,128)(2,1)}, u32[]{:S(2)}, u32[]{:S(2)}) async-start(bf16[16,2,128,256]{3,2,1,0:T(8,128)(2,1)} %maximum_bitcast_fusion), calls=%async_computation | async-start | bytes 4194304 | tf_op jit(solution)/shard_map/all_to_all | solution.py:558
  70.9 38.0 %copy-start.4 = (bf16[128,2048]{1,0:T(8,128)(2,1)S(1)}, bf16[128,2048]{1,0:T(8,128)(2,1)}, u32[]{:S(2)}) copy-start(bf16[128,2048]{1,0:T(8,128)(2,1)} %get-tuple-element.36.q_got) | copy-start | bytes 1572868
  70.9 38.0 %copy-start.5 = (bf16[128,2048]{1,0:T(8,128)(2,1)S(1)}, bf16[128,2048]{1,0:T(8,128)(2,1)}, u32[]{:S(2)}) copy-start(bf16[128,2048]{1,0:T(8,128)(2,1)} %get-tuple-element.37.dy_got) | copy-start | bytes 1572868
  70.9 38.0 %copy-start.6 = (bf16[128,2048]{1,0:T(8,128)(2,1)S(1)}, bf16[128,2048]{1,0:T(8,128)(2,1)}, u32[]{:S(2)}) copy-start(bf16[128,2048]{1,0:T(8,128)(2,1)} %get-tuple-element.38.x_got) | copy-start | bytes 1572868
  104.2 0.8 copy-start
  105.0 0.8 copy-start.1
  105.8 54.7 %collective-permute-start = (bf16[128,2048]{1,0:T(8,128)(2,1)S(1)}, bf16[128,2048]{1,0:T(8,128)(2,1)S(1)}, u32[]{:S(2)}, u32[]{:S(2)}) collective-permute-start(bf16[128,2048]{1,0:T(8,128)(2,1)S(1)} %get-tuple-element.34), channel_id=1, source_target_pairs={{0,16},{1,17},{2,18},{3,19},{4,20},{5,21},{6,22},{7,23},{8,24},{9,... | collective-permute-start | bytes 1572872 | tf_op jit(solution)/shard_map/ppermute | solution.py:539
  107.1 53.4 %collective-permute-start.1 = (bf16[128,2048]{1,0:T(8,128)(2,1)S(1)}, bf16[128,2048]{1,0:T(8,128)(2,1)}, u32[]{:S(2)}, u32[]{:S(2)}) collective-permute-start(bf16[128,2048]{1,0:T(8,128)(2,1)S(1)} %get-tuple-element.35), channel_id=1, source_target_pairs={{0,17},{1,16},{2,19},{3,18},{4,21},{5,20},{6,23},{7,22},{8,25},{9,... | collective-permute-start | bytes 1572872 | tf_op jit(solution)/shard_map/ppermute | solution.py:540
  142.6 0.8 copy-start.2
  143.4 0.8 copy-start.3
  144.2 18.8 %collective-permute-start.2 = (bf16[128,2048]{1,0:T(8,128)(2,1)S(1)}, bf16[128,2048]{1,0:T(8,128)(2,1)S(1)}, u32[]{:S(2)}, u32[]{:S(2)}) collective-permute-start(bf16[128,2048]{1,0:T(8,128)(2,1)S(1)} %get-tuple-element.40), channel_id=1, source_target_pairs={{0,112},{1,113},{2,114},{3,115},{4,116},{5,117},{6,118},{7,119},{8... | collective-permute-start | bytes 1572872 | tf_op jit(solution)/shard_map/ppermute | solution.py:539
  148.0 22.7 %collective-permute-start.3 = (bf16[128,2048]{1,0:T(8,128)(2,1)S(1)}, bf16[128,2048]{1,0:T(8,128)(2,1)}, u32[]{:S(2)}, u32[]{:S(2)}) collective-permute-start(bf16[128,2048]{1,0:T(8,128)(2,1)S(1)} %get-tuple-element.41), channel_id=1, source_target_pairs={{0,113},{1,112},{2,115},{3,114},{4,117},{5,116},{6,119},{7,118},{8... | collective-permute-start | bytes 1572872 | tf_op jit(solution)/shard_map/ppermute | solution.py:540
  298.0 3.7 %copy-start.16 = (bf16[128,4096]{1,0:T(8,128)(2,1)S(1)}, bf16[128,4096]{1,0:T(8,128)(2,1)}, u32[]{:S(2)}) copy-start(bf16[128,4096]{1,0:T(8,128)(2,1)} %get-tuple-element.51) | copy-start | bytes 3145732
  299.3 3.4 %copy-start.15 = (f32[256,1024]{1,0:T(8,128)S(1)}, f32[256,1024]{1,0:T(8,128)}, u32[]{:S(2)}) copy-start(f32[256,1024]{1,0:T(8,128)} %get-tuple-element.52) | copy-start | bytes 3145732
